TPU v7x, 32 devices: a whole 2x2x4 slice. The times are simulated.
32 devices in a mesh: dp: 8 (over z, y), tensor: 4 (over x, core).
Axes of the slice: x: 2, y: 2, z: 4, core: 2. Of those that a mesh axis runs over, the one named last changes fastest.
Arguments:
- acts: bfloat16 [8, 2048, 2048], P(None, 'dp', 'tensor'), may hold values from -24 to 24
- out_cot: bfloat16 [8, 2048, 1024], P(None, 'dp', 'tensor'), may hold values from -24 to 24
- emb_ids: int32 [2048], P(('dp', 'tensor')), may hold values from 0 to 8191
- emb_cot: bfloat16 [2048, 1024], P('dp', 'tensor'), may hold values from -24 to 24
- grad_w: float32 [8192, 2048], P(('dp', 'tensor')), may hold values from -6 to 6
- grad_e: float32 [8192, 1024], P(('dp', 'tensor')), may hold values from -6 to 6
Outputs:
- update_w: float32 [8192, 2048], P('dp', 'tensor')
- update_e: float32 [8192, 1024], P(('dp', 'tensor'))
All inputs are finite; a program needn't handle non-finite values. Where the computation divides by a largest or mean magnitude, that divisor is 1e-20 or more.
Results may differ from a plain program's by a relative error of at most 0.0003.
Values sent between devices are 32-bit elements; how exact they have to be, the bound alone decides.
No kernel may reach another device: no remote copies, remote signals or barrier semaphores. Data moves between devices by JAX's collectives and lax.ppermute only.
A program may use at most 64 MiB of HBM per device.

v0:
```python
import jax
import jax.numpy as jnp
from jax import lax
from jax.sharding import PartitionSpec as P

HEAD = 64
NS_ITERS = 4


damp_root = 0.7


def newton_inverse(matrices):
    size = matrices.shape[-1]
    eye = jnp.eye(size, dtype=jnp.float32)
    bound = jnp.max(jnp.sum(jnp.abs(matrices), axis=-1), axis=-1)
    approx = eye[None] / bound[:, None, None]
    for sweep in range(NS_ITERS):
        image = jnp.einsum("bij,bjk->bik", matrices, approx, precision=lax.Precision.HIGHEST)
        approx = jnp.einsum(
            "bij,bjk->bik", approx, 2.0 * eye[None] - image, precision=lax.Precision.HIGHEST
        )
    return approx


def local(acts, out_cot, emb_ids, emb_cot, grad_w, grad_e):
    n_dp = lax.axis_size("dp")
    n_tp = lax.axis_size("tensor")
    layers, tok_rows, inner_part = acts.shape
    width_part = out_cot.shape[2]
    heads_part = inner_part // HEAD
    groups_part = width_part // HEAD
    tokens_all = tok_rows * n_dp
    width = width_part * n_tp
    inner = inner_part * n_tp
    groups_all = width // HEAD
    rows_e = grad_e.shape[0]
    vocab = rows_e * n_dp * n_tp
    dp_index = lax.axis_index("dp")
    flat_index = dp_index * n_tp + lax.axis_index("tensor")
    tile_rows = grad_w.shape[0] * n_tp
    block_rows = tile_rows // HEAD
    layer_rows = min(tile_rows, width)
    layer_span = tile_rows // layer_rows
    first_layer = dp_index * tile_rows // width
    split_acts = acts.reshape(layers, tok_rows, heads_part, HEAD)
    gram_a = jnp.einsum(
        "lthi,lthj->lhij", split_acts, split_acts, preferred_element_type=jnp.float32
    )
    split_cot = out_cot.reshape(layers, tok_rows, groups_part, HEAD)
    gram_g = jnp.einsum("lthi,lthj->lhij", split_cot, split_cot, preferred_element_type=jnp.float32)
    split_emb = emb_cot.reshape(tok_rows, groups_part, HEAD)
    gram_e = jnp.einsum("thi,thj->hij", split_emb, split_emb, preferred_element_type=jnp.float32)
    blocks = jnp.concatenate(
        [gram_a.reshape(-1, HEAD, HEAD), gram_g.reshape(-1, HEAD, HEAD), gram_e], axis=0
    )
    block_count = blocks.shape[0]
    diagonal_sums = jnp.trace(blocks, axis1=1, axis2=2)
    local_a = jnp.sum(diagonal_sums[: layers * heads_part].reshape(layers, heads_part), axis=1)
    local_g = jnp.sum(
        diagonal_sums[layers * heads_part : layers * (heads_part + groups_part)].reshape(
            layers, groups_part
        ),
        axis=1,
    )
    local_e = jnp.sum(diagonal_sums[layers * (heads_part + groups_part) :])
    trace_local = jnp.concatenate([local_a, local_g, local_e[None]])
    local_counts = jnp.sum(
        (emb_ids[:, None] == jnp.arange(vocab, dtype=jnp.int32)[None, :]).astype(jnp.float32),
        axis=0,
    )
    traces, counts_all = lax.psum((trace_local, local_counts), ("dp", "tensor"))
    counts_mine = lax.dynamic_slice_in_dim(counts_all, flat_index * rows_e, rows_e)
    trace_a = traces[:layers]
    trace_g = traces[layers : 2 * layers]
    trace_e = traces[2 * layers]
    ratio = jnp.sqrt(trace_a / (tokens_all * inner) / (trace_g / (tokens_all * width)))
    ratio_e = jnp.sqrt(tokens_all / vocab / (trace_e / (tokens_all * width)))
    shift = jnp.concatenate(
        [
            jnp.repeat(damp_root * ratio, heads_part),
            jnp.repeat(damp_root / ratio, groups_part),
            jnp.full((groups_part,), 1.0, jnp.float32) * (damp_root / ratio_e),
        ]
    )
    eye = jnp.eye(HEAD, dtype=jnp.float32)
    owned = -(-block_count // n_dp)
    slots = owned * n_dp
    padded = jnp.pad(blocks.reshape(block_count, HEAD * HEAD), ((0, slots - block_count), (0, 0)))
    mine = lax.psum_scatter(padded, "dp", scatter_dimension=0, tiled=True)
    shift_pad = jnp.pad(shift, (0, slots - block_count), constant_values=1.0)
    shift_mine = lax.dynamic_slice_in_dim(shift_pad, dp_index * owned, owned)
    damped = mine.reshape(owned, HEAD, HEAD) / tokens_all + shift_mine[:, None, None] * eye
    inverse_mine = newton_inverse(damped)
    gathered = lax.all_gather(inverse_mine.reshape(owned, HEAD * HEAD), "dp", axis=0, tiled=True)
    inverses = gathered[:block_count].reshape(block_count, HEAD, HEAD)
    inv_a = inverses[: layers * heads_part].reshape(layers, heads_part, HEAD, HEAD)
    inv_g_part = inverses[layers * heads_part : layers * (heads_part + groups_part)].reshape(
        layers, groups_part, HEAD * HEAD
    )
    inv_e_part = inverses[layers * (heads_part + groups_part) :].reshape(groups_part, HEAD * HEAD)
    base_layer = 0
    sending = jnp.concatenate(
        [inv_g_part.reshape(layers * groups_part, HEAD * HEAD), inv_e_part], axis=0
    )
    shared = lax.all_gather(sending[None], "tensor", axis=0, tiled=True)
    inv_g = shared[:, : layers * groups_part].reshape(n_tp, layers, groups_part, HEAD, HEAD)
    inv_g = jnp.transpose(inv_g, (1, 0, 2, 3, 4)).reshape(layers * groups_all, HEAD, HEAD)
    inv_e = shared[:, layers * groups_part :].reshape(groups_all, HEAD, HEAD)
    tile = lax.all_to_all(grad_w, "tensor", split_axis=1, concat_axis=0, tiled=True)
    g_sel = lax.dynamic_slice_in_dim(
        inv_g, dp_index * block_rows - base_layer * groups_all, block_rows, 0
    )
    left = jnp.einsum(
        "bij,bjc->bic",
        g_sel,
        tile.reshape(block_rows, HEAD, inner_part),
        precision=lax.Precision.HIGHEST,
    )
    a_sel = lax.dynamic_slice_in_dim(inv_a, first_layer, layer_span, 0)
    right = jnp.einsum(
        "lrhi,lhij->lrhj",
        left.reshape(layer_span, layer_rows, heads_part, HEAD),
        a_sel,
        precision=lax.Precision.HIGHEST,
    )
    update_w = right.reshape(tile_rows, inner_part)
    scaled = jnp.einsum(
        "rgi,gij->rgj",
        grad_e.reshape(rows_e, groups_all, HEAD),
        inv_e,
        precision=lax.Precision.HIGHEST,
    )
    update_e = scaled.reshape(rows_e, width) / (counts_mine + damp_root * ratio_e)[:, None]
    return (update_w, update_e)


def solution(mesh):
    in_specs = (
        P(None, "dp", "tensor"),
        P(None, "dp", "tensor"),
        P(("dp", "tensor")),
        P("dp", "tensor"),
        P(("dp", "tensor"), None),
        P(("dp", "tensor"), None),
    )
    out_specs = (P("dp", "tensor"), P(("dp", "tensor"), None))
    return jax.shard_map(local, mesh=mesh, in_specs=in_specs, out_specs=out_specs, check_vma=False)
```

profile of v0, /device:TPU:0, one launch (start us, length us, event | category | flops | bytes accessed | tf_op | source)
XLA Modules:
  0.0 260.1 jit_solution(6523595323034215726)
XLA Ops:
  7.2 3.9 %copy.41 = bf16[8,256,512]{1,2,0:T(8,128)(2,1)} copy(bf16[8,256,512]{2,1,0:T(8,128)(2,1)} %param.6) | data formatting | bytes 4194304 | tf_op args[0]
  11.1 3.0 %fusion.28 = f32[8,8,64,64]{3,2,1,0:T(8,128)S(1)} fusion(bf16[8,256,8,64]{1,3,2,0:T(8,128)(2,1)} %bitcast.60), kind=kOutput, calls=%fused_computation.52 | convolution fusion | flops 134217728 | bytes 3145728 | tf_op jit(solution)/shard_map/lthi,lthj->lhij/dot_general | solution.py:47
  14.1 1.3 copy.42
  15.4 2.0 fusion.29
  17.7 1.6 concatenate.21
  20.6 2.7 %select_maximum_fusion = f32[104,4096]{1,0:T(8,128)} fusion(f32[4,4096]{1,0:T(4,128)S(1)} %concatenate.23, f32[32,4096]{1,0:T(8,128)} %concatenate.22, f32[64,4096]{1,0:T(8,128)} %concatenate.21), kind=kLoop, calls=%fused_computation.7 | loop fusion | flops 2555904 | bytes 3342336 | tf_op jit(solution)/shard_map/concatenate | solution.py:54
  23.3 52.6 %fusion = f32[16,4096]{1,0:T(8,128)S(1)} fusion(f32[104,4096]{1,0:T(8,128)} %select_maximum_fusion), kind=kCustom, calls=%all-reduce-scatter | all-reduce-scatter fusion | flops 524289 | bytes 1966592
  76.0 2.0 collective-permute-start
  81.0 3.1 %collective-permute-start.1 = (f32[5,4096]{1,0:T(8,128)S(1)}, f32[5,4096]{1,0:T(8,128)S(1)}, u32[]{:S(2)}, u32[]{:S(2)}) collective-permute-start(f32[5,4096]{1,0:T(8,128)S(1)} %slice.57), channel_id=1, source_target_pairs={{0,8},{4,12},{8,16},{12,20},{16,24},{20,28},{1,9},{5,13},{9,17},{1... | collective-permute-start | bytes 245768
  84.2 39.6 %all-reduce.4 = (f32[17]{0:T(128)S(1)}, f32[8192]{0:T(1024)S(1)}) all-reduce(f32[17]{0:T(128)S(1)} %pad_maximum_fusion, f32[8192]{0:T(1024)S(1)} %convert_reduce_fusion), channel_id=1, replica_groups=mesh['dp'=8,'tensor'=4] {'dp','tensor'}, use_global_device_ids=true, to_apply=%region_5.6 | all-reduce | flops 8209 | bytes 65672 | tf_op jit(solution)/shard_map/psum | solution.py:72
  127.0 2.3 concatenate.30
  135.8 50.1 %all-gather.6.cloned.1.call-done = f32[8,13,4096]{2,1,0:T(8,128)} async-done(((f32[1,13,4096]{2,1,0:T(8,128)}), f32[8,13,4096]{2,1,0:T(8,128)}) %all-gather.6.cloned.1.call-update) | async-done | bytes 1703952 | tf_op jit(solution)/shard_map/all_gather | solution.py:95
  185.8 1.8 reshape.145
  188.6 3.1 %copy.57 = f32[32,4,8,512]{3,2,0,1:T(8,128)} copy(f32[32,4,8,512]{3,2,1,0:T(8,128)} %bitcast.68) | data formatting | bytes 4194304 | tf_op jit(solution)/shard_map/all_to_all | solution.py:110
  191.7 4.9 %all-to-all-start = ((f32[256,4,512]{2,0,1:T(8,128)}), f32[256,4,512]{2,0,1:T(8,128)}, u32[]{:S(2)}, u32[]{:S(2)}) async-start(f32[256,4,512]{2,0,1:T(8,128)} %bitcast.57), calls=%async_computation | async-start | bytes 4194304 | tf_op jit(solution)/shard_map/all_to_all | solution.py:110
  198.1 2.1 reshape.133
  200.2 24.3 %all-gather.8.cloned.1.call-done = f32[4,36,4096]{2,1,0:T(8,128)} async-done(((f32[1,36,4096]{2,1,0:T(8,128)}), f32[4,36,4096]{2,1,0:T(8,128)}) %all-gather.8.cloned.1.call-update) | async-done | bytes 2359312 | tf_op jit(solution)/shard_map/all_gather | solution.py:106
  227.3 1.6 slice-done
  228.9 3.0 %reshape.135 = f32[4,8,4,64,64]{4,3,2,1,0:T(8,128)} reshape(f32[4,32,4096]{2,1,0:T(8,128)S(1)} %slice-done) | data formatting | bytes 4194304 | tf_op jit(solution)/shard_map/reshape | solution.py:107
  231.9 4.7 %copy.45 = f32[8,4,4,64,64]{4,3,2,1,0:T(8,128)} copy(f32[8,4,4,64,64]{4,3,2,0,1:T(8,128)} %bitcast.61) | data formatting | bytes 4194304 | tf_op jit(solution)/shard_map/transpose | solution.py:108
  236.6 3.6 %fusion.4 = f32[16,64,512]{2,1,0:T(8,128)S(1)} fusion(f32[16,64,512]{2,1,0:T(8,128)} %bitcast.12, f32[128,64,64]{2,1,0:T(8,128)} %bitcast.65, s32[]{:T(128)S(6)} %select_n.26), kind=kOutput, calls=%fused_computation.16 | convolution fusion | flops 402653184 | bytes 4718596 | tf_op jit(solution)/shard_map/bij,bjc->bic/dot_general | solution.py:114
  240.2 2.4 reshape.138
  242.5 7.8 %fusion.1 = f32[8,64,1024]{2,1,0:T(8,128)S(1)} fusion(f32[1024,8,64]{2,1,0:T(8,128)} %reshape.138, f32[8,8,64,64]{3,2,1,0:T(8,128)} %reshape.133, s32[]{:T(128)S(6)} %select_n.25), kind=kOutput, calls=%fused_computation | convolution fusion | flops 402653184 | bytes 6553604 | tf_op jit(solution)/shard_map/lrhi,lhij->lrhj/dot_general | solution.py:121
  250.4 1.8 copy.51
  (70 shorter events, 19.0 us)
Async XLA Ops:
  7.2 178.7 %all-gather.6.cloned.1.call-start = ((), (), s32[]{:S(2)}) async-start(), calls=%async_computation.1 | async-start | bytes 2359296 | tf_op jit(solution)/shard_map/all_gather | solution.py:95
  11.1 3.0 %copy-start.1 = (bf16[8,256,256]{2,1,0:T(8,128)(2,1)S(1)}, bf16[8,256,256]{2,1,0:T(8,128)(2,1)}, u32[]{:S(2)}) copy-start(bf16[8,256,256]{2,1,0:T(8,128)(2,1)} %param.7) | copy-start | bytes 3145732
  15.4 2.0 copy-start.3
  76.0 4.0 %copy-start.4 = (s32[64]{0:T(128)S(1)}, s32[64]{0:T(128)}, u32[]{:S(2)}) copy-start(s32[64]{0:T(128)} %param.8) | copy-start | bytes 772
  76.0 49.7 %copy-start.5 = (u32[32]{0:T(128)S(1)}, u32[32]{0:T(128)}, u32[]{:S(2)}) copy-start(u32[32]{0:T(128)} %constant.85) | copy-start | bytes 388
  76.0 51.0 %collective-permute-start = (f32[16,4096]{1,0:T(8,128)S(1)}, f32[16,4096]{1,0:T(8,128)}, u32[]{:S(2)}, u32[]{:S(2)}) collective-permute-start(f32[16,4096]{1,0:T(8,128)S(1)} %fusion), channel_id=1, source_target_pairs={{0,4},{4,8},{8,12},{12,16},{16,20},{20,24},{24,28},{1,5},{5,9},{9,... | collective-permute-start | bytes 786440
  81.0 45.9 %collective-permute-start.1 = (f32[5,4096]{1,0:T(8,128)S(1)}, f32[5,4096]{1,0:T(8,128)S(1)}, u32[]{:S(2)}, u32[]{:S(2)}) collective-permute-start(f32[5,4096]{1,0:T(8,128)S(1)} %slice.57), channel_id=1, source_target_pairs={{0,8},{4,12},{8,16},{12,20},{16,24},{20,28},{1,9},{5,13},{9,17},{1... | collective-permute-start | bytes 245768
  135.7 88.8 %all-gather.8.cloned.1.call-start = ((), (), s32[]{:S(2)}) async-start(), calls=%async_computation.2 | async-start | bytes 3276800 | tf_op jit(solution)/shard_map/all_gather | solution.py:106
  191.7 4.9 %copy-start.2 = (f32[256,1024]{1,0:T(8,128)S(1)}, f32[256,1024]{1,0:T(8,128)}, u32[]{:S(2)}) copy-start(f32[256,1024]{1,0:T(8,128)} %param.11) | copy-start | bytes 3145732
  191.7 44.9 %all-to-all-start = ((f32[256,4,512]{2,0,1:T(8,128)}), f32[256,4,512]{2,0,1:T(8,128)}, u32[]{:S(2)}, u32[]{:S(2)}) async-start(f32[256,4,512]{2,0,1:T(8,128)} %bitcast.57), calls=%async_computation | async-start | bytes 4194304 | tf_op jit(solution)/shard_map/all_to_all | solution.py:110
  198.1 27.8 %copy-start = (f32[256,1024]{0,1:T(8,128)S(1)}, f32[256,1024]{0,1:T(8,128)}, u32[]{:S(2)}) copy-start(f32[256,1024]{0,1:T(8,128)} %copy.48) | copy-start | bytes 3145732
  227.3 1.6 slice-start
Sparse Core Ops, SparseCore 0:
  135.8 49.9 all-gather.5
  188.7 35.7 all-gather.7
where the time goes:
time: 262 us; the launch traced here: 260 us
  blocking collectives  92.2 us (35%)
  waiting for transfers between devices  74.4 us (28%)
  local copies, waits for them, and re-layouts  37.9 us (14%)
  matrix products  22.5 us (9%)
  between operations  15.8 us (6%)
  starting transfers between devices  10 us (4%)
  other arithmetic  7.31 us (3%)
    unnamed x1, blocking collectives  52.6 us
    all_gather x1, waiting for transfers between devices, local(): lax.all_gather(inverse_mine.reshape(owned, HEAD * HEAD), 'dp', axis=0, ti...  50.1 us
    psum x1, blocking collectives, local(): traces, counts_all = lax.psum((trace_local, local_counts), ('dp', 'tensor'))  39.6 us
    all_gather x1, waiting for transfers between devices, local(): shared = lax.all_gather(sending[None], 'tensor', axis=0, tiled=True)  24.3 us
    unnamed x23, local copies, waits for them, and re-layouts  14.9 us
    dot_general x1, matrix products, local(): jnp.einsum('lrhi,lhij->lrhj', left.reshape(layer_span, layer_rows, heads_...  7.81 us
  transfers between devices with their start and end apart: 5, of which 2 were waited for; matrix products, arithmetic and copies ran while one was open for 8% of the time, Pallas kernels for 0%

commit v1 on v0

--- a/solution.py
+++ b/solution.py
@@ -1,10 +1,17 @@
+import functools
+
 import jax
 import jax.numpy as jnp
 from jax import lax
+from jax.experimental import pallas as pl
+from jax.experimental.pallas import tpu as pltpu
 from jax.sharding import PartitionSpec as P
 
 HEAD = 64
 NS_ITERS = 4
+LANES = 128
+HALF = HEAD
+ROWS = 8
 
 
 damp_root = 0.7
@@ -23,7 +30,7 @@
     return approx
 
 
-def local(acts, out_cot, emb_ids, emb_cot, grad_w, grad_e):
+def general_local(acts, out_cot, emb_ids, emb_cot, grad_w, grad_e):
     n_dp = lax.axis_size("dp")
     n_tp = lax.axis_size("tensor")
     layers, tok_rows, inner_part = acts.shape
@@ -135,6 +142,379 @@
     return (update_w, update_e)
 
 
+def pair_masks():
+    row = lax.broadcasted_iota(jnp.int32, (HEAD, LANES), 0)
+    lane = lax.broadcasted_iota(jnp.int32, (HEAD, LANES), 1)
+    col = jnp.where(lane < HALF, lane, lane - HALF)
+    return row, lane, col
+
+
+def gram_pair(rows):
+    full = lax.dot_general(
+        rows, rows, (((0,), (0,)), ((), ())), preferred_element_type=jnp.float32
+    )
+    _, lane, _ = pair_masks()
+    return jnp.where(lane < HALF, full[:HEAD], full[HEAD:])
+
+
+def pack_quad(first, second):
+    row, _, col = pair_masks()
+    quad = jnp.where(col >= row, first, second)
+    diagonal = jnp.sum(jnp.where(col == row, second, 0.0), axis=0, keepdims=True)
+    return quad, diagonal
+
+
+def unpack_quads(quad_a, diag_a, quad_b, diag_b):
+    row, lane, col = pair_masks()
+    turned = jnp.concatenate([quad_a, quad_b], axis=0).T
+    top, low = turned[:HEAD], turned[HEAD:]
+    turn_a = jnp.where(lane < HALF, top, pltpu.roll(low, HALF, 1))
+    turn_b = jnp.where(lane < HALF, pltpu.roll(top, HALF, 1), low)
+
+    def both(quad, turn, diag):
+        first = jnp.where(col >= row, quad, turn)
+        second = jnp.where(col < row, quad, jnp.where(col == row, diag, turn))
+        return first, second
+
+    return both(quad_a, turn_a, diag_a) + both(quad_b, turn_b, diag_b)
+
+
+def split(value):
+    high = value.astype(jnp.bfloat16)
+    low = (value - high.astype(jnp.float32)).astype(jnp.bfloat16)
+    return high, low
+
+
+def block_diagonal(pair):
+    row = lax.broadcasted_iota(jnp.int32, (LANES, LANES), 0)
+    lane = lax.broadcasted_iota(jnp.int32, (LANES, LANES), 1)
+    double = jnp.concatenate([pair, pair], axis=0)
+    return jnp.where((row < HALF) == (lane < HALF), double, 0.0)
+
+
+def right_factor(pair):
+    high, low = split(block_diagonal(pair))
+    wide = jnp.concatenate([high, low], axis=1)
+    return jnp.concatenate([wide, wide], axis=0)
+
+
+def times_right(value, factor):
+    high, low = split(value)
+    both = jnp.dot(
+        jnp.concatenate([high, low], axis=1), factor, preferred_element_type=jnp.float32
+    )
+    return both[:, :LANES] + both[:, LANES:]
+
+
+def left_factor(pair):
+    high, low = split(block_diagonal(pair))
+    return jnp.concatenate(
+        [jnp.concatenate([high, high], axis=1), jnp.concatenate([low, low], axis=1)], axis=0
+    )
+
+
+def times_left(factor, value):
+    high, low = split(value)
+    both = jnp.dot(
+        factor, jnp.concatenate([high, low], axis=0), preferred_element_type=jnp.float32
+    )
+    return both[:LANES] + both[LANES:]
+
+
+def gram_kernel(quads_a, quads_g, me_ref, acts_ref, cot_ref, emb_ref, ids_ref, *refs):
+    outs, emb_rows = refs[:-1], refs[-1]
+    step = pl.program_id(0)
+    quads = quads_a + 2 * quads_g
+    diag_at = quads * HEAD
+
+    def pack(source, at):
+        first = gram_pair(source[:, at * 2 * LANES : (at * 2 + 1) * LANES])
+        second = gram_pair(source[:, (at * 2 + 1) * LANES : (at * 2 + 2) * LANES])
+        return pack_quad(first, second)
+
+    @pl.when(step == 0)
+    def _():
+        for q in range(quads_g):
+            quad, diagonal = pack(emb_ref[...], q)
+            emb_rows[q * HEAD : (q + 1) * HEAD, :] = quad
+            emb_rows[quads_g * HEAD + q : quads_g * HEAD + q + 1, :] = diagonal
+
+    acts = acts_ref[0]
+    cot = cot_ref[0]
+    packed = [pack(acts, q) for q in range(quads_a)] + [pack(cot, q) for q in range(quads_g)]
+    packed += [
+        (
+            emb_rows[q * HEAD : (q + 1) * HEAD, :],
+            emb_rows[quads_g * HEAD + q : quads_g * HEAD + q + 1, :],
+        )
+        for q in range(quads_g)
+    ]
+    for j, out in enumerate(outs):
+
+        @pl.when(step == j)
+        def _(out=out):
+            for q, (quad, diagonal) in enumerate(packed):
+                out[q * HEAD : (q + 1) * HEAD, :] = quad
+                out[diag_at + q : diag_at + q + 1, :] = diagonal
+            out[diag_at + quads : diag_at + quads + 1, :] = ids_ref[...]
+
+
+def grams(acts, out_cot, emb_cot, ids_row, dp_index, n_dp, quads_a, quads_g, payload_rows):
+    layers, rows, width_a = acts.shape
+    width_g = out_cot.shape[2]
+    emb_scratch = -(-(quads_g * HEAD + quads_g) // ROWS) * ROWS
+    spec = pltpu.PrefetchScalarGridSpec(
+        num_scalar_prefetch=1,
+        grid=(n_dp,),
+        in_specs=[
+            pl.BlockSpec((1, rows, width_a), lambda k, me: (lax.bitwise_xor(me[0], k), 0, 0)),
+            pl.BlockSpec((1, rows, width_g), lambda k, me: (lax.bitwise_xor(me[0], k), 0, 0)),
+            pl.BlockSpec((rows, width_g), lambda k, me: (0, 0)),
+            pl.BlockSpec((1, LANES), lambda k, me: (0, 0)),
+        ],
+        out_specs=[pl.BlockSpec((payload_rows, LANES), lambda k, me: (0, 0))] * n_dp,
+        scratch_shapes=[pltpu.VMEM((emb_scratch, LANES), jnp.float32)],
+    )
+    return pl.pallas_call(
+        functools.partial(gram_kernel, quads_a, quads_g),
+        grid_spec=spec,
+        out_shape=[jax.ShapeDtypeStruct((payload_rows, LANES), jnp.float32)] * n_dp,
+        cost_estimate=pl.CostEstimate(flops=1000, bytes_accessed=1000, transcendentals=0),
+        name="grams",
+    )(dp_index.reshape(1), acts, out_cot, emb_cot, ids_row)
+
+
+def sum_kernel(quads_a, quads_g, *refs):
+    n_dp = len(refs) - 2
+    parts, (own_ref, share_ref) = refs[:n_dp], refs[n_dp:]
+    quads = quads_a + 2 * quads_g
+    diag_at = quads * HEAD
+
+    def total(at, size):
+        value = parts[0][at : at + size, :]
+        for part in parts[1:]:
+            value = value + part[at : at + size, :]
+        return value
+
+    row, _, col = pair_masks()
+    traces = []
+    first = 0
+    for count, where in ((quads_a, own_ref), (quads_g, share_ref), (quads_g, share_ref)):
+        trace = jnp.zeros((1, LANES), jnp.float32)
+        for q in range(first, first + count):
+            quad = total(q * HEAD, HEAD)
+            diagonal = total(diag_at + q, 1)
+            trace = trace + diagonal
+            trace = trace + jnp.sum(jnp.where(col == row, quad, 0.0), axis=0, keepdims=True)
+            if where is own_ref:
+                own_ref[q * HEAD : (q + 1) * HEAD, :] = quad
+                own_ref[quads_a * HEAD + q : quads_a * HEAD + q + 1, :] = diagonal
+            else:
+                at = q - quads_a
+                share_ref[at * HEAD : (at + 1) * HEAD, :] = quad
+                share_ref[2 * quads_g * HEAD + at : 2 * quads_g * HEAD + at + 1, :] = diagonal
+        traces.append(trace)
+        first += count
+    at = 2 * quads_g * (HEAD + 1)
+    for trace in traces:
+        share_ref[at : at + 1, :] = trace
+        at += 1
+    for part in parts:
+        share_ref[at : at + 1, :] = part[diag_at + quads : diag_at + quads + 1, :]
+        at += 1
+
+
+def invert_apply_kernel(sizes, own_ref, share_ref, w_ref, e_ref, w_out, e_out, right_a, left_g, right_e, scale):
+    quads_a, quads_g, n_tp, n_dp, tokens, vocab, inner, width = sizes
+    step = pl.program_id(0)
+    trace_at = 2 * quads_g * (HEAD + 1)
+
+    @pl.when(step == 0)
+    def _():
+        def trace_of(kind):
+            value = share_ref[0, trace_at + kind : trace_at + kind + 1, :]
+            for t in range(1, n_tp):
+                value = value + share_ref[t, trace_at + kind : trace_at + kind + 1, :]
+            return jnp.sum(value, axis=1, keepdims=True)
+
+        trace_a, trace_g, trace_e = trace_of(0), trace_of(1), trace_of(2)
+        ratio = jnp.sqrt(trace_a / (tokens * inner) / (trace_g / (tokens * width)))
+        ratio_e = jnp.sqrt(tokens / vocab / (trace_e / (tokens * width)))
+
+        rows_e = scale.shape[0]
+        base = (
+            (lax.axis_index("dp") * n_tp + lax.axis_index("tensor")) * rows_e
+        ).astype(jnp.float32)
+        index = lax.broadcasted_iota(jnp.int32, (rows_e, LANES), 0).astype(jnp.float32) + base
+        hits = jnp.zeros((rows_e, LANES), jnp.float32)
+        for t in range(n_tp):
+            for d in range(n_dp):
+                ids = share_ref[t, trace_at + 3 + d : trace_at + 4 + d, :]
+                hits = hits + jnp.where(index == ids, 1.0, 0.0)
+        counts = jnp.sum(hits, axis=1, keepdims=True)
+        scale[...] = jnp.broadcast_to(
+            1.0 / (counts + damp_root * ratio_e), (rows_e, LANES)
+        )
+
+        packed = []
+        for q in range(quads_a):
+            packed.append((own_ref, (), q, quads_a * HEAD + q))
+        for kind in range(2):
+            for t in range(n_tp):
+                for q in range(kind * quads_g, (kind + 1) * quads_g):
+                    packed.append((share_ref, (t,), q, 2 * quads_g * HEAD + q))
+        loaded = [
+            (
+                ref[(*lead, slice(q * HEAD, (q + 1) * HEAD), slice(None))],
+                ref[(*lead, slice(d, d + 1), slice(None))],
+            )
+            for ref, lead, q, d in packed
+        ]
+        pairs = []
+        for i in range(0, len(loaded), 2):
+            pairs += unpack_quads(*loaded[i], *loaded[i + 1])
+
+        row, lane, col = pair_masks()
+        eye = jnp.where(col == row, 1.0, 0.0)
+        shifts = (
+            [damp_root * ratio] * (2 * quads_a)
+            + [damp_root / ratio] * (2 * quads_g * n_tp)
+            + [damp_root / ratio_e] * (2 * quads_g * n_tp)
+        )
+        scaled, over = [], []
+        for pair, shift in zip(pairs, shifts):
+            damped = pair / tokens + shift * eye
+            sums = jnp.sum(jnp.abs(damped), axis=0, keepdims=True)
+            lane_row = lane[:1]
+            bound = jnp.where(
+                lane_row < HALF,
+                jnp.max(jnp.where(lane_row < HALF, sums, 0.0), axis=1, keepdims=True),
+                jnp.max(jnp.where(lane_row < HALF, 0.0, sums), axis=1, keepdims=True),
+            )
+            inverse_bound = 1.0 / bound
+            scaled.append(damped * inverse_bound)
+            over.append(inverse_bound)
+
+        for i in range(len(pairs)):
+            image = scaled[i]
+            approx = 2.0 * eye - image
+            image = 2.0 * image - times_right(image, right_factor(image))
+            for sweep in range(1, NS_ITERS):
+                factor = right_factor(image)
+                if sweep < NS_ITERS - 1:
+                    product = times_right(jnp.concatenate([approx, image], axis=0), factor)
+                    approx = 2.0 * approx - product[:HEAD]
+                    image = 2.0 * image - product[HEAD:]
+                else:
+                    approx = 2.0 * approx - times_right(approx, factor)
+            inverse = approx * over[i]
+            if i < 2 * quads_a:
+                right_a[i] = right_factor(inverse)
+            elif i < 2 * quads_a + 2 * quads_g * n_tp:
+                left_g[i - 2 * quads_a] = left_factor(inverse)
+            else:
+                right_e[i - 2 * quads_a - 2 * quads_g * n_tp] = right_factor(inverse)
+
+    left = times_left(left_g[step], w_ref[...])
+    for h in range(2 * quads_a):
+        at = slice(h * LANES, (h + 1) * LANES)
+        w_out[:, at] = times_right(left[:, at], right_a[h])
+    e_out[...] = times_right(e_ref[...], right_e[step]) * scale[...]
+
+
+def local(acts, out_cot, emb_ids, emb_cot, grad_w, grad_e):
+    n_dp = lax.axis_size("dp")
+    n_tp = lax.axis_size("tensor")
+    layers, tok_rows, inner_part = acts.shape
+    width_part = out_cot.shape[2]
+    width = width_part * n_tp
+    rows_e = grad_e.shape[0]
+    tile_rows = grad_w.shape[0] * n_tp
+    direct = (
+        layers == n_dp
+        and n_dp & (n_dp - 1) == 0
+        and tile_rows == width
+        and inner_part % (2 * LANES) == 0
+        and width_part % (2 * LANES) == 0
+        and (inner_part // (2 * LANES)) % 2 == 0
+        and n_tp % 2 == 0
+        and emb_ids.shape[0] <= LANES
+        and rows_e % ROWS == 0
+    )
+    if not direct:
+        return general_local(acts, out_cot, emb_ids, emb_cot, grad_w, grad_e)
+    quads_a = inner_part // (2 * LANES)
+    quads_g = width_part // (2 * LANES)
+    quads = quads_a + 2 * quads_g
+    dp_index = lax.axis_index("dp")
+    sending = grad_w.reshape(grad_w.shape[0], n_tp, inner_part).transpose(1, 0, 2)
+    tile = lax.all_to_all(sending, "tensor", split_axis=0, concat_axis=0, tiled=True)
+    tile = tile.reshape(tile_rows, inner_part)
+
+    ids_row = jnp.pad(
+        emb_ids.astype(jnp.float32), (0, LANES - emb_ids.shape[0]), constant_values=-1.0
+    ).reshape(1, LANES)
+    payload_rows = -(-(quads * (HEAD + 1) + 1) // ROWS) * ROWS
+    parts = grams(
+        acts, out_cot, emb_cot, ids_row, dp_index, n_dp, quads_a, quads_g, payload_rows
+    )
+    arrived = [parts[0]] + [
+        lax.ppermute(parts[k], "dp", [(i, i ^ k) for i in range(n_dp)])
+        for k in range(n_dp - 1, 0, -1)
+    ]
+    own_rows = -(-quads_a * (HEAD + 1) // ROWS) * ROWS
+    share_rows = -(-(2 * quads_g * (HEAD + 1) + 3 + n_dp) // ROWS) * ROWS
+    own, share = pl.pallas_call(
+        functools.partial(sum_kernel, quads_a, quads_g),
+        out_shape=[
+            jax.ShapeDtypeStruct((own_rows, LANES), jnp.float32),
+            jax.ShapeDtypeStruct((share_rows, LANES), jnp.float32),
+        ],
+        cost_estimate=pl.CostEstimate(flops=1000, bytes_accessed=1000, transcendentals=0),
+        name="sums",
+    )(*arrived)
+    shared = lax.all_gather(share[None], "tensor", axis=0, tiled=True)
+
+    steps = tile_rows // LANES
+    sizes = (
+        quads_a,
+        quads_g,
+        n_tp,
+        n_dp,
+        tok_rows * n_dp,
+        rows_e * n_dp * n_tp,
+        inner_part * n_tp,
+        width,
+    )
+    return pl.pallas_call(
+        functools.partial(invert_apply_kernel, sizes),
+        grid=(steps,),
+        in_specs=[
+            pl.BlockSpec((own_rows, LANES), lambda i: (0, 0)),
+            pl.BlockSpec((n_tp, share_rows, LANES), lambda i: (0, 0, 0)),
+            pl.BlockSpec((LANES, inner_part), lambda i: (i, 0)),
+            pl.BlockSpec((rows_e, LANES), lambda i: (0, i)),
+        ],
+        out_specs=[
+            pl.BlockSpec((LANES, inner_part), lambda i: (i, 0)),
+            pl.BlockSpec((rows_e, LANES), lambda i: (0, i)),
+        ],
+        out_shape=[
+            jax.ShapeDtypeStruct((tile_rows, inner_part), jnp.float32),
+            jax.ShapeDtypeStruct((rows_e, width), jnp.float32),
+        ],
+        scratch_shapes=[
+            pltpu.VMEM((2 * quads_a, 2 * LANES, 2 * LANES), jnp.bfloat16),
+            pltpu.VMEM((steps, 2 * LANES, 2 * LANES), jnp.bfloat16),
+            pltpu.VMEM((steps, 2 * LANES, 2 * LANES), jnp.bfloat16),
+            pltpu.VMEM((rows_e, LANES), jnp.float32),
+        ],
+        compiler_params=pltpu.CompilerParams(vmem_limit_bytes=32 * 1024 * 1024),
+        cost_estimate=pl.CostEstimate(flops=1000, bytes_accessed=1000, transcendentals=0),
+        name="invert_apply",
+    )(own, shared, tile, grad_e)
+
+
 def solution(mesh):
     in_specs = (
         P(None, "dp", "tensor"),

time: 262 us -> 70.4 us (0.27)
  blocking collectives: 92.2 us -> 6.19 us
  waiting for transfers between devices: 74.4 us -> 7.12 us
  local copies, waits for them, and re-layouts: 37.9 us -> 4.57 us
  Pallas kernels: 0 us -> 23.3 us
  matrix products: 22.5 us -> 0 us
  starting transfers between devices: 10 us -> 28.1 us
  between operations: 15.8 us -> 0.66 us
  other arithmetic: 7.31 us -> 0.01 us
    all_gather x2 -> x0, waiting for transfers between devices: 74.4 us -> none  [the longest x1 50.1 us: local(): lax.all_gather(inverse_mine.reshape(owned, HEAD * HEAD), 'dp', axis=0, ti...]
    unnamed x1 -> x0, blocking collectives: 52.6 us -> none
    psum x1 -> x0, blocking collectives: 39.6 us -> none  [local(): traces, counts_all = lax.psum((trace_local, local_counts), ('dp', 'tensor'))]
    ppermute x0 -> x7, starting transfers between devices: none -> 23.7 us  [local(): lax.ppermute(parts[k], 'dp', [(i, i ^ k) for i in range(n_dp)])]
    pallas_call x0 -> x3, Pallas kernels: none -> 23.3 us  [the longest x1 14.1 us: local(): pl.pallas_call(functools.partial(invert_apply_kernel, sizes), grid=(steps...]
    dot_general x14 -> x0, matrix products: 22.5 us -> none  [the longest x1 7.81 us: local(): jnp.einsum('lrhi,lhij->lrhj', left.reshape(layer_span, layer_rows, heads_...]
    unnamed x23 -> x12, local copies, waits for them, and re-layouts: 14.9 us -> 0.9 us
    ppermute x0 -> x7, waiting for transfers between devices: none -> 7.12 us  [local(): lax.ppermute(parts[k], 'dp', [(i, i ^ k) for i in range(n_dp)])]
  transfers between devices with their start and end apart: 5 -> 8, of which waited for: 2 -> 3; matrix products, arithmetic and copies ran while one was open for 8% -> 1% of each run, Pallas kernels for 0% -> 13%
where the time goes in v1:
time: 70.4 us; the launch traced here: 70 us
  starting transfers between devices  28.1 us (40%)
  Pallas kernels  23.3 us (33%)
  waiting for transfers between devices  7.12 us (10%)
  blocking collectives  6.19 us (9%)
  local copies, waits for them, and re-layouts  4.57 us (6%)
    ppermute x7, starting transfers between devices, local(): lax.ppermute(parts[k], 'dp', [(i, i ^ k) for i in range(n_dp)])  23.7 us
    pallas_call x1, Pallas kernels, local(): pl.pallas_call(functools.partial(invert_apply_kernel, sizes), grid=(steps...  14.1 us
    pallas_call x1, Pallas kernels, grams(): pl.pallas_call(functools.partial(gram_kernel, quads_a, quads_g), grid_spe...  7.25 us
    ppermute x7, waiting for transfers between devices, local(): lax.ppermute(parts[k], 'dp', [(i, i ^ k) for i in range(n_dp)])  7.12 us
    all_gather x1, blocking collectives, local(): shared = lax.all_gather(share[None], 'tensor', axis=0, tiled=True)  6.19 us
    all_to_all x1, starting transfers between devices, local(): lax.all_to_all(sending, 'tensor', split_axis=0, concat_axis=0, tiled=True)  4.34 us
    reshape x1, local copies, waits for them, and re-layouts, local(): grad_w.reshape(grad_w.shape[0], n_tp, inner_part).transpose(1, 0, 2)  3.14 us
    pallas_call x1, Pallas kernels, local(): pl.pallas_call(functools.partial(sum_kernel, quads_a, quads_g), out_shape...  2 us
  transfers between devices with their start and end apart: 8, of which 3 were waited for; matrix products, arithmetic and copies ran while one was open for 1% of the time, Pallas kernels for 13%

profile of v1, /device:TPU:0, one launch (start us, length us, event | category | flops | bytes accessed | tf_op | source)
XLA Modules:
  0.0 70.0 jit_solution(4426274355372787405)
XLA Ops:
  0.6 3.1 %copy.11 = f32[32,4,8,512]{3,2,0,1:T(8,128)} copy(f32[32,4,8,512]{3,2,1,0:T(8,128)} %bitcast.15) | data formatting | bytes 4194304 | tf_op jit(solution)/shard_map/reshape | solution.py:450
  3.8 4.3 %all-to-all-start = ((f32[4,256,512]{2,1,0:T(8,128)}), f32[4,256,512]{2,1,0:T(8,128)S(1)}, u32[]{:S(2)}, u32[]{:S(2)}) async-start(f32[4,256,512]{2,1,0:T(8,128)} %bitcast.14), calls=%async_computation | async-start | bytes 4194304 | tf_op jit(solution)/shard_map/all_to_all | solution.py:451
  8.1 0.0 copy-done.5
  8.1 0.5 pad_bitcast_fusion.ids_ref
  8.6 7.2 %grams.1 = (f32[264,128]{1,0:T(8,128)}, f32[264,128]{1,0:T(8,128)}, f32[264,128]{1,0:T(8,128)}, f32[264,128]{1,0:T(8,128)}, f32[264,128]{1,0:T(8,128)}, /*index=...) custom-call(s32[1]{0:T(128)} %bitcast.me_ref, bf16[8,256,512]{2,1,0:T(8,128)(2,1)} %acts_ref.1, ...), custom_call_target="tpu_custom_call" | custom-call | flops 1000 | bytes 1000 | tf_op jit(solution)/shard_map/grams/pallas_call | solution.py:278
  15.9 5.5 %collective-permute-start = (f32[264,128]{1,0:T(8,128)}, f32[264,128]{1,0:T(8,128)S(1)}, u32[]{:S(2)}, u32[]{:S(2)}) collective-permute-start(f32[264,128]{1,0:T(8,128)} %get-tuple-element.13), channel_id=1, source_target_pairs={{0,28},{4,24},{8,20},{12,16},{16,12},{20,8},{24,4},{28,0},{1,29},{... | collective-permute-start | bytes 405512 | tf_op jit(solution)/shard_map/ppermute | solution.py:462
  21.4 0.2 collective-permute-start.1
  21.6 0.7 %collective-permute-start.2 = (f32[264,128]{1,0:T(8,128)}, f32[264,128]{1,0:T(8,128)S(1)}, u32[]{:S(2)}, u32[]{:S(2)}) collective-permute-start(f32[264,128]{1,0:T(8,128)} %get-tuple-element.15), channel_id=1, source_target_pairs={{0,20},{4,16},{8,28},{12,24},{16,4},{20,0},{24,12},{28,8},{1,21},{... | collective-permute-start | bytes 405512 | tf_op jit(solution)/shard_map/ppermute | solution.py:462
  22.3 2.0 %collective-permute-start.3 = (f32[264,128]{1,0:T(8,128)}, f32[264,128]{1,0:T(8,128)}, u32[]{:S(2)}, u32[]{:S(2)}) collective-permute-start(f32[264,128]{1,0:T(8,128)} %get-tuple-element.16), channel_id=1, source_target_pairs={{0,16},{4,20},{8,24},{12,28},{16,0},{20,4},{24,8},{28,12},{1,17},{... | collective-permute-start | bytes 405512 | tf_op jit(solution)/shard_map/ppermute | solution.py:462
  24.4 2.3 %collective-permute-start.4 = (f32[264,128]{1,0:T(8,128)}, f32[264,128]{1,0:T(8,128)}, u32[]{:S(2)}, u32[]{:S(2)}) collective-permute-start(f32[264,128]{1,0:T(8,128)} %get-tuple-element.17), channel_id=1, source_target_pairs={{0,12},{4,8},{8,4},{12,0},{16,28},{20,24},{24,20},{28,16},{1,13},{... | collective-permute-start | bytes 405512 | tf_op jit(solution)/shard_map/ppermute | solution.py:462
  26.7 0.0 collective-permute-done.refs_1_
  26.7 11.5 %collective-permute-start.5 = (f32[264,128]{1,0:T(8,128)}, f32[264,128]{1,0:T(8,128)}, u32[]{:S(2)}, u32[]{:S(2)}) collective-permute-start(f32[264,128]{1,0:T(8,128)} %get-tuple-element.18), channel_id=1, source_target_pairs={{0,8},{4,12},{8,0},{12,4},{16,24},{20,28},{24,16},{28,20},{1,9},{5... | collective-permute-start | bytes 405512 | tf_op jit(solution)/shard_map/ppermute | solution.py:462
  38.1 0.0 collective-permute-done.1.refs_2_
  38.1 1.5 %collective-permute-start.6 = (f32[264,128]{1,0:T(8,128)}, f32[264,128]{1,0:T(8,128)}, u32[]{:S(2)}, u32[]{:S(2)}) collective-permute-start(f32[264,128]{1,0:T(8,128)} %get-tuple-element.19), channel_id=1, source_target_pairs={{0,4},{4,0},{8,12},{12,8},{16,20},{20,16},{24,28},{28,24},{1,5},{5... | collective-permute-start | bytes 405512 | tf_op jit(solution)/shard_map/ppermute | solution.py:462
  39.6 3.2 %collective-permute-done.2.refs_3_ = f32[264,128]{1,0:T(8,128)S(1)} collective-permute-done((f32[264,128]{1,0:T(8,128)}, f32[264,128]{1,0:T(8,128)S(1)}, u32[]{:S(2)}, u32[]{:S(2)}) %collective-permute-start.2) | collective-permute-done | bytes 135200 | tf_op jit(solution)/shard_map/ppermute | solution.py:462
  42.8 2.6 %collective-permute-done.3.refs_4_ = f32[264,128]{1,0:T(8,128)} collective-permute-done((f32[264,128]{1,0:T(8,128)}, f32[264,128]{1,0:T(8,128)}, u32[]{:S(2)}, u32[]{:S(2)}) %collective-permute-start.3) | collective-permute-done | bytes 135200 | tf_op jit(solution)/shard_map/ppermute | solution.py:462
  45.4 0.0 collective-permute-done.4.refs_5_
  45.4 1.3 %collective-permute-done.5.refs_6_ = f32[264,128]{1,0:T(8,128)} collective-permute-done((f32[264,128]{1,0:T(8,128)}, f32[264,128]{1,0:T(8,128)}, u32[]{:S(2)}, u32[]{:S(2)}) %collective-permute-start.5) | collective-permute-done | bytes 135200 | tf_op jit(solution)/shard_map/ppermute | solution.py:462
  46.8 0.0 collective-permute-done.6.refs_7_
  46.8 2.0 %sums.1 = (f32[136,128]{1,0:T(8,128)}, f32[144,128]{1,0:T(8,128)}) custom-call(f32[264,128]{1,0:T(8,128)} %get-tuple-element.12.refs_0_, f32[264,128]{1,0:T(8,128)} %copy-done.2, f32[264,128]{1,0:T(8,128)} %copy-done.3, f32[264,128]{1,0:T(8,128)} %copy-done.4, f32[264,128]{1,0:T(8,128)} %collective-permute-done.3.refs_4_, ...), custom_call_target="tpu_custom_call" | custom-call | flops 1000 | bytes 1000 | tf_op jit(solution)/shard_map/sums/pallas_call | solution.py:467
  48.8 6.2 %all-gather = f32[576,128]{1,0:T(8,128)S(1)} all-gather(f32[144,128]{1,0:T(8,128)} %get-tuple-element.21), channel_id=2, replica_groups=mesh['dp'=8,'tensor'=4] {'tensor'}, dimensions={0}, use_global_device_ids=true | all-gather | bytes 368640 | tf_op jit(solution)/shard_map/all_gather | solution.py:476
  55.0 0.0 all-to-all-done
  55.0 0.9 %copy-done.1 = f32[136,128]{1,0:T(8,128)S(1)} copy-done((f32[136,128]{1,0:T(8,128)S(1)}, f32[136,128]{1,0:T(8,128)}, u32[]{:S(2)}) %copy-start.1) | copy-done | bytes 69656
  55.9 14.1 %invert_apply.1 = (f32[1024,512]{1,0:T(8,128)}, f32[256,1024]{1,0:T(8,128)}) custom-call(f32[136,128]{1,0:T(8,128)S(1)} %copy-done.1, f32[4,144,128]{2,1,0:T(8,128)S(1)} %bitcast.13, f32[1024,512]{1,0:T(8,128)S(1)} %bitcast.12, f32[256,1024]{1,0:T(8,128)S(1)} %copy-done), custom_call_target="tpu_custom_call" | custom-call | flops 1000 | bytes 1000 | tf_op jit(solution)/shard_map/invert_apply/pallas_call | solution.py:489
  (11 shorter events, 0.0 us)
Async XLA Ops:
  3.8 4.3 %copy-start.5 = (s32[64]{0:T(128)S(1)}, s32[64]{0:T(128)}, u32[]{:S(2)}) copy-start(s32[64]{0:T(128)} %param.8) | copy-start | bytes 772
  3.8 51.2 %all-to-all-start = ((f32[4,256,512]{2,1,0:T(8,128)}), f32[4,256,512]{2,1,0:T(8,128)S(1)}, u32[]{:S(2)}, u32[]{:S(2)}) async-start(f32[4,256,512]{2,1,0:T(8,128)} %bitcast.14), calls=%async_computation | async-start | bytes 4194304 | tf_op jit(solution)/shard_map/all_to_all | solution.py:451
  8.6 46.3 %copy-start = (f32[256,1024]{1,0:T(8,128)S(1)}, f32[256,1024]{1,0:T(8,128)}, u32[]{:S(2)}) copy-start(f32[256,1024]{1,0:T(8,128)} %e_ref.1) | copy-start | bytes 3145732
  15.9 10.8 %collective-permute-start = (f32[264,128]{1,0:T(8,128)}, f32[264,128]{1,0:T(8,128)S(1)}, u32[]{:S(2)}, u32[]{:S(2)}) collective-permute-start(f32[264,128]{1,0:T(8,128)} %get-tuple-element.13), channel_id=1, source_target_pairs={{0,28},{4,24},{8,20},{12,16},{16,12},{20,8},{24,4},{28,0},{1,29},{... | collective-permute-start | bytes 405512 | tf_op jit(solution)/shard_map/ppermute | solution.py:462
  21.4 16.8 %collective-permute-start.1 = (f32[264,128]{1,0:T(8,128)}, f32[264,128]{1,0:T(8,128)S(1)}, u32[]{:S(2)}, u32[]{:S(2)}) collective-permute-start(f32[264,128]{1,0:T(8,128)} %get-tuple-element.14), channel_id=1, source_target_pairs={{0,24},{4,28},{8,16},{12,20},{16,8},{20,12},{24,0},{28,4},{1,25},{... | collective-permute-start | bytes 405512 | tf_op jit(solution)/shard_map/ppermute | solution.py:462
  21.6 21.2 %collective-permute-start.2 = (f32[264,128]{1,0:T(8,128)}, f32[264,128]{1,0:T(8,128)S(1)}, u32[]{:S(2)}, u32[]{:S(2)}) collective-permute-start(f32[264,128]{1,0:T(8,128)} %get-tuple-element.15), channel_id=1, source_target_pairs={{0,20},{4,16},{8,28},{12,24},{16,4},{20,0},{24,12},{28,8},{1,21},{... | collective-permute-start | bytes 405512 | tf_op jit(solution)/shard_map/ppermute | solution.py:462
  22.3 23.1 %collective-permute-start.3 = (f32[264,128]{1,0:T(8,128)}, f32[264,128]{1,0:T(8,128)}, u32[]{:S(2)}, u32[]{:S(2)}) collective-permute-start(f32[264,128]{1,0:T(8,128)} %get-tuple-element.16), channel_id=1, source_target_pairs={{0,16},{4,20},{8,24},{12,28},{16,0},{20,4},{24,8},{28,12},{1,17},{... | collective-permute-start | bytes 405512 | tf_op jit(solution)/shard_map/ppermute | solution.py:462
  24.4 21.0 %collective-permute-start.4 = (f32[264,128]{1,0:T(8,128)}, f32[264,128]{1,0:T(8,128)}, u32[]{:S(2)}, u32[]{:S(2)}) collective-permute-start(f32[264,128]{1,0:T(8,128)} %get-tuple-element.17), channel_id=1, source_target_pairs={{0,12},{4,8},{8,4},{12,0},{16,28},{20,24},{24,20},{28,16},{1,13},{... | collective-permute-start | bytes 405512 | tf_op jit(solution)/shard_map/ppermute | solution.py:462
  26.7 20.1 %copy-start.2 = (f32[264,128]{1,0:T(8,128)}, f32[264,128]{1,0:T(8,128)S(1)}, u32[]{:S(2)}) copy-start(f32[264,128]{1,0:T(8,128)S(1)} %collective-permute-done.refs_1_) | copy-start | bytes 405508
  26.7 20.1 %collective-permute-start.5 = (f32[264,128]{1,0:T(8,128)}, f32[264,128]{1,0:T(8,128)}, u32[]{:S(2)}, u32[]{:S(2)}) collective-permute-start(f32[264,128]{1,0:T(8,128)} %get-tuple-element.18), channel_id=1, source_target_pairs={{0,8},{4,12},{8,0},{12,4},{16,24},{20,28},{24,16},{28,20},{1,9},{5... | collective-permute-start | bytes 405512 | tf_op jit(solution)/shard_map/ppermute | solution.py:462
  38.1 8.6 %copy-start.3 = (f32[264,128]{1,0:T(8,128)}, f32[264,128]{1,0:T(8,128)S(1)}, u32[]{:S(2)}) copy-start(f32[264,128]{1,0:T(8,128)S(1)} %collective-permute-done.1.refs_2_) | copy-start | bytes 405508
  38.1 8.6 %collective-permute-start.6 = (f32[264,128]{1,0:T(8,128)}, f32[264,128]{1,0:T(8,128)}, u32[]{:S(2)}, u32[]{:S(2)}) collective-permute-start(f32[264,128]{1,0:T(8,128)} %get-tuple-element.19), channel_id=1, source_target_pairs={{0,4},{4,0},{8,12},{12,8},{16,20},{20,16},{24,28},{28,24},{1,5},{5... | collective-permute-start | bytes 405512 | tf_op jit(solution)/shard_map/ppermute | solution.py:462
  42.8 4.0 %copy-start.4 = (f32[264,128]{1,0:T(8,128)}, f32[264,128]{1,0:T(8,128)S(1)}, u32[]{:S(2)}) copy-start(f32[264,128]{1,0:T(8,128)S(1)} %collective-permute-done.2.refs_3_) | copy-start | bytes 405508
  55.0 0.9 %copy-start.1 = (f32[136,128]{1,0:T(8,128)S(1)}, f32[136,128]{1,0:T(8,128)}, u32[]{:S(2)}) copy-start(f32[136,128]{1,0:T(8,128)} %get-tuple-element.20.own_ref) | copy-start | bytes 208900

commit v2 on v0

--- a/solution.py
+++ b/solution.py
@@ -1,10 +1,17 @@
+import functools
+
 import jax
 import jax.numpy as jnp
 from jax import lax
+from jax.experimental import pallas as pl
+from jax.experimental.pallas import tpu as pltpu
 from jax.sharding import PartitionSpec as P
 
 HEAD = 64
 NS_ITERS = 4
+LANES = 128
+HALF = HEAD
+ROWS = 8
 
 
 damp_root = 0.7
@@ -23,7 +30,7 @@
     return approx
 
 
-def local(acts, out_cot, emb_ids, emb_cot, grad_w, grad_e):
+def general_local(acts, out_cot, emb_ids, emb_cot, grad_w, grad_e):
     n_dp = lax.axis_size("dp")
     n_tp = lax.axis_size("tensor")
     layers, tok_rows, inner_part = acts.shape
@@ -135,6 +142,484 @@
     return (update_w, update_e)
 
 
+def pair_masks():
+    row = lax.broadcasted_iota(jnp.int32, (HEAD, LANES), 0)
+    lane = lax.broadcasted_iota(jnp.int32, (HEAD, LANES), 1)
+    col = jnp.where(lane < HALF, lane, lane - HALF)
+    return row, lane, col
+
+
+def gram_pair(rows):
+    full = lax.dot_general(
+        rows, rows, (((0,), (0,)), ((), ())), preferred_element_type=jnp.float32
+    )
+    _, lane, _ = pair_masks()
+    return jnp.where(lane < HALF, full[:HEAD], full[HEAD:])
+
+
+def pack_quad(first, second):
+    row, _, col = pair_masks()
+    quad = jnp.where(col >= row, first, second)
+    diagonal = jnp.sum(jnp.where(col == row, second, 0.0), axis=0, keepdims=True)
+    return quad, diagonal
+
+
+def unpack_quads(quad_a, diag_a, quad_b, diag_b):
+    row, lane, col = pair_masks()
+    turned = jnp.concatenate([quad_a, quad_b], axis=0).T
+    top, low = turned[:HEAD], turned[HEAD:]
+    turn_a = jnp.where(lane < HALF, top, pltpu.roll(low, HALF, 1))
+    turn_b = jnp.where(lane < HALF, pltpu.roll(top, HALF, 1), low)
+
+    def both(quad, turn, diag):
+        first = jnp.where(col >= row, quad, turn)
+        second = jnp.where(col < row, quad, jnp.where(col == row, diag, turn))
+        return first, second
+
+    return both(quad_a, turn_a, diag_a) + both(quad_b, turn_b, diag_b)
+
+
+def split(value):
+    high = value.astype(jnp.bfloat16)
+    low = (value - high.astype(jnp.float32)).astype(jnp.bfloat16)
+    return high, low
+
+
+def block_diagonal(pair):
+    row = lax.broadcasted_iota(jnp.int32, (LANES, LANES), 0)
+    lane = lax.broadcasted_iota(jnp.int32, (LANES, LANES), 1)
+    double = jnp.concatenate([pair, pair], axis=0)
+    return jnp.where((row < HALF) == (lane < HALF), double, jnp.zeros_like(double))
+
+
+def blocks_right(high, low):
+    wide = jnp.concatenate([block_diagonal(high), block_diagonal(low)], axis=1)
+    return jnp.concatenate([wide, wide], axis=0)
+
+
+def blocks_left(high, low):
+    high, low = block_diagonal(high), block_diagonal(low)
+    return jnp.concatenate(
+        [jnp.concatenate([high, high], axis=1), jnp.concatenate([low, low], axis=1)], axis=0
+    )
+
+
+def add_halves(both):
+    return both[:, :LANES] + both[:, LANES:]
+
+
+def split_times(parts, factor):
+    return add_halves(
+        jnp.dot(jnp.concatenate(parts, axis=1), factor, preferred_element_type=jnp.float32)
+    )
+
+
+def gram_kernel(counts, me_ref, ids_ref, acts_hbm, cot_hbm, emb_hbm, w_hbm, *refs):
+    quads_a, quads_g, n_dp, n_tp = counts
+    half = n_dp // 2
+    outs, w_out = refs[:half], refs[half]
+    acts, cot, emb, acts_sem, cot_sem, emb_sem, w_sem = refs[half + 1 :]
+    me = me_ref[0]
+    order = [k for j in list(range(1, half)) + [0] for k in (j, j + half)]
+
+    def fetch(k):
+        layer = lax.bitwise_xor(me, k)
+        return (
+            pltpu.make_async_copy(acts_hbm.at[layer], acts.at[k], acts_sem.at[k]),
+            pltpu.make_async_copy(cot_hbm.at[layer], cot.at[k], cot_sem.at[k]),
+        )
+
+    emb_copy = pltpu.make_async_copy(emb_hbm, emb, emb_sem)
+    emb_copy.start()
+    for k in order:
+        for copy in fetch(k):
+            copy.start()
+    part = w_hbm.shape[1] // n_tp
+    moves = [
+        pltpu.make_async_copy(w_hbm.at[:, pl.ds(t * part, part)], w_out.at[t], w_sem.at[t])
+        for t in range(n_tp)
+    ]
+    for move in moves:
+        move.start()
+
+    def pack(source, at):
+        first = gram_pair(source[:, at * 2 * LANES : (at * 2 + 1) * LANES])
+        second = gram_pair(source[:, (at * 2 + 1) * LANES : (at * 2 + 2) * LANES])
+        return pack_quad(first, second)
+
+    emb_copy.wait()
+    emb_rows = emb[...]
+    packed_e = [pack(emb_rows, q) for q in range(quads_g)]
+    ids = jnp.concatenate(
+        [
+            ids_ref[...].astype(jnp.float32),
+            jnp.full((1, LANES - ids_ref.shape[1]), -1.0, jnp.float32),
+        ],
+        axis=1,
+    )
+    for j in list(range(1, half)) + [0]:
+        packed = []
+        for k in (j, j + half):
+            for copy in fetch(k):
+                copy.wait()
+            rows_a, rows_g = acts[k], cot[k]
+            packed += [pack(rows_a, q) for q in range(quads_a)]
+            packed += [pack(rows_g, q) for q in range(quads_g)]
+        packed += packed_e
+        for q, (quad, diagonal) in enumerate(packed):
+            outs[j][q * HEAD : (q + 1) * HEAD, :] = quad
+            at = len(packed) * HEAD + q
+            outs[j][at : at + 1, :] = diagonal
+        at = len(packed) * (HEAD + 1)
+        outs[j][at : at + 1, :] = ids
+    for move in moves:
+        move.wait()
+
+
+def small_cost():
+    return pl.CostEstimate(flops=1000, bytes_accessed=1000, transcendentals=0)
+
+
+def round_up(value, unit):
+    return -(-value // unit) * unit
+
+
+def grams(acts, out_cot, emb_cot, emb_ids, grad_w, dp_index, n_dp, n_tp, quads_a, quads_g):
+    layers, rows, width_a = acts.shape
+    width_g = out_cot.shape[2]
+    half = n_dp // 2
+    payload_rows = round_up((2 * (quads_a + quads_g) + quads_g) * (HEAD + 1) + 1, ROWS)
+    part = grad_w.shape[1] // n_tp
+    vmem = pl.BlockSpec(memory_space=pltpu.VMEM)
+    hbm = pl.BlockSpec(memory_space=pltpu.HBM)
+    return pl.pallas_call(
+        functools.partial(gram_kernel, (quads_a, quads_g, n_dp, n_tp)),
+        in_specs=[pl.BlockSpec(memory_space=pltpu.SMEM), vmem, hbm, hbm, hbm, hbm],
+        out_specs=[vmem] * half + [hbm],
+        out_shape=[jax.ShapeDtypeStruct((payload_rows, LANES), jnp.float32)] * half
+        + [jax.ShapeDtypeStruct((n_tp, grad_w.shape[0], part), jnp.float32)],
+        scratch_shapes=[
+            pltpu.VMEM((layers, rows, width_a), jnp.bfloat16),
+            pltpu.VMEM((layers, rows, width_g), jnp.bfloat16),
+            pltpu.VMEM((rows, width_g), jnp.bfloat16),
+            pltpu.SemaphoreType.DMA((layers,)),
+            pltpu.SemaphoreType.DMA((layers,)),
+            pltpu.SemaphoreType.DMA,
+            pltpu.SemaphoreType.DMA((n_tp,)),
+        ],
+        compiler_params=pltpu.CompilerParams(vmem_limit_bytes=32 * 1024 * 1024),
+        cost_estimate=small_cost(),
+        name="grams",
+    )(dp_index.reshape(1), emb_ids.reshape(1, -1), acts, out_cot, emb_cot, grad_w)
+
+
+def half_sum_kernel(quads_layer, quads_g, *refs):
+    parts, outs = refs[:-2], refs[-2:]
+    quads_in = 2 * quads_layer + quads_g
+    quads_out = quads_layer + quads_g
+
+    def total(at, size):
+        value = parts[0][at : at + size, :]
+        for part in parts[1:]:
+            value = value + part[at : at + size, :]
+        return value
+
+    shared = [
+        (total(q * HEAD, HEAD), total(quads_in * HEAD + q, 1))
+        for q in range(2 * quads_layer, quads_in)
+    ]
+    for place, out in enumerate(outs):
+        both = [
+            (total(q * HEAD, HEAD), total(quads_in * HEAD + q, 1))
+            for q in range(place * quads_layer, (place + 1) * quads_layer)
+        ]
+        for q, (quad, diagonal) in enumerate(both + shared):
+            out[q * HEAD : (q + 1) * HEAD, :] = quad
+            out[quads_out * HEAD + q : quads_out * HEAD + q + 1, :] = diagonal
+        at = quads_out * (HEAD + 1)
+        for i, part in enumerate(parts):
+            ids_at = quads_in * (HEAD + 1)
+            out[at + i : at + i + 1, :] = part[ids_at : ids_at + 1, :]
+
+
+def sum_kernel(quads_a, quads_g, half, kept, came, own_ref, share_ref):
+    quads = quads_a + 2 * quads_g
+    diag_at = quads * HEAD
+    row, _, col = pair_masks()
+    traces = []
+    first = 0
+    for count, where in ((quads_a, own_ref), (quads_g, share_ref), (quads_g, share_ref)):
+        trace = jnp.zeros((1, LANES), jnp.float32)
+        for q in range(first, first + count):
+            at = slice(q * HEAD, (q + 1) * HEAD)
+            quad = kept[at, :] + came[at, :]
+            at = slice(diag_at + q, diag_at + q + 1)
+            diagonal = kept[at, :] + came[at, :]
+            trace = trace + diagonal
+            trace = trace + jnp.sum(jnp.where(col == row, quad, 0.0), axis=0, keepdims=True)
+            if where is own_ref:
+                own_ref[q * HEAD : (q + 1) * HEAD, :] = quad
+                own_ref[quads_a * HEAD + q : quads_a * HEAD + q + 1, :] = diagonal
+            else:
+                at = q - quads_a
+                share_ref[at * HEAD : (at + 1) * HEAD, :] = quad
+                share_ref[2 * quads_g * HEAD + at : 2 * quads_g * HEAD + at + 1, :] = diagonal
+        traces.append(trace)
+        first += count
+    at = 2 * quads_g * (HEAD + 1)
+    for trace in traces:
+        share_ref[at : at + 1, :] = trace
+        at += 1
+    for ref in (kept, came):
+        for i in range(half):
+            ids_at = quads * (HEAD + 1) + i
+            share_ref[at : at + 1, :] = ref[ids_at : ids_at + 1, :]
+            at += 1
+
+
+def invert_apply_kernel(sizes, own_ref, share_hbm, w_hbm, e_hbm, w_out, e_out, *scratch):
+    quads_a, quads_g, n_tp, n_dp, tokens, vocab, inner, width, chunk = sizes
+    share, w_in, e_in, w_done, e_done, share_sem, w_sem, e_sem, w_out_sem, e_out_sem = scratch
+    tile_rows, inner_part = w_in.shape
+    rows_e = e_in.shape[0]
+    chunks = tile_rows // chunk
+    e_parts = 2
+    e_cols = width // e_parts
+    share_copy = pltpu.make_async_copy(share_hbm, share, share_sem)
+    w_loads = [
+        pltpu.make_async_copy(
+            w_hbm.at[pl.ds(c * chunk, chunk)], w_in.at[pl.ds(c * chunk, chunk)], w_sem.at[c]
+        )
+        for c in range(chunks)
+    ]
+    e_load = pltpu.make_async_copy(e_hbm, e_in, e_sem)
+    share_copy.start()
+    e_load.start()
+    for load in w_loads:
+        load.start()
+    share_copy.wait()
+
+    trace_at = 2 * quads_g * (HEAD + 1)
+
+    def trace_of(kind):
+        value = share[0, trace_at + kind : trace_at + kind + 1, :]
+        for t in range(1, n_tp):
+            value = value + share[t, trace_at + kind : trace_at + kind + 1, :]
+        return jnp.sum(value, axis=1, keepdims=True)
+
+    trace_a, trace_g, trace_e = trace_of(0), trace_of(1), trace_of(2)
+    ratio = jnp.sqrt(trace_a / (tokens * inner) / (trace_g / (tokens * width)))
+    ratio_e = jnp.sqrt(tokens / vocab / (trace_e / (tokens * width)))
+
+    loaded = [
+        (
+            own_ref[q * HEAD : (q + 1) * HEAD, :],
+            own_ref[quads_a * HEAD + q : quads_a * HEAD + q + 1, :],
+        )
+        for q in range(quads_a)
+    ]
+    diag_at = 2 * quads_g * HEAD
+    for kind in range(2):
+        for t in range(n_tp):
+            for q in range(kind * quads_g, (kind + 1) * quads_g):
+                loaded.append(
+                    (
+                        share[t, q * HEAD : (q + 1) * HEAD, :],
+                        share[t, diag_at + q : diag_at + q + 1, :],
+                    )
+                )
+    pairs = []
+    for i in range(0, len(loaded), 2):
+        pairs += unpack_quads(*loaded[i], *loaded[i + 1])
+    n_a, n_g = 2 * quads_a, 2 * quads_g * n_tp
+
+    row, lane, col = pair_masks()
+    eye = jnp.where(col == row, 1.0, 0.0)
+    low_lane = lane[:1] < HALF
+    shifts = [damp_root * ratio] * n_a + [damp_root / ratio] * n_g + [damp_root / ratio_e] * n_g
+    images, over = [], []
+    for pair, shift in zip(pairs, shifts):
+        damped = pair * (1.0 / tokens) + shift * eye
+        sums = jnp.sum(jnp.abs(damped), axis=0, keepdims=True)
+        bound = jnp.where(
+            low_lane,
+            jnp.max(jnp.where(low_lane, sums, 0.0), axis=1, keepdims=True),
+            jnp.max(jnp.where(low_lane, 0.0, sums), axis=1, keepdims=True),
+        )
+        inverse_bound = 1.0 / bound
+        images.append(damped * inverse_bound)
+        over.append(inverse_bound)
+    approx = [2.0 * eye - image for image in images]
+    for sweep in range(NS_ITERS):
+        splits = [split(image) for image in images]
+        factors = [blocks_right(*parts) for parts in splits]
+        if sweep == 0:
+            images = [
+                2.0 * image - split_times(parts, factor)
+                for image, parts, factor in zip(images, splits, factors)
+            ]
+        elif sweep < NS_ITERS - 1:
+            products = []
+            for value, parts, factor in zip(approx, splits, factors):
+                stacked = [
+                    jnp.concatenate([a, b], axis=0) for a, b in zip(split(value), parts)
+                ]
+                products.append(split_times(stacked, factor))
+            approx = [2.0 * a - p[:HEAD] for a, p in zip(approx, products)]
+            images = [2.0 * b - p[HEAD:] for b, p in zip(images, products)]
+        else:
+            approx = [
+                2.0 * a - split_times(split(a), factor) for a, factor in zip(approx, factors)
+            ]
+    inverses = [split(a * b) for a, b in zip(approx, over)]
+    right_a = [blocks_right(*parts) for parts in inverses[:n_a]]
+
+    base = ((lax.axis_index("dp") * n_tp + lax.axis_index("tensor")) * rows_e).astype(jnp.float32)
+    index = lax.broadcasted_iota(jnp.int32, (rows_e, LANES), 0).astype(jnp.float32) + base
+    hits = jnp.zeros((rows_e, LANES), jnp.float32)
+    for t in range(n_tp):
+        for d in range(n_dp):
+            ids = share[t, trace_at + 3 + d : trace_at + 4 + d, :]
+            hits = hits + jnp.where(index == ids, 1.0, 0.0)
+    scale = 1.0 / (jnp.sum(hits, axis=1, keepdims=True) + damp_root * ratio_e)
+
+    e_load.wait()
+    stores = []
+    for p in range(e_parts):
+        for i in range(p * n_g // e_parts, (p + 1) * n_g // e_parts):
+            at = slice(i * LANES, (i + 1) * LANES)
+            factor = blocks_right(*inverses[n_a + n_g + i])
+            e_done[:, at] = split_times(split(e_in[:, at]), factor) * scale
+        cols = pl.ds(p * e_cols, e_cols)
+        stores.append(
+            pltpu.make_async_copy(e_done.at[:, cols], e_out.at[:, cols], e_out_sem.at[p])
+        )
+        stores[-1].start()
+    per_chunk = chunk // LANES
+    for c in range(chunks):
+        w_loads[c].wait()
+        for i in range(c * per_chunk, (c + 1) * per_chunk):
+            rows = slice(i * LANES, (i + 1) * LANES)
+            factor = blocks_left(*inverses[n_a + i])
+            both = jnp.dot(
+                factor,
+                jnp.concatenate(split(w_in[rows, :]), axis=0),
+                preferred_element_type=jnp.float32,
+            )
+            left = both[:LANES] + both[LANES:]
+            for h in range(n_a):
+                at = slice(h * LANES, (h + 1) * LANES)
+                w_done[rows, at] = split_times(split(left[:, at]), right_a[h])
+        rows = pl.ds(c * chunk, chunk)
+        stores.append(
+            pltpu.make_async_copy(w_done.at[rows], w_out.at[rows], w_out_sem.at[c])
+        )
+        stores[-1].start()
+    for store in stores:
+        store.wait()
+
+
+def invert_apply(own, shared, tile, grad_e, sizes):
+    n_tp = shared.shape[0]
+    chunk = sizes[-1]
+    tile_rows, inner_part = tile.shape
+    rows_e, width = grad_e.shape
+    vmem = pl.BlockSpec(memory_space=pltpu.VMEM)
+    hbm = pl.BlockSpec(memory_space=pltpu.HBM)
+    return pl.pallas_call(
+        functools.partial(invert_apply_kernel, sizes),
+        in_specs=[vmem, hbm, hbm, hbm],
+        out_specs=[hbm, hbm],
+        out_shape=[
+            jax.ShapeDtypeStruct((tile_rows, inner_part), jnp.float32),
+            jax.ShapeDtypeStruct((rows_e, width), jnp.float32),
+        ],
+        scratch_shapes=[
+            pltpu.VMEM(shared.shape, jnp.float32),
+            pltpu.VMEM(tile.shape, jnp.float32),
+            pltpu.VMEM(grad_e.shape, jnp.float32),
+            pltpu.VMEM(tile.shape, jnp.float32),
+            pltpu.VMEM(grad_e.shape, jnp.float32),
+            pltpu.SemaphoreType.DMA,
+            pltpu.SemaphoreType.DMA((tile_rows // chunk,)),
+            pltpu.SemaphoreType.DMA,
+            pltpu.SemaphoreType.DMA((tile_rows // chunk,)),
+            pltpu.SemaphoreType.DMA((2,)),
+        ],
+        compiler_params=pltpu.CompilerParams(vmem_limit_bytes=32 * 1024 * 1024),
+        cost_estimate=small_cost(),
+        name="invert_apply",
+    )(own, shared, tile, grad_e)
+
+
+def local(acts, out_cot, emb_ids, emb_cot, grad_w, grad_e):
+    n_dp = lax.axis_size("dp")
+    n_tp = lax.axis_size("tensor")
+    layers, tok_rows, inner_part = acts.shape
+    width_part = out_cot.shape[2]
+    width = width_part * n_tp
+    rows_e = grad_e.shape[0]
+    tile_rows = grad_w.shape[0] * n_tp
+    direct = (
+        layers == n_dp
+        and n_dp > 1
+        and n_dp & (n_dp - 1) == 0
+        and tile_rows == width
+        and inner_part % (4 * LANES) == 0
+        and width_part % (2 * LANES) == 0
+        and n_tp % 2 == 0
+        and emb_ids.shape[0] < LANES
+        and rows_e % ROWS == 0
+    )
+    if not direct:
+        return general_local(acts, out_cot, emb_ids, emb_cot, grad_w, grad_e)
+    quads_a = inner_part // (2 * LANES)
+    quads_g = width_part // (2 * LANES)
+    half = n_dp // 2
+
+    def trade(value, k):
+        return lax.ppermute(value, "dp", [(i, i ^ k) for i in range(n_dp)])
+
+    *parts, sending = grams(
+        acts, out_cot, emb_cot, emb_ids, grad_w, lax.axis_index("dp"), n_dp, n_tp, quads_a, quads_g
+    )
+    tile = lax.all_to_all(sending, "tensor", split_axis=0, concat_axis=0, tiled=True)
+    tile = tile.reshape(tile_rows, inner_part)
+    arrived = [parts[0]] + [trade(parts[k], k) for k in range(1, half)]
+    kept_rows = round_up((quads_a + 2 * quads_g) * (HEAD + 1) + half, ROWS)
+    kept, mirror = pl.pallas_call(
+        functools.partial(half_sum_kernel, quads_a + quads_g, quads_g),
+        out_shape=[jax.ShapeDtypeStruct((kept_rows, LANES), jnp.float32)] * 2,
+        cost_estimate=small_cost(),
+        name="half_sums",
+    )(*arrived)
+    came = trade(mirror, half)
+    own_rows = round_up(quads_a * (HEAD + 1), ROWS)
+    share_rows = round_up(2 * quads_g * (HEAD + 1) + 3 + n_dp, ROWS)
+    own, share = pl.pallas_call(
+        functools.partial(sum_kernel, quads_a, quads_g, half),
+        out_shape=[
+            jax.ShapeDtypeStruct((own_rows, LANES), jnp.float32),
+            jax.ShapeDtypeStruct((share_rows, LANES), jnp.float32),
+        ],
+        cost_estimate=small_cost(),
+        name="sums",
+    )(kept, came)
+    shared = lax.all_gather(share[None], "tensor", axis=0, tiled=True)
+    sizes = (
+        quads_a,
+        quads_g,
+        n_tp,
+        n_dp,
+        tok_rows * n_dp,
+        rows_e * n_dp * n_tp,
+        inner_part * n_tp,
+        width,
+        2 * LANES,
+    )
+    return tuple(invert_apply(own, shared, tile, grad_e, sizes))
+
+
 def solution(mesh):
     in_specs = (
         P(None, "dp", "tensor"),

time: 262 us -> 62.8 us (0.24)
  blocking collectives: 92.2 us -> 6.07 us
  waiting for transfers between devices: 74.4 us -> 17.5 us
  local copies, waits for them, and re-layouts: 37.9 us -> 11.6 us
  matrix products: 22.5 us -> 0 us
  Pallas kernels: 0 us -> 15.4 us
  between operations: 15.8 us -> 0.68 us
  other arithmetic: 7.31 us -> 0 us
    all_gather x2 -> x0, waiting for transfers between devices: 74.4 us -> none  [the longest x1 50.1 us: local(): lax.all_gather(inverse_mine.reshape(owned, HEAD * HEAD), 'dp', axis=0, ti...]
    unnamed x1 -> x0, blocking collectives: 52.6 us -> none
    psum x1 -> x0, blocking collectives: 39.6 us -> none  [local(): traces, counts_all = lax.psum((trace_local, local_counts), ('dp', 'tensor'))]
    dot_general x14 -> x0, matrix products: 22.5 us -> none  [the longest x1 7.81 us: local(): jnp.einsum('lrhi,lhij->lrhj', left.reshape(layer_span, layer_rows, heads_...]
    ppermute x0 -> x4, waiting for transfers between devices: none -> 17.5 us  [trade(): return lax.ppermute(value, 'dp', [(i, i ^ k) for i in range(n_dp)])]
    pallas_call x0 -> x4, Pallas kernels: none -> 15.4 us  [the longest x1 6.99 us: invert_apply(): pl.pallas_call(functools.partial(invert_apply_kernel, sizes), in_specs=[v...]
    ppermute x0 -> x4, starting transfers between devices: none -> 6.77 us  [trade(): return lax.ppermute(value, 'dp', [(i, i ^ k) for i in range(n_dp)])]
    reshape x8 -> x0, local copies, waits for them, and re-layouts: 6.1 us -> none  [the longest x1 3.03 us: local(): shared[:, :layers * groups_part]]
  transfers between devices with their start and end apart: 5 -> 5, of which waited for: 2 -> 4; matrix products, arithmetic and copies ran while one was open for 8% -> 0% of each run, Pallas kernels for 0% -> 6%
where the time goes in v2:
time: 62.8 us; the launch traced here: 62.3 us
  waiting for transfers between devices  17.5 us (28%)
  Pallas kernels  15.4 us (25%)
  local copies, waits for them, and re-layouts  11.6 us (18%)
  starting transfers between devices  11.1 us (18%)
  blocking collectives  6.07 us (10%)
  between operations  0.68 us (1%)
    ppermute x4, waiting for transfers between devices, trade(): return lax.ppermute(value, 'dp', [(i, i ^ k) for i in range(n_dp)])  17.5 us
    unnamed x30, local copies, waits for them, and re-layouts  11.6 us
    pallas_call x1, Pallas kernels, invert_apply(): pl.pallas_call(functools.partial(invert_apply_kernel, sizes), in_specs=[v...  6.99 us
    ppermute x4, starting transfers between devices, trade(): return lax.ppermute(value, 'dp', [(i, i ^ k) for i in range(n_dp)])  6.77 us
    all_gather x1, blocking collectives, local(): shared = lax.all_gather(share[None], 'tensor', axis=0, tiled=True)  6.07 us
    pallas_call x1, Pallas kernels, grams(): pl.pallas_call(functools.partial(gram_kernel, (quads_a, quads_g, n_dp, n_...  4.76 us
    all_to_all x1, starting transfers between devices, local(): lax.all_to_all(sending, 'tensor', split_axis=0, concat_axis=0, tiled=True)  4.34 us
    pallas_call x1, Pallas kernels, local(): pl.pallas_call(functools.partial(half_sum_kernel, quads_a + quads_g, quad...  2.03 us
  transfers between devices with their start and end apart: 5, of which 4 were waited for; matrix products, arithmetic and copies ran while one was open for 0% of the time, Pallas kernels for 6%

profile of v2, /device:TPU:0, one launch (start us, length us, event | category | flops | bytes accessed | tf_op | source)
XLA Modules:
  0.0 62.3 jit_solution(6918950986414773781)
XLA Ops:
  0.6 1.6 %copy-done = bf16[8,256,512]{2,1,0:T(8,128)(2,1)S(1)} copy-done((bf16[8,256,512]{2,1,0:T(8,128)(2,1)S(1)}, bf16[8,256,512]{2,1,0:T(8,128)(2,1)}, u32[]{:S(2)}) %copy-start) | copy-done | bytes 2097176
  2.2 1.6 %copy-done.1 = f32[256,2048]{1,0:T(8,128)S(1)} copy-done((f32[256,2048]{1,0:T(8,128)S(1)}, f32[256,2048]{1,0:T(8,128)}, u32[]{:S(2)}) %copy-start.1) | copy-done | bytes 2097176
  3.8 1.2 %copy-done.3 = bf16[8,256,256]{2,1,0:T(8,128)(2,1)S(1)} copy-done((bf16[8,256,256]{2,1,0:T(8,128)(2,1)S(1)}, bf16[8,256,256]{2,1,0:T(8,128)(2,1)}, u32[]{:S(2)}) %copy-start.3) | copy-done | bytes 1048600
  5.0 0.9 %copy-done.6 = bf16[256,256]{1,0:T(8,128)(2,1)S(1)} copy-done((bf16[256,256]{1,0:T(8,128)(2,1)S(1)}, bf16[256,256]{1,0:T(8,128)(2,1)}, u32[]{:S(2)}) %copy-start.6) | copy-done | bytes 131096
  6.6 4.8 %grams.1 = (f32[456,128]{1,0:T(8,128)S(1)}, f32[456,128]{1,0:T(8,128)S(1)}, f32[456,128]{1,0:T(8,128)S(1)}, f32[456,128]{1,0:T(8,128)S(1)}, f32[4,256,512]{2,1,0:T(8,128)S(1)}) custom-call(s32[1]{0:T(128)} %bitcast.me_ref, s32[1,64]{1,0:T(1,128)S(1)} %bitcast.6, bf16[8,256,512]{2,1,0:T(8,128)(2,1)S(1)} %copy-done, bf16[8,256,256]{2,1,0:T(8,128)(2,1)S(1)} %copy-done.3, ...), custom_call_target="tpu_custom_call" | custom-call | flops 1000 | bytes 1000 | tf_op jit(solution)/shard_map/grams/pallas_call | solution.py:295
  11.4 1.3 %copy-done.2 = f32[4,256,512]{2,1,0:T(8,128)} copy-done((f32[4,256,512]{2,1,0:T(8,128)}, f32[4,256,512]{2,1,0:T(8,128)S(1)}, u32[]{:S(2)}) %copy-start.2) | copy-done | bytes 2097176
  12.7 0.7 %copy-done.5 = f32[456,128]{1,0:T(8,128)} copy-done((f32[456,128]{1,0:T(8,128)}, f32[456,128]{1,0:T(8,128)S(1)}, u32[]{:S(2)}) %copy-start.5) | copy-done | bytes 233496
  13.4 0.7 %copy-done.9 = f32[456,128]{1,0:T(8,128)} copy-done((f32[456,128]{1,0:T(8,128)}, f32[456,128]{1,0:T(8,128)S(1)}, u32[]{:S(2)}) %copy-start.9) | copy-done | bytes 233496
  14.1 0.7 %copy-done.10 = f32[456,128]{1,0:T(8,128)} copy-done((f32[456,128]{1,0:T(8,128)}, f32[456,128]{1,0:T(8,128)S(1)}, u32[]{:S(2)}) %copy-start.10) | copy-done | bytes 233496
  14.8 4.3 %all-to-all-start = ((f32[4,256,512]{2,1,0:T(8,128)}), f32[4,256,512]{2,1,0:T(8,128)S(1)}, u32[]{:S(2)}, u32[]{:S(2)}) async-start(f32[4,256,512]{2,1,0:T(8,128)} %copy-done.2), calls=%async_computation | async-start | bytes 4194304 | tf_op jit(solution)/shard_map/all_to_all | solution.py:586
  19.1 2.4 %collective-permute-start = (f32[456,128]{1,0:T(8,128)}, f32[456,128]{1,0:T(8,128)S(1)}, u32[]{:S(2)}, u32[]{:S(2)}) collective-permute-start(f32[456,128]{1,0:T(8,128)} %copy-done.10), channel_id=1, source_target_pairs={{0,4},{4,0},{8,12},{12,8},{16,20},{20,16},{24,28},{28,24},{1,5},{5... | collective-permute-start | bytes 700424 | tf_op jit(solution)/shard_map/ppermute | solution.py:581
  21.5 1.6 %collective-permute-start.1 = (f32[456,128]{1,0:T(8,128)}, f32[456,128]{1,0:T(8,128)S(1)}, u32[]{:S(2)}, u32[]{:S(2)}) collective-permute-start(f32[456,128]{1,0:T(8,128)} %copy-done.9), channel_id=1, source_target_pairs={{0,8},{4,12},{8,0},{12,4},{16,24},{20,28},{24,16},{28,20},{1,9},{5... | collective-permute-start | bytes 700424 | tf_op jit(solution)/shard_map/ppermute | solution.py:581
  23.1 4.9 %collective-permute-done.refs_1_ = f32[456,128]{1,0:T(8,128)S(1)} collective-permute-done((f32[456,128]{1,0:T(8,128)}, f32[456,128]{1,0:T(8,128)S(1)}, u32[]{:S(2)}, u32[]{:S(2)}) %collective-permute-start) | collective-permute-done | bytes 233504 | tf_op jit(solution)/shard_map/ppermute | solution.py:581
  28.0 2.3 %collective-permute-done.1.refs_2_ = f32[456,128]{1,0:T(8,128)S(1)} collective-permute-done((f32[456,128]{1,0:T(8,128)}, f32[456,128]{1,0:T(8,128)S(1)}, u32[]{:S(2)}, u32[]{:S(2)}) %collective-permute-start.1) | collective-permute-done | bytes 233504 | tf_op jit(solution)/shard_map/ppermute | solution.py:581
  30.3 4.0 %collective-permute-done.2.refs_3_ = f32[456,128]{1,0:T(8,128)S(1)} collective-permute-done((f32[456,128]{1,0:T(8,128)S(1)}, f32[456,128]{1,0:T(8,128)S(1)}, u32[]{:S(2)}, u32[]{:S(2)}) %collective-permute-start.2) | collective-permute-done | bytes 233504 | tf_op jit(solution)/shard_map/ppermute | solution.py:581
  34.3 0.7 %copy-done.13 = f32[456,128]{1,0:T(8,128)} copy-done((f32[456,128]{1,0:T(8,128)}, f32[456,128]{1,0:T(8,128)S(1)}, u32[]{:S(2)}) %copy-start.13) | copy-done | bytes 233496
  35.0 2.0 %half_sums.1 = (f32[264,128]{1,0:T(8,128)}, f32[264,128]{1,0:T(8,128)}) custom-call(f32[456,128]{1,0:T(8,128)} %copy-done.5, f32[456,128]{1,0:T(8,128)} %copy-done.11, f32[456,128]{1,0:T(8,128)} %copy-done.12, f32[456,128]{1,0:T(8,128)} %copy-done.13), custom_call_target="tpu_custom_call" | custom-call | flops 1000 | bytes 1000 | tf_op jit(solution)/shard_map/half_sums/pallas_call | solution.py:590
  37.0 2.8 %collective-permute-start.3 = (f32[264,128]{1,0:T(8,128)}, f32[264,128]{1,0:T(8,128)S(1)}, u32[]{:S(2)}, u32[]{:S(2)}) collective-permute-start(f32[264,128]{1,0:T(8,128)} %get-tuple-element.16), channel_id=1, source_target_pairs={{0,16},{4,20},{8,24},{12,28},{16,0},{20,4},{24,8},{28,12},{1,17},{... | collective-permute-start | bytes 405512 | tf_op jit(solution)/shard_map/ppermute | solution.py:581
  39.7 6.4 %collective-permute-done.3.came = f32[264,128]{1,0:T(8,128)S(1)} collective-permute-done((f32[264,128]{1,0:T(8,128)}, f32[264,128]{1,0:T(8,128)S(1)}, u32[]{:S(2)}, u32[]{:S(2)}) %collective-permute-start.3) | collective-permute-done | bytes 135200 | tf_op jit(solution)/shard_map/ppermute | solution.py:581
  46.1 0.7 %copy-done.14 = f32[264,128]{1,0:T(8,128)} copy-done((f32[264,128]{1,0:T(8,128)}, f32[264,128]{1,0:T(8,128)S(1)}, u32[]{:S(2)}) %copy-start.14) | copy-done | bytes 135192
  46.8 1.6 %sums.1 = (f32[136,128]{1,0:T(8,128)}, f32[144,128]{1,0:T(8,128)}) custom-call(f32[264,128]{1,0:T(8,128)} %get-tuple-element.15.kept, f32[264,128]{1,0:T(8,128)} %copy-done.14), custom_call_target="tpu_custom_call" | custom-call | flops 1000 | bytes 1000 | tf_op jit(solution)/shard_map/sums/pallas_call | solution.py:599
  48.4 6.1 %all-gather = f32[576,128]{1,0:T(8,128)S(1)} all-gather(f32[144,128]{1,0:T(8,128)} %get-tuple-element.18), channel_id=2, replica_groups=mesh['dp'=8,'tensor'=4] {'tensor'}, dimensions={0}, use_global_device_ids=true | all-gather | bytes 368640 | tf_op jit(solution)/shard_map/all_gather | solution.py:608
  54.5 0.9 %copy-done.7 = f32[136,128]{1,0:T(8,128)S(1)} copy-done((f32[136,128]{1,0:T(8,128)S(1)}, f32[136,128]{1,0:T(8,128)}, u32[]{:S(2)}) %copy-start.7) | copy-done | bytes 69656
  55.4 7.0 %invert_apply.1 = (f32[1024,512]{1,0:T(8,128)}, f32[256,1024]{1,0:T(8,128)}) custom-call(f32[136,128]{1,0:T(8,128)S(1)} %copy-done.7, f32[4,144,128]{2,1,0:T(8,128)S(1)} %bitcast.5, f32[1024,512]{1,0:T(8,128)S(1)} %bitcast.4, f32[256,1024]{1,0:T(8,128)S(1)} %copy-done.4), custom_call_target="tpu_custom_call" | custom-call | flops 1000 | bytes 1000 | tf_op jit(solution)/shard_map/invert_apply/pallas_call | solution.py:529
  (21 shorter events, 0.7 us)
Async XLA Ops:
  0.6 1.6 %copy-start = (bf16[8,256,512]{2,1,0:T(8,128)(2,1)S(1)}, bf16[8,256,512]{2,1,0:T(8,128)(2,1)}, u32[]{:S(2)}) copy-start(bf16[8,256,512]{2,1,0:T(8,128)(2,1)} %acts_hbm.1) | copy-start | bytes 6291460
  2.2 1.6 %copy-start.1 = (f32[256,2048]{1,0:T(8,128)S(1)}, f32[256,2048]{1,0:T(8,128)}, u32[]{:S(2)}) copy-start(f32[256,2048]{1,0:T(8,128)} %w_hbm.1) | copy-start | bytes 6291460
  3.8 1.2 %copy-start.3 = (bf16[8,256,256]{2,1,0:T(8,128)(2,1)S(1)}, bf16[8,256,256]{2,1,0:T(8,128)(2,1)}, u32[]{:S(2)}) copy-start(bf16[8,256,256]{2,1,0:T(8,128)(2,1)} %cot_hbm.1) | copy-start | bytes 3145732
  5.0 0.9 %copy-start.6 = (bf16[256,256]{1,0:T(8,128)(2,1)S(1)}, bf16[256,256]{1,0:T(8,128)(2,1)}, u32[]{:S(2)}) copy-start(bf16[256,256]{1,0:T(8,128)(2,1)} %emb_hbm.1) | copy-start | bytes 393220
  5.9 0.7 %copy-start.8 = (s32[64]{0:T(128)S(1)}, s32[64]{0:T(128)}, u32[]{:S(2)}) copy-start(s32[64]{0:T(128)} %param.8) | copy-start | bytes 772
  11.4 1.3 %copy-start.2 = (f32[4,256,512]{2,1,0:T(8,128)}, f32[4,256,512]{2,1,0:T(8,128)S(1)}, u32[]{:S(2)}) copy-start(f32[4,256,512]{2,1,0:T(8,128)S(1)} %get-tuple-element.19) | copy-start | bytes 6291460
  12.7 0.7 %copy-start.5 = (f32[456,128]{1,0:T(8,128)}, f32[456,128]{1,0:T(8,128)S(1)}, u32[]{:S(2)}) copy-start(f32[456,128]{1,0:T(8,128)S(1)} %get-tuple-element.11.refs_0_) | copy-start | bytes 700420
  13.4 0.7 %copy-start.9 = (f32[456,128]{1,0:T(8,128)}, f32[456,128]{1,0:T(8,128)S(1)}, u32[]{:S(2)}) copy-start(f32[456,128]{1,0:T(8,128)S(1)} %get-tuple-element.13) | copy-start | bytes 700420
  14.1 0.7 %copy-start.10 = (f32[456,128]{1,0:T(8,128)}, f32[456,128]{1,0:T(8,128)S(1)}, u32[]{:S(2)}) copy-start(f32[456,128]{1,0:T(8,128)S(1)} %get-tuple-element.12) | copy-start | bytes 700420
  14.8 39.7 %copy-start.4 = (f32[256,1024]{1,0:T(8,128)S(1)}, f32[256,1024]{1,0:T(8,128)}, u32[]{:S(2)}) copy-start(f32[256,1024]{1,0:T(8,128)} %e_hbm.1) | copy-start | bytes 3145732
  14.8 39.7 %all-to-all-start = ((f32[4,256,512]{2,1,0:T(8,128)}), f32[4,256,512]{2,1,0:T(8,128)S(1)}, u32[]{:S(2)}, u32[]{:S(2)}) async-start(f32[4,256,512]{2,1,0:T(8,128)} %copy-done.2), calls=%async_computation | async-start | bytes 4194304 | tf_op jit(solution)/shard_map/all_to_all | solution.py:586
  19.1 8.9 %collective-permute-start = (f32[456,128]{1,0:T(8,128)}, f32[456,128]{1,0:T(8,128)S(1)}, u32[]{:S(2)}, u32[]{:S(2)}) collective-permute-start(f32[456,128]{1,0:T(8,128)} %copy-done.10), channel_id=1, source_target_pairs={{0,4},{4,0},{8,12},{12,8},{16,20},{20,16},{24,28},{28,24},{1,5},{5... | collective-permute-start | bytes 700424 | tf_op jit(solution)/shard_map/ppermute | solution.py:581
  21.5 8.7 %collective-permute-start.1 = (f32[456,128]{1,0:T(8,128)}, f32[456,128]{1,0:T(8,128)S(1)}, u32[]{:S(2)}, u32[]{:S(2)}) collective-permute-start(f32[456,128]{1,0:T(8,128)} %copy-done.9), channel_id=1, source_target_pairs={{0,8},{4,12},{8,0},{12,4},{16,24},{20,28},{24,16},{28,20},{1,9},{5... | collective-permute-start | bytes 700424 | tf_op jit(solution)/shard_map/ppermute | solution.py:581
  23.1 11.2 %collective-permute-start.2 = (f32[456,128]{1,0:T(8,128)S(1)}, f32[456,128]{1,0:T(8,128)S(1)}, u32[]{:S(2)}, u32[]{:S(2)}) collective-permute-start(f32[456,128]{1,0:T(8,128)S(1)} %get-tuple-element.14), channel_id=1, source_target_pairs={{0,12},{4,8},{8,4},{12,0},{16,28},{20,24},{24,20},{28,16},{1,13},{... | collective-permute-start | bytes 700424 | tf_op jit(solution)/shard_map/ppermute | solution.py:581
  28.0 6.3 %copy-start.11 = (f32[456,128]{1,0:T(8,128)}, f32[456,128]{1,0:T(8,128)S(1)}, u32[]{:S(2)}) copy-start(f32[456,128]{1,0:T(8,128)S(1)} %collective-permute-done.refs_1_) | copy-start | bytes 700420
  30.3 4.0 %copy-start.12 = (f32[456,128]{1,0:T(8,128)}, f32[456,128]{1,0:T(8,128)S(1)}, u32[]{:S(2)}) copy-start(f32[456,128]{1,0:T(8,128)S(1)} %collective-permute-done.1.refs_2_) | copy-start | bytes 700420
  34.3 0.7 %copy-start.13 = (f32[456,128]{1,0:T(8,128)}, f32[456,128]{1,0:T(8,128)S(1)}, u32[]{:S(2)}) copy-start(f32[456,128]{1,0:T(8,128)S(1)} %collective-permute-done.2.refs_3_) | copy-start | bytes 700420
  37.0 9.1 %collective-permute-start.3 = (f32[264,128]{1,0:T(8,128)}, f32[264,128]{1,0:T(8,128)S(1)}, u32[]{:S(2)}, u32[]{:S(2)}) collective-permute-start(f32[264,128]{1,0:T(8,128)} %get-tuple-element.16), channel_id=1, source_target_pairs={{0,16},{4,20},{8,24},{12,28},{16,0},{20,4},{24,8},{28,12},{1,17},{... | collective-permute-start | bytes 405512 | tf_op jit(solution)/shard_map/ppermute | solution.py:581
  46.1 0.7 %copy-start.14 = (f32[264,128]{1,0:T(8,128)}, f32[264,128]{1,0:T(8,128)S(1)}, u32[]{:S(2)}) copy-start(f32[264,128]{1,0:T(8,128)S(1)} %collective-permute-done.3.came) | copy-start | bytes 405508
  54.5 0.9 %copy-start.7 = (f32[136,128]{1,0:T(8,128)S(1)}, f32[136,128]{1,0:T(8,128)}, u32[]{:S(2)}) copy-start(f32[136,128]{1,0:T(8,128)} %get-tuple-element.17.own_ref) | copy-start | bytes 208900

commit v3 on v2

--- a/solution.py
+++ b/solution.py
@@ -217,8 +217,8 @@
 def gram_kernel(counts, me_ref, ids_ref, acts_hbm, cot_hbm, emb_hbm, w_hbm, *refs):
     quads_a, quads_g, n_dp, n_tp = counts
     half = n_dp // 2
-    outs, w_out = refs[:half], refs[half]
-    acts, cot, emb, acts_sem, cot_sem, emb_sem, w_sem = refs[half + 1 :]
+    outs_hbm, w_out = refs[:half], refs[half]
+    acts, cot, emb, w, outs, acts_sem, cot_sem, emb_sem, w_sem, move_sem, out_sem = refs[half + 1 :]
     me = me_ref[0]
     order = [k for j in list(range(1, half)) + [0] for k in (j, j + half)]
 
@@ -231,16 +231,24 @@
 
     emb_copy = pltpu.make_async_copy(emb_hbm, emb, emb_sem)
     emb_copy.start()
-    for k in order:
+    for k in order[:2]:
         for copy in fetch(k):
             copy.start()
     part = w_hbm.shape[1] // n_tp
-    moves = [
-        pltpu.make_async_copy(w_hbm.at[:, pl.ds(t * part, part)], w_out.at[t], w_sem.at[t])
+    loads = [
+        pltpu.make_async_copy(
+            w_hbm.at[:, pl.ds(t * part, part)], w.at[t], w_sem.at[t]
+        )
         for t in range(n_tp)
     ]
-    for move in moves:
-        move.start()
+    for load in loads:
+        load.start()
+    for k in order[2:]:
+        for copy in fetch(k):
+            copy.start()
+    moves = [
+        pltpu.make_async_copy(w.at[t], w_out.at[t], move_sem.at[t]) for t in range(n_tp)
+    ]
 
     def pack(source, at):
         first = gram_pair(source[:, at * 2 * LANES : (at * 2 + 1) * LANES])
@@ -257,6 +265,7 @@
         ],
         axis=1,
     )
+    stores = []
     for j in list(range(1, half)) + [0]:
         packed = []
         for k in (j, j + half):
@@ -267,13 +276,19 @@
             packed += [pack(rows_g, q) for q in range(quads_g)]
         packed += packed_e
         for q, (quad, diagonal) in enumerate(packed):
-            outs[j][q * HEAD : (q + 1) * HEAD, :] = quad
+            outs[j, q * HEAD : (q + 1) * HEAD, :] = quad
             at = len(packed) * HEAD + q
-            outs[j][at : at + 1, :] = diagonal
+            outs[j, at : at + 1, :] = diagonal
         at = len(packed) * (HEAD + 1)
-        outs[j][at : at + 1, :] = ids
-    for move in moves:
-        move.wait()
+        outs[j, at : at + 1, :] = ids
+        stores.append(pltpu.make_async_copy(outs.at[j], outs_hbm[j], out_sem.at[j]))
+        stores[-1].start()
+        if j == 1 % half:
+            for load, move in zip(loads, moves):
+                load.wait()
+                move.start()
+    for copy in moves + stores:
+        copy.wait()
 
 
 def small_cost():
@@ -295,19 +310,23 @@
     return pl.pallas_call(
         functools.partial(gram_kernel, (quads_a, quads_g, n_dp, n_tp)),
         in_specs=[pl.BlockSpec(memory_space=pltpu.SMEM), vmem, hbm, hbm, hbm, hbm],
-        out_specs=[vmem] * half + [hbm],
+        out_specs=[hbm] * (half + 1),
         out_shape=[jax.ShapeDtypeStruct((payload_rows, LANES), jnp.float32)] * half
         + [jax.ShapeDtypeStruct((n_tp, grad_w.shape[0], part), jnp.float32)],
         scratch_shapes=[
             pltpu.VMEM((layers, rows, width_a), jnp.bfloat16),
             pltpu.VMEM((layers, rows, width_g), jnp.bfloat16),
             pltpu.VMEM((rows, width_g), jnp.bfloat16),
+            pltpu.VMEM((n_tp, grad_w.shape[0], part), jnp.float32),
+            pltpu.VMEM((half, payload_rows, LANES), jnp.float32),
             pltpu.SemaphoreType.DMA((layers,)),
             pltpu.SemaphoreType.DMA((layers,)),
             pltpu.SemaphoreType.DMA,
             pltpu.SemaphoreType.DMA((n_tp,)),
+            pltpu.SemaphoreType.DMA((n_tp,)),
+            pltpu.SemaphoreType.DMA((half,)),
         ],
-        compiler_params=pltpu.CompilerParams(vmem_limit_bytes=32 * 1024 * 1024),
+        compiler_params=pltpu.CompilerParams(vmem_limit_bytes=62 * 1024 * 1024),
         cost_estimate=small_cost(),
         name="grams",
     )(dp_index.reshape(1), emb_ids.reshape(1, -1), acts, out_cot, emb_cot, grad_w)
@@ -576,6 +595,7 @@
     quads_a = inner_part // (2 * LANES)
     quads_g = width_part // (2 * LANES)
     half = n_dp // 2
+    vmem = pl.BlockSpec(memory_space=pltpu.VMEM)
 
     def trade(value, k):
         return lax.ppermute(value, "dp", [(i, i ^ k) for i in range(n_dp)])
@@ -589,7 +609,10 @@
     kept_rows = round_up((quads_a + 2 * quads_g) * (HEAD + 1) + half, ROWS)
     kept, mirror = pl.pallas_call(
         functools.partial(half_sum_kernel, quads_a + quads_g, quads_g),
+        in_specs=[vmem] * half,
+        out_specs=[vmem] * 2,
         out_shape=[jax.ShapeDtypeStruct((kept_rows, LANES), jnp.float32)] * 2,
+        compiler_params=pltpu.CompilerParams(vmem_limit_bytes=8 * 1024 * 1024),
         cost_estimate=small_cost(),
         name="half_sums",
     )(*arrived)
@@ -598,10 +621,13 @@
     share_rows = round_up(2 * quads_g * (HEAD + 1) + 3 + n_dp, ROWS)
     own, share = pl.pallas_call(
         functools.partial(sum_kernel, quads_a, quads_g, half),
+        in_specs=[vmem] * 2,
+        out_specs=[vmem] * 2,
         out_shape=[
             jax.ShapeDtypeStruct((own_rows, LANES), jnp.float32),
             jax.ShapeDtypeStruct((share_rows, LANES), jnp.float32),
         ],
+        compiler_params=pltpu.CompilerParams(vmem_limit_bytes=8 * 1024 * 1024),
         cost_estimate=small_cost(),
         name="sums",
     )(kept, came)

time: 62.8 us -> 49 us (0.78)
  local copies, waits for them, and re-layouts: 11.6 us -> 0.01 us
  Pallas kernels: 15.4 us -> 13.7 us
    unnamed x30 -> x4, local copies, waits for them, and re-layouts: 11.6 us -> 0.01 us
    pallas_call x1, Pallas kernels: 2.03 us -> 0.08 us  [local(): pl.pallas_call(functools.partial(half_sum_kernel, quads_a + quads_g, quad...]
    pallas_call x1, Pallas kernels: 4.76 us -> 6.56 us  [grams(): pl.pallas_call(functools.partial(gram_kernel, (quads_a, quads_g, n_dp, n_...]
    pallas_call x1, Pallas kernels: 1.63 us -> 0.04 us  [local(): pl.pallas_call(functools.partial(sum_kernel, quads_a, quads_g, half), in_...]
  transfers between devices with their start and end apart: 5 -> 5, of which waited for: 4 -> 4; matrix products, arithmetic and copies ran while one was open for 0% -> 0% of each run, Pallas kernels for 6% -> 0%
where the time goes in v3:
time: 49 us; the launch traced here: 48.7 us
  waiting for transfers between devices  17.3 us (35%)
  Pallas kernels  13.7 us (28%)
  starting transfers between devices  11.2 us (23%)
  blocking collectives  5.88 us (12%)
  between operations  0.67 us (1%)
    ppermute x4, waiting for transfers between devices, trade(): return lax.ppermute(value, 'dp', [(i, i ^ k) for i in range(n_dp)])  17.3 us
    pallas_call x1, Pallas kernels, invert_apply(): pl.pallas_call(functools.partial(invert_apply_kernel, sizes), in_specs=[v...  6.99 us
    ppermute x4, starting transfers between devices, trade(): return lax.ppermute(value, 'dp', [(i, i ^ k) for i in range(n_dp)])  6.84 us
    pallas_call x1, Pallas kernels, grams(): pl.pallas_call(functools.partial(gram_kernel, (quads_a, quads_g, n_dp, n_...  6.56 us
    all_gather x1, blocking collectives, local(): shared = lax.all_gather(share[None], 'tensor', axis=0, tiled=True)  5.88 us
    all_to_all x1, starting transfers between devices, local(): lax.all_to_all(sending, 'tensor', split_axis=0, concat_axis=0, tiled=True)  4.35 us
  transfers between devices with their start and end apart: 5, of which 4 were waited for; matrix products, arithmetic and copies ran while one was open for 0% of the time, Pallas kernels for 0%

profile of v3, /device:TPU:0, one launch (start us, length us, event | category | flops | bytes accessed | tf_op | source)
XLA Modules:
  0.0 48.7 jit_solution(4975221048021242648)
XLA Ops:
  0.6 6.6 %grams.1 = (f32[456,128]{1,0:T(8,128)}, f32[456,128]{1,0:T(8,128)}, f32[456,128]{1,0:T(8,128)}, f32[456,128]{1,0:T(8,128)}, f32[4,256,512]{2,1,0:T(8,128)}) custom-call(s32[1]{0:T(128)} %bitcast.me_ref, s32[1,64]{1,0:T(1,128)} %bitcast.6, bf16[8,256,512]{2,1,0:T(8,128)(2,1)} %acts_hbm.1, bf16[8,256,256]{2,1,0:T(8,128)(2,1)} %cot_hbm.1, ...), custom_call_target="tpu_custom_call" | custom-call | flops 1000 | bytes 1000 | tf_op jit(solution)/shard_map/grams/pallas_call | solution.py:310
  7.2 0.0 copy-start.1
  7.2 0.0 copy-start
  7.2 4.3 %all-to-all-start = ((f32[4,256,512]{2,1,0:T(8,128)}), f32[4,256,512]{2,1,0:T(8,128)S(1)}, u32[]{:S(2)}, u32[]{:S(2)}) async-start(f32[4,256,512]{2,1,0:T(8,128)} %get-tuple-element.19), calls=%async_computation | async-start | bytes 4194304 | tf_op jit(solution)/shard_map/all_to_all | solution.py:606
  11.6 2.4 %collective-permute-start = (f32[456,128]{1,0:T(8,128)}, f32[456,128]{1,0:T(8,128)S(1)}, u32[]{:S(2)}, u32[]{:S(2)}) collective-permute-start(f32[456,128]{1,0:T(8,128)} %get-tuple-element.12), channel_id=1, source_target_pairs={{0,4},{4,0},{8,12},{12,8},{16,20},{20,16},{24,28},{28,24},{1,5},{5... | collective-permute-start | bytes 700424 | tf_op jit(solution)/shard_map/ppermute | solution.py:601
  14.0 1.6 %collective-permute-start.1 = (f32[456,128]{1,0:T(8,128)}, f32[456,128]{1,0:T(8,128)S(1)}, u32[]{:S(2)}, u32[]{:S(2)}) collective-permute-start(f32[456,128]{1,0:T(8,128)} %get-tuple-element.13), channel_id=1, source_target_pairs={{0,8},{4,12},{8,0},{12,4},{16,24},{20,28},{24,16},{28,20},{1,9},{5... | collective-permute-start | bytes 700424 | tf_op jit(solution)/shard_map/ppermute | solution.py:601
  15.6 0.0 collective-permute-start.2
  15.6 4.9 %collective-permute-done.refs_1_ = f32[456,128]{1,0:T(8,128)S(1)} collective-permute-done((f32[456,128]{1,0:T(8,128)}, f32[456,128]{1,0:T(8,128)S(1)}, u32[]{:S(2)}, u32[]{:S(2)}) %collective-permute-start) | collective-permute-done | bytes 233504 | tf_op jit(solution)/shard_map/ppermute | solution.py:601
  20.5 2.3 %collective-permute-done.1.refs_2_ = f32[456,128]{1,0:T(8,128)S(1)} collective-permute-done((f32[456,128]{1,0:T(8,128)}, f32[456,128]{1,0:T(8,128)S(1)}, u32[]{:S(2)}, u32[]{:S(2)}) %collective-permute-start.1) | collective-permute-done | bytes 233504 | tf_op jit(solution)/shard_map/ppermute | solution.py:601
  22.8 4.0 %collective-permute-done.2.refs_3_ = f32[456,128]{1,0:T(8,128)S(1)} collective-permute-done((f32[456,128]{1,0:T(8,128)}, f32[456,128]{1,0:T(8,128)S(1)}, u32[]{:S(2)}, u32[]{:S(2)}) %collective-permute-start.2) | collective-permute-done | bytes 233504 | tf_op jit(solution)/shard_map/ppermute | solution.py:601
  26.8 0.0 copy-done.1
  26.8 0.1 half_sums.1
  26.8 2.8 %collective-permute-start.3 = (f32[264,128]{1,0:T(8,128)S(1)}, f32[264,128]{1,0:T(8,128)S(1)}, u32[]{:S(2)}, u32[]{:S(2)}) collective-permute-start(f32[264,128]{1,0:T(8,128)S(1)} %get-tuple-element.16), channel_id=1, source_target_pairs={{0,16},{4,20},{8,24},{12,28},{16,0},{20,4},{24,8},{28,12},{1,17},{... | collective-permute-start | bytes 405512 | tf_op jit(solution)/shard_map/ppermute | solution.py:601
  29.7 6.2 %collective-permute-done.3.came = f32[264,128]{1,0:T(8,128)S(1)} collective-permute-done((f32[264,128]{1,0:T(8,128)S(1)}, f32[264,128]{1,0:T(8,128)S(1)}, u32[]{:S(2)}, u32[]{:S(2)}) %collective-permute-start.3) | collective-permute-done | bytes 135200 | tf_op jit(solution)/shard_map/ppermute | solution.py:601
  35.9 5.9 %all-gather = f32[576,128]{1,0:T(8,128)S(1)} all-gather(f32[144,128]{1,0:T(8,128)S(1)} %get-tuple-element.18), channel_id=2, replica_groups=mesh['dp'=8,'tensor'=4] {'tensor'}, dimensions={0}, use_global_device_ids=true | all-gather | bytes 368640 | tf_op jit(solution)/shard_map/all_gather | solution.py:634
  41.7 0.0 all-to-all-done
  41.7 0.0 copy-done
  41.7 7.0 %invert_apply.1 = (f32[1024,512]{1,0:T(8,128)}, f32[256,1024]{1,0:T(8,128)}) custom-call(f32[136,128]{1,0:T(8,128)S(1)} %get-tuple-element.17.own_ref, f32[4,144,128]{2,1,0:T(8,128)S(1)} %bitcast.5, f32[1024,512]{1,0:T(8,128)S(1)} %bitcast.4, f32[256,1024]{1,0:T(8,128)S(1)} %copy-done), custom_call_target="tpu_custom_call" | custom-call | flops 1000 | bytes 1000 | tf_op jit(solution)/shard_map/invert_apply/pallas_call | solution.py:548
  (1 shorter events, 0.0 us)
Async XLA Ops:
  7.2 19.6 %copy-start.1 = (f32[456,128]{1,0:T(8,128)S(1)}, f32[456,128]{1,0:T(8,128)}, u32[]{:S(2)}) copy-start(f32[456,128]{1,0:T(8,128)} %get-tuple-element.11.refs_0_) | copy-start | bytes 700420
  7.2 34.5 %copy-start = (f32[256,1024]{1,0:T(8,128)S(1)}, f32[256,1024]{1,0:T(8,128)}, u32[]{:S(2)}) copy-start(f32[256,1024]{1,0:T(8,128)} %e_hbm.1) | copy-start | bytes 3145732
  7.2 34.5 %all-to-all-start = ((f32[4,256,512]{2,1,0:T(8,128)}), f32[4,256,512]{2,1,0:T(8,128)S(1)}, u32[]{:S(2)}, u32[]{:S(2)}) async-start(f32[4,256,512]{2,1,0:T(8,128)} %get-tuple-element.19), calls=%async_computation | async-start | bytes 4194304 | tf_op jit(solution)/shard_map/all_to_all | solution.py:606
  11.6 8.9 %collective-permute-start = (f32[456,128]{1,0:T(8,128)}, f32[456,128]{1,0:T(8,128)S(1)}, u32[]{:S(2)}, u32[]{:S(2)}) collective-permute-start(f32[456,128]{1,0:T(8,128)} %get-tuple-element.12), channel_id=1, source_target_pairs={{0,4},{4,0},{8,12},{12,8},{16,20},{20,16},{24,28},{28,24},{1,5},{5... | collective-permute-start | bytes 700424 | tf_op jit(solution)/shard_map/ppermute | solution.py:601
  14.0 8.7 %collective-permute-start.1 = (f32[456,128]{1,0:T(8,128)}, f32[456,128]{1,0:T(8,128)S(1)}, u32[]{:S(2)}, u32[]{:S(2)}) collective-permute-start(f32[456,128]{1,0:T(8,128)} %get-tuple-element.13), channel_id=1, source_target_pairs={{0,8},{4,12},{8,0},{12,4},{16,24},{20,28},{24,16},{28,20},{1,9},{5... | collective-permute-start | bytes 700424 | tf_op jit(solution)/shard_map/ppermute | solution.py:601
  15.6 11.2 %collective-permute-start.2 = (f32[456,128]{1,0:T(8,128)}, f32[456,128]{1,0:T(8,128)S(1)}, u32[]{:S(2)}, u32[]{:S(2)}) collective-permute-start(f32[456,128]{1,0:T(8,128)} %get-tuple-element.14), channel_id=1, source_target_pairs={{0,12},{4,8},{8,4},{12,0},{16,28},{20,24},{24,20},{28,16},{1,13},{... | collective-permute-start | bytes 700424 | tf_op jit(solution)/shard_map/ppermute | solution.py:601
  26.8 9.0 %collective-permute-start.3 = (f32[264,128]{1,0:T(8,128)S(1)}, f32[264,128]{1,0:T(8,128)S(1)}, u32[]{:S(2)}, u32[]{:S(2)}) collective-permute-start(f32[264,128]{1,0:T(8,128)S(1)} %get-tuple-element.16), channel_id=1, source_target_pairs={{0,16},{4,20},{8,24},{12,28},{16,0},{20,4},{24,8},{28,12},{1,17},{... | collective-permute-start | bytes 405512 | tf_op jit(solution)/shard_map/ppermute | solution.py:601

commit v4 on v2

--- a/solution.py
+++ b/solution.py
@@ -214,66 +214,52 @@
     )
 
 
-def gram_kernel(counts, me_ref, ids_ref, acts_hbm, cot_hbm, emb_hbm, w_hbm, *refs):
-    quads_a, quads_g, n_dp, n_tp = counts
+def pack_all(source, quads):
+    row, _, col = pair_masks()
+    packed, trace = [], jnp.zeros((1, LANES), jnp.float32)
+    for q in range(quads):
+        first = gram_pair(source[:, q * 2 * LANES : (q * 2 + 1) * LANES])
+        second = gram_pair(source[:, (q * 2 + 1) * LANES : (q * 2 + 2) * LANES])
+        quad, diagonal = pack_quad(first, second)
+        packed.append((quad, diagonal))
+        trace = trace + diagonal
+        trace = trace + jnp.sum(jnp.where(col == row, first, 0.0), axis=0, keepdims=True)
+    return packed, trace
+
+
+def put_packed(out, packed, more=()):
+    for q, (quad, diagonal) in enumerate(packed):
+        out[q * HEAD : (q + 1) * HEAD, :] = quad
+        at = len(packed) * HEAD + q
+        out[at : at + 1, :] = diagonal
+    for i, line in enumerate(more):
+        at = len(packed) * (HEAD + 1) + i
+        out[at : at + 1, :] = line
+
+
+def gram_kernel(counts, ids, acts, cot, emb, after, *outs):
+    quads_a, quads_g, n_dp = counts
     half = n_dp // 2
-    outs, w_out = refs[:half], refs[half]
-    acts, cot, emb, acts_sem, cot_sem, emb_sem, w_sem = refs[half + 1 :]
-    me = me_ref[0]
-    order = [k for j in list(range(1, half)) + [0] for k in (j, j + half)]
-
-    def fetch(k):
-        layer = lax.bitwise_xor(me, k)
-        return (
-            pltpu.make_async_copy(acts_hbm.at[layer], acts.at[k], acts_sem.at[k]),
-            pltpu.make_async_copy(cot_hbm.at[layer], cot.at[k], cot_sem.at[k]),
-        )
-
-    emb_copy = pltpu.make_async_copy(emb_hbm, emb, emb_sem)
-    emb_copy.start()
-    for k in order:
-        for copy in fetch(k):
-            copy.start()
-    part = w_hbm.shape[1] // n_tp
-    moves = [
-        pltpu.make_async_copy(w_hbm.at[:, pl.ds(t * part, part)], w_out.at[t], w_sem.at[t])
-        for t in range(n_tp)
-    ]
-    for move in moves:
-        move.start()
-
-    def pack(source, at):
-        first = gram_pair(source[:, at * 2 * LANES : (at * 2 + 1) * LANES])
-        second = gram_pair(source[:, (at * 2 + 1) * LANES : (at * 2 + 2) * LANES])
-        return pack_quad(first, second)
-
-    emb_copy.wait()
-    emb_rows = emb[...]
-    packed_e = [pack(emb_rows, q) for q in range(quads_g)]
-    ids = jnp.concatenate(
+    outs_g, outs_a = outs[:half], outs[half:]
+    me = lax.axis_index("dp")
+    packed_e, _ = pack_all(emb[...], quads_g)
+    ids_row = jnp.concatenate(
         [
-            ids_ref[...].astype(jnp.float32),
-            jnp.full((1, LANES - ids_ref.shape[1]), -1.0, jnp.float32),
+            ids[...].astype(jnp.float32),
+            jnp.full((1, LANES - ids.shape[1]), -1.0, jnp.float32),
         ],
         axis=1,
     )
-    for j in list(range(1, half)) + [0]:
-        packed = []
+    for j in range(half):
+        packed_g, packed_a, traces = [], [], []
         for k in (j, j + half):
-            for copy in fetch(k):
-                copy.wait()
-            rows_a, rows_g = acts[k], cot[k]
-            packed += [pack(rows_a, q) for q in range(quads_a)]
-            packed += [pack(rows_g, q) for q in range(quads_g)]
-        packed += packed_e
-        for q, (quad, diagonal) in enumerate(packed):
-            outs[j][q * HEAD : (q + 1) * HEAD, :] = quad
-            at = len(packed) * HEAD + q
-            outs[j][at : at + 1, :] = diagonal
-        at = len(packed) * (HEAD + 1)
-        outs[j][at : at + 1, :] = ids
-    for move in moves:
-        move.wait()
+            layer = lax.bitwise_xor(me, k)
+            packed_g += pack_all(cot[layer], quads_g)[0]
+            packed, trace = pack_all(acts[layer], quads_a)
+            packed_a += packed
+            traces.append(trace)
+        put_packed(outs_g[j], packed_g + packed_e, traces + [ids_row])
+        put_packed(outs_a[j], packed_a)
 
 
 def small_cost():
@@ -284,121 +270,130 @@
     return -(-value // unit) * unit
 
 
-def grams(acts, out_cot, emb_cot, emb_ids, grad_w, dp_index, n_dp, n_tp, quads_a, quads_g):
+def grams(acts, out_cot, emb_cot, emb_ids, after, n_dp, quads_a, quads_g):
     layers, rows, width_a = acts.shape
     width_g = out_cot.shape[2]
     half = n_dp // 2
-    payload_rows = round_up((2 * (quads_a + quads_g) + quads_g) * (HEAD + 1) + 1, ROWS)
-    part = grad_w.shape[1] // n_tp
+    rows_g = round_up(3 * quads_g * (HEAD + 1) + 3, ROWS)
+    rows_a = round_up(2 * quads_a * (HEAD + 1), ROWS)
     vmem = pl.BlockSpec(memory_space=pltpu.VMEM)
     hbm = pl.BlockSpec(memory_space=pltpu.HBM)
-    return pl.pallas_call(
-        functools.partial(gram_kernel, (quads_a, quads_g, n_dp, n_tp)),
-        in_specs=[pl.BlockSpec(memory_space=pltpu.SMEM), vmem, hbm, hbm, hbm, hbm],
-        out_specs=[vmem] * half + [hbm],
-        out_shape=[jax.ShapeDtypeStruct((payload_rows, LANES), jnp.float32)] * half
-        + [jax.ShapeDtypeStruct((n_tp, grad_w.shape[0], part), jnp.float32)],
-        scratch_shapes=[
-            pltpu.VMEM((layers, rows, width_a), jnp.bfloat16),
-            pltpu.VMEM((layers, rows, width_g), jnp.bfloat16),
-            pltpu.VMEM((rows, width_g), jnp.bfloat16),
-            pltpu.SemaphoreType.DMA((layers,)),
-            pltpu.SemaphoreType.DMA((layers,)),
-            pltpu.SemaphoreType.DMA,
-            pltpu.SemaphoreType.DMA((n_tp,)),
-        ],
-        compiler_params=pltpu.CompilerParams(vmem_limit_bytes=32 * 1024 * 1024),
+    outs = pl.pallas_call(
+        functools.partial(gram_kernel, (quads_a, quads_g, n_dp)),
+        in_specs=[vmem] * 4 + [hbm],
+        out_specs=[vmem] * (2 * half),
+        out_shape=[jax.ShapeDtypeStruct((rows_g, LANES), jnp.float32)] * half
+        + [jax.ShapeDtypeStruct((rows_a, LANES), jnp.float32)] * half,
+        compiler_params=pltpu.CompilerParams(vmem_limit_bytes=24 * 1024 * 1024),
         cost_estimate=small_cost(),
         name="grams",
-    )(dp_index.reshape(1), emb_ids.reshape(1, -1), acts, out_cot, emb_cot, grad_w)
-
-
-def half_sum_kernel(quads_layer, quads_g, *refs):
+    )(emb_ids.reshape(1, -1), acts, out_cot, emb_cot, after)
+    return outs[:half], outs[half:]
+
+
+def column_parts_kernel(n_tp, w_hbm, *refs):
+    outs = refs[: n_tp - 1]
+    w, load_sem, move_sem = refs[n_tp - 1 :]
+    me = lax.axis_index("tensor")
+    part = w.shape[2]
+    loads, moves = [], []
+    for k in range(n_tp - 1, 0, -1):
+        at = pl.multiple_of(lax.bitwise_xor(me, k) * part, part)
+        loads.append(
+            pltpu.make_async_copy(
+                w_hbm.at[:, pl.ds(at, part)], w.at[k - 1], load_sem.at[k - 1]
+            )
+        )
+        moves.append(pltpu.make_async_copy(w.at[k - 1], outs[k - 1], move_sem.at[k - 1]))
+        loads[-1].start()
+    for load, move in zip(loads, moves):
+        load.wait()
+        move.start()
+    for move in moves:
+        move.wait()
+
+
+def column_parts(grad_w, n_tp):
+    rows, width = grad_w.shape
+    part = (rows, width // n_tp)
+    hbm = pl.BlockSpec(memory_space=pltpu.HBM)
+    return pl.pallas_call(
+        functools.partial(column_parts_kernel, n_tp),
+        in_specs=[hbm],
+        out_specs=[hbm] * (n_tp - 1),
+        out_shape=[jax.ShapeDtypeStruct(part, jnp.float32)] * (n_tp - 1),
+        scratch_shapes=[
+            pltpu.VMEM((n_tp - 1, *part), jnp.float32),
+            pltpu.SemaphoreType.DMA((n_tp - 1,)),
+            pltpu.SemaphoreType.DMA((n_tp - 1,)),
+        ],
+        compiler_params=pltpu.CompilerParams(vmem_limit_bytes=40 * 1024 * 1024),
+        cost_estimate=small_cost(),
+        name="column_parts",
+    )(grad_w)
+
+
+def total_of(parts, at, size):
+    value = parts[0][at : at + size, :]
+    for part in parts[1:]:
+        value = value + part[at : at + size, :]
+    return value
+
+
+def take_packed(parts, first, count, quads):
+    return [
+        (total_of(parts, q * HEAD, HEAD), total_of(parts, quads * HEAD + q, 1))
+        for q in range(first, first + count)
+    ]
+
+
+def half_sum_a_kernel(quads_a, *refs):
     parts, outs = refs[:-2], refs[-2:]
-    quads_in = 2 * quads_layer + quads_g
-    quads_out = quads_layer + quads_g
-
-    def total(at, size):
-        value = parts[0][at : at + size, :]
-        for part in parts[1:]:
-            value = value + part[at : at + size, :]
-        return value
-
-    shared = [
-        (total(q * HEAD, HEAD), total(quads_in * HEAD + q, 1))
-        for q in range(2 * quads_layer, quads_in)
-    ]
     for place, out in enumerate(outs):
-        both = [
-            (total(q * HEAD, HEAD), total(quads_in * HEAD + q, 1))
-            for q in range(place * quads_layer, (place + 1) * quads_layer)
-        ]
-        for q, (quad, diagonal) in enumerate(both + shared):
-            out[q * HEAD : (q + 1) * HEAD, :] = quad
-            out[quads_out * HEAD + q : quads_out * HEAD + q + 1, :] = diagonal
-        at = quads_out * (HEAD + 1)
-        for i, part in enumerate(parts):
-            ids_at = quads_in * (HEAD + 1)
-            out[at + i : at + i + 1, :] = part[ids_at : ids_at + 1, :]
-
-
-def sum_kernel(quads_a, quads_g, half, kept, came, own_ref, share_ref):
-    quads = quads_a + 2 * quads_g
-    diag_at = quads * HEAD
+        put_packed(out, take_packed(parts, place * quads_a, quads_a, 2 * quads_a))
+
+
+def half_sum_g_kernel(quads_g, *refs):
+    parts, outs = refs[:-2], refs[-2:]
+    quads = 3 * quads_g
+    shared = take_packed(parts, 2 * quads_g, quads_g, quads)
+    at = quads * (HEAD + 1)
+    ids = [part[at + 2 : at + 3, :] for part in parts]
+    for place, out in enumerate(outs):
+        own = take_packed(parts, place * quads_g, quads_g, quads)
+        put_packed(out, own + shared, [total_of(parts, at + place, 1)] + ids)
+
+
+def sum_g_kernel(quads_g, half, kept, came, share):
+    quads = 2 * quads_g
     row, _, col = pair_masks()
-    traces = []
-    first = 0
-    for count, where in ((quads_a, own_ref), (quads_g, share_ref), (quads_g, share_ref)):
+    packed = take_packed((kept, came), 0, quads, quads)
+    at = quads * (HEAD + 1)
+    traces = [kept[at : at + 1, :] + came[at : at + 1, :]]
+    for kind in range(2):
         trace = jnp.zeros((1, LANES), jnp.float32)
-        for q in range(first, first + count):
-            at = slice(q * HEAD, (q + 1) * HEAD)
-            quad = kept[at, :] + came[at, :]
-            at = slice(diag_at + q, diag_at + q + 1)
-            diagonal = kept[at, :] + came[at, :]
+        for quad, diagonal in packed[kind * quads_g : (kind + 1) * quads_g]:
             trace = trace + diagonal
             trace = trace + jnp.sum(jnp.where(col == row, quad, 0.0), axis=0, keepdims=True)
-            if where is own_ref:
-                own_ref[q * HEAD : (q + 1) * HEAD, :] = quad
-                own_ref[quads_a * HEAD + q : quads_a * HEAD + q + 1, :] = diagonal
-            else:
-                at = q - quads_a
-                share_ref[at * HEAD : (at + 1) * HEAD, :] = quad
-                share_ref[2 * quads_g * HEAD + at : 2 * quads_g * HEAD + at + 1, :] = diagonal
         traces.append(trace)
-        first += count
-    at = 2 * quads_g * (HEAD + 1)
-    for trace in traces:
-        share_ref[at : at + 1, :] = trace
-        at += 1
-    for ref in (kept, came):
-        for i in range(half):
-            ids_at = quads * (HEAD + 1) + i
-            share_ref[at : at + 1, :] = ref[ids_at : ids_at + 1, :]
-            at += 1
-
-
-def invert_apply_kernel(sizes, own_ref, share_hbm, w_hbm, e_hbm, w_out, e_out, *scratch):
-    quads_a, quads_g, n_tp, n_dp, tokens, vocab, inner, width, chunk = sizes
-    share, w_in, e_in, w_done, e_done, share_sem, w_sem, e_sem, w_out_sem, e_out_sem = scratch
-    tile_rows, inner_part = w_in.shape
+    ids = [ref[at + 1 + i : at + 2 + i, :] for ref in (kept, came) for i in range(half)]
+    put_packed(share, packed, traces + ids)
+
+
+def invert_apply_kernel(sizes, kept_a, came_a, share, e_in, w_hbm, *refs):
+    quads_a, quads_g, n_tp, n_dp, tokens, vocab, inner, width = sizes
+    came_w, w_out, e_out = refs[: n_tp - 1], refs[n_tp - 1], refs[n_tp]
+    w_own, w_done, e_done, w_sem, w_out_sem, e_out_sem = refs[n_tp + 1 :]
+    chunk, part = w_own.shape
     rows_e = e_in.shape[0]
-    chunks = tile_rows // chunk
+    me = lax.axis_index("tensor")
+    w_load = pltpu.make_async_copy(
+        w_hbm.at[:, pl.ds(pl.multiple_of(me * part, part), part)], w_own, w_sem
+    )
+    w_load.start()
+    w_in = [w_own, *came_w]
     e_parts = 2
     e_cols = width // e_parts
-    share_copy = pltpu.make_async_copy(share_hbm, share, share_sem)
-    w_loads = [
-        pltpu.make_async_copy(
-            w_hbm.at[pl.ds(c * chunk, chunk)], w_in.at[pl.ds(c * chunk, chunk)], w_sem.at[c]
-        )
-        for c in range(chunks)
-    ]
-    e_load = pltpu.make_async_copy(e_hbm, e_in, e_sem)
-    share_copy.start()
-    e_load.start()
-    for load in w_loads:
-        load.start()
-    share_copy.wait()
-
     trace_at = 2 * quads_g * (HEAD + 1)
 
     def trace_of(kind):
@@ -411,21 +406,16 @@
     ratio = jnp.sqrt(trace_a / (tokens * inner) / (trace_g / (tokens * width)))
     ratio_e = jnp.sqrt(tokens / vocab / (trace_e / (tokens * width)))
 
-    loaded = [
-        (
-            own_ref[q * HEAD : (q + 1) * HEAD, :],
-            own_ref[quads_a * HEAD + q : quads_a * HEAD + q + 1, :],
-        )
-        for q in range(quads_a)
-    ]
+    loaded = take_packed((kept_a, came_a), 0, quads_a, quads_a)
     diag_at = 2 * quads_g * HEAD
     for kind in range(2):
         for t in range(n_tp):
+            source = lax.bitwise_xor(me, t) if kind == 0 else t
             for q in range(kind * quads_g, (kind + 1) * quads_g):
                 loaded.append(
                     (
-                        share[t, q * HEAD : (q + 1) * HEAD, :],
-                        share[t, diag_at + q : diag_at + q + 1, :],
+                        share[source, q * HEAD : (q + 1) * HEAD, :],
+                        share[source, diag_at + q : diag_at + q + 1, :],
                     )
                 )
     pairs = []
@@ -483,7 +473,6 @@
             hits = hits + jnp.where(index == ids, 1.0, 0.0)
     scale = 1.0 / (jnp.sum(hits, axis=1, keepdims=True) + damp_root * ratio_e)
 
-    e_load.wait()
     stores = []
     for p in range(e_parts):
         for i in range(p * n_g // e_parts, (p + 1) * n_g // e_parts):
@@ -496,60 +485,67 @@
         )
         stores[-1].start()
     per_chunk = chunk // LANES
-    for c in range(chunks):
-        w_loads[c].wait()
-        for i in range(c * per_chunk, (c + 1) * per_chunk):
+    for k in range(n_tp):
+        if k == 0:
+            w_load.wait()
+        for i in range(per_chunk):
             rows = slice(i * LANES, (i + 1) * LANES)
-            factor = blocks_left(*inverses[n_a + i])
+            factor = blocks_left(*inverses[n_a + k * per_chunk + i])
             both = jnp.dot(
                 factor,
-                jnp.concatenate(split(w_in[rows, :]), axis=0),
+                jnp.concatenate(split(w_in[k][rows, :]), axis=0),
                 preferred_element_type=jnp.float32,
             )
             left = both[:LANES] + both[LANES:]
             for h in range(n_a):
                 at = slice(h * LANES, (h + 1) * LANES)
-                w_done[rows, at] = split_times(split(left[:, at]), right_a[h])
-        rows = pl.ds(c * chunk, chunk)
-        stores.append(
-            pltpu.make_async_copy(w_done.at[rows], w_out.at[rows], w_out_sem.at[c])
-        )
+                w_done[k, rows, at] = split_times(split(left[:, at]), right_a[h])
+        rows = pl.ds(pl.multiple_of(lax.bitwise_xor(me, k) * chunk, chunk), chunk)
+        stores.append(pltpu.make_async_copy(w_done.at[k], w_out.at[rows], w_out_sem.at[k]))
         stores[-1].start()
     for store in stores:
         store.wait()
 
 
-def invert_apply(own, shared, tile, grad_e, sizes):
-    n_tp = shared.shape[0]
-    chunk = sizes[-1]
-    tile_rows, inner_part = tile.shape
+def invert_apply(kept_a, came_a, shared, grad_e, grad_w, came_w, sizes):
+    n_tp = len(came_w) + 1
+    chunk, part = came_w[0].shape
     rows_e, width = grad_e.shape
     vmem = pl.BlockSpec(memory_space=pltpu.VMEM)
     hbm = pl.BlockSpec(memory_space=pltpu.HBM)
     return pl.pallas_call(
         functools.partial(invert_apply_kernel, sizes),
-        in_specs=[vmem, hbm, hbm, hbm],
+        in_specs=[vmem] * 4 + [hbm] + [vmem] * (n_tp - 1),
         out_specs=[hbm, hbm],
         out_shape=[
-            jax.ShapeDtypeStruct((tile_rows, inner_part), jnp.float32),
+            jax.ShapeDtypeStruct((chunk * n_tp, part), jnp.float32),
             jax.ShapeDtypeStruct((rows_e, width), jnp.float32),
         ],
         scratch_shapes=[
-            pltpu.VMEM(shared.shape, jnp.float32),
-            pltpu.VMEM(tile.shape, jnp.float32),
-            pltpu.VMEM(grad_e.shape, jnp.float32),
-            pltpu.VMEM(tile.shape, jnp.float32),
+            pltpu.VMEM((chunk, part), jnp.float32),
+            pltpu.VMEM((n_tp, chunk, part), jnp.float32),
             pltpu.VMEM(grad_e.shape, jnp.float32),
             pltpu.SemaphoreType.DMA,
-            pltpu.SemaphoreType.DMA((tile_rows // chunk,)),
-            pltpu.SemaphoreType.DMA,
-            pltpu.SemaphoreType.DMA((tile_rows // chunk,)),
+            pltpu.SemaphoreType.DMA((n_tp,)),
             pltpu.SemaphoreType.DMA((2,)),
         ],
-        compiler_params=pltpu.CompilerParams(vmem_limit_bytes=32 * 1024 * 1024),
+        compiler_params=pltpu.CompilerParams(vmem_limit_bytes=24 * 1024 * 1024),
         cost_estimate=small_cost(),
         name="invert_apply",
-    )(own, shared, tile, grad_e)
+    )(kept_a, came_a, shared, grad_e, grad_w, *came_w)
+
+
+def add_up(kernel, name, operands, rows):
+    vmem = pl.BlockSpec(memory_space=pltpu.VMEM)
+    return pl.pallas_call(
+        kernel,
+        in_specs=[vmem] * len(operands),
+        out_specs=[vmem] * len(rows),
+        out_shape=[jax.ShapeDtypeStruct((size, LANES), jnp.float32) for size in rows],
+        compiler_params=pltpu.CompilerParams(vmem_limit_bytes=8 * 1024 * 1024),
+        cost_estimate=small_cost(),
+        name=name,
+    )(*operands)
 
 
 def local(acts, out_cot, emb_ids, emb_cot, grad_w, grad_e):
@@ -567,7 +563,8 @@
         and tile_rows == width
         and inner_part % (4 * LANES) == 0
         and width_part % (2 * LANES) == 0
-        and n_tp % 2 == 0
+        and n_tp > 1
+        and n_tp & (n_tp - 1) == 0
         and emb_ids.shape[0] < LANES
         and rows_e % ROWS == 0
     )
@@ -577,34 +574,29 @@
     quads_g = width_part // (2 * LANES)
     half = n_dp // 2
 
-    def trade(value, k):
-        return lax.ppermute(value, "dp", [(i, i ^ k) for i in range(n_dp)])
-
-    *parts, sending = grams(
-        acts, out_cot, emb_cot, emb_ids, grad_w, lax.axis_index("dp"), n_dp, n_tp, quads_a, quads_g
-    )
-    tile = lax.all_to_all(sending, "tensor", split_axis=0, concat_axis=0, tiled=True)
-    tile = tile.reshape(tile_rows, inner_part)
-    arrived = [parts[0]] + [trade(parts[k], k) for k in range(1, half)]
-    kept_rows = round_up((quads_a + 2 * quads_g) * (HEAD + 1) + half, ROWS)
-    kept, mirror = pl.pallas_call(
-        functools.partial(half_sum_kernel, quads_a + quads_g, quads_g),
-        out_shape=[jax.ShapeDtypeStruct((kept_rows, LANES), jnp.float32)] * 2,
-        cost_estimate=small_cost(),
-        name="half_sums",
-    )(*arrived)
-    came = trade(mirror, half)
-    own_rows = round_up(quads_a * (HEAD + 1), ROWS)
+    def trade(value, k, axis="dp"):
+        size = lax.axis_size(axis)
+        return lax.ppermute(value, axis, [(i, i ^ k) for i in range(size)])
+
+    columns = column_parts(grad_w, n_tp)
+    came_w = [trade(columns[k - 1], k, "tensor") for k in range(1, n_tp)]
+    parts_g, parts_a = grams(acts, out_cot, emb_cot, emb_ids, came_w[0], n_dp, quads_a, quads_g)
+    arrived_g = [parts_g[0]] + [trade(parts_g[k], k) for k in range(1, half)]
+    arrived_a = [parts_a[0]] + [trade(parts_a[k], k) for k in range(1, half)]
+    kept_rows = round_up(2 * quads_g * (HEAD + 1) + 1 + half, ROWS)
+    kept_g, mirror_g = add_up(
+        functools.partial(half_sum_g_kernel, quads_g), "half_sums_g", arrived_g, [kept_rows] * 2
+    )
+    came_g = trade(mirror_g, half)
+    kept_rows = round_up(quads_a * (HEAD + 1), ROWS)
+    kept_a, mirror_a = add_up(
+        functools.partial(half_sum_a_kernel, quads_a), "half_sums_a", arrived_a, [kept_rows] * 2
+    )
+    came_a = trade(mirror_a, half)
     share_rows = round_up(2 * quads_g * (HEAD + 1) + 3 + n_dp, ROWS)
-    own, share = pl.pallas_call(
-        functools.partial(sum_kernel, quads_a, quads_g, half),
-        out_shape=[
-            jax.ShapeDtypeStruct((own_rows, LANES), jnp.float32),
-            jax.ShapeDtypeStruct((share_rows, LANES), jnp.float32),
-        ],
-        cost_estimate=small_cost(),
-        name="sums",
-    )(kept, came)
+    (share,) = add_up(
+        functools.partial(sum_g_kernel, quads_g, half), "sums_g", [kept_g, came_g], [share_rows]
+    )
     shared = lax.all_gather(share[None], "tensor", axis=0, tiled=True)
     sizes = (
         quads_a,
@@ -615,9 +607,8 @@
         rows_e * n_dp * n_tp,
         inner_part * n_tp,
         width,
-        2 * LANES,
-    )
-    return tuple(invert_apply(own, shared, tile, grad_e, sizes))
+    )
+    return tuple(invert_apply(kept_a, came_a, shared, grad_e, grad_w, came_w, sizes))
 
 
 def solution(mesh):

time: 62.8 us -> 39.8 us (0.63)
  waiting for transfers between devices: 17.5 us -> 4.21 us
  local copies, waits for them, and re-layouts: 11.6 us -> 3.72 us
  Pallas kernels: 15.4 us -> 7.66 us
  starting transfers between devices: 11.1 us -> 17.1 us
    ppermute x4 -> x11, waiting for transfers between devices: 17.5 us -> 4.21 us  [trade(): return lax.ppermute(value, axis, [(i, i ^ k) for i in range(size)])]
    ppermute x4 -> x11, starting transfers between devices: 6.77 us -> 17.1 us  [trade(): return lax.ppermute(value, axis, [(i, i ^ k) for i in range(size)])]
    unnamed x30 -> x12, local copies, waits for them, and re-layouts: 11.6 us -> 3.72 us
    pallas_call x3 -> x5, Pallas kernels: 8.42 us -> 1.5 us  [the longest x1 1.07 us: grams(): pl.pallas_call(functools.partial(gram_kernel, (quads_a, quads_g, n_dp)),...]
    all_to_all x1 -> x0, starting transfers between devices: 4.34 us -> none  [local(): lax.all_to_all(sending, 'tensor', split_axis=0, concat_axis=0, tiled=True)]
    pallas_call x1, Pallas kernels: 6.99 us -> 6.17 us  [invert_apply(): pl.pallas_call(functools.partial(invert_apply_kernel, sizes), in_specs=[v...]
  transfers between devices with their start and end apart: 5 -> 11, of which waited for: 4 -> 6; matrix products, arithmetic and copies ran while one was open for 0% -> 0% of each run, Pallas kernels for 6% -> 3%
where the time goes in v4:
time: 39.8 us; the launch traced here: 39.3 us
  starting transfers between devices  17.1 us (43%)
  Pallas kernels  7.66 us (19%)
  blocking collectives  5.93 us (15%)
  waiting for transfers between devices  4.21 us (11%)
  local copies, waits for them, and re-layouts  3.72 us (9%)
  between operations  0.69 us (2%)
    ppermute x11, starting transfers between devices, trade(): return lax.ppermute(value, axis, [(i, i ^ k) for i in range(size)])  17.1 us
    pallas_call x1, Pallas kernels, invert_apply(): pl.pallas_call(functools.partial(invert_apply_kernel, sizes), in_specs=[v...  6.17 us
    all_gather x1, blocking collectives, local(): shared = lax.all_gather(share[None], 'tensor', axis=0, tiled=True)  5.93 us
    ppermute x11, waiting for transfers between devices, trade(): return lax.ppermute(value, axis, [(i, i ^ k) for i in range(size)])  4.21 us
    unnamed x12, local copies, waits for them, and re-layouts  3.72 us
    pallas_call x1, Pallas kernels, grams(): pl.pallas_call(functools.partial(gram_kernel, (quads_a, quads_g, n_dp)),...  1.07 us
  transfers between devices with their start and end apart: 11, of which 6 were waited for; matrix products, arithmetic and copies ran while one was open for 0% of the time, Pallas kernels for 3%

profile of v4, /device:TPU:0, one launch (start us, length us, event | category | flops | bytes accessed | tf_op | source)
XLA Modules:
  0.0 39.3 jit_solution(16711252548474298396)
XLA Ops:
  0.6 1.6 %copy-done = f32[256,2048]{1,0:T(8,128)S(1)} copy-done((f32[256,2048]{1,0:T(8,128)S(1)}, f32[256,2048]{1,0:T(8,128)}, u32[]{:S(2)}) %copy-start) | copy-done | bytes 2097176
  2.2 0.3 column_parts.1
  2.5 0.5 %collective-permute-start = (f32[256,512]{1,0:T(8,128)S(1)}, f32[256,512]{1,0:T(8,128)S(1)}, u32[]{:S(2)}, u32[]{:S(2)}) collective-permute-start(f32[256,512]{1,0:T(8,128)S(1)} %get-tuple-element.17), channel_id=1, source_target_pairs={{0,1},{1,0},{2,3},{3,2},{4,5},{5,4},{6,7},{7,6},{8,9},{9,8},{10,11... | collective-permute-start | bytes 1572872 | tf_op jit(solution)/shard_map/ppermute | solution.py:579
  3.1 2.6 %collective-permute-start.9 = (f32[256,512]{1,0:T(8,128)S(1)}, f32[256,512]{1,0:T(8,128)S(1)}, u32[]{:S(2)}, u32[]{:S(2)}) collective-permute-start(f32[256,512]{1,0:T(8,128)S(1)} %get-tuple-element.30), channel_id=1, source_target_pairs={{0,2},{1,3},{2,0},{3,1},{4,6},{5,7},{6,4},{7,5},{8,10},{9,11},{10,... | collective-permute-start | bytes 1572872 | tf_op jit(solution)/shard_map/ppermute | solution.py:579
  5.6 0.1 collective-permute-start.10
  5.7 1.2 %copy-done.3 = bf16[8,256,256]{2,1,0:T(8,128)(2,1)S(1)} copy-done((bf16[8,256,256]{2,1,0:T(8,128)(2,1)S(1)}, bf16[8,256,256]{2,1,0:T(8,128)(2,1)}, u32[]{:S(2)}) %copy-start.3) | copy-done | bytes 1048600
  6.9 0.9 %copy-done.4 = bf16[256,256]{1,0:T(8,128)(2,1)S(1)} copy-done((bf16[256,256]{1,0:T(8,128)(2,1)S(1)}, bf16[256,256]{1,0:T(8,128)(2,1)}, u32[]{:S(2)}) %copy-start.4) | copy-done | bytes 131096
  7.8 1.1 %grams.1 = (f32[200,128]{1,0:T(8,128)S(1)}, f32[200,128]{1,0:T(8,128)S(1)}, f32[200,128]{1,0:T(8,128)S(1)}, f32[200,128]{1,0:T(8,128)S(1)}, f32[264,128]{1,0:T(8...) custom-call(s32[1,64]{1,0:T(1,128)S(1)} %bitcast.3, ...), custom_call_target="tpu_custom_call" | custom-call | flops 1000 | bytes 1000 | tf_op jit(solution)/shard_map/grams/pallas_call | solution.py:281
  8.9 1.8 %collective-permute-start.5 = (f32[200,128]{1,0:T(8,128)S(1)}, f32[200,128]{1,0:T(8,128)S(1)}, u32[]{:S(2)}, u32[]{:S(2)}) collective-permute-start(f32[200,128]{1,0:T(8,128)S(1)} %get-tuple-element.25), channel_id=1, source_target_pairs={{0,4},{4,0},{8,12},{12,8},{16,20},{20,16},{24,28},{28,24},{1,5},{5... | collective-permute-start | bytes 307208 | tf_op jit(solution)/shard_map/ppermute | solution.py:579
  10.8 1.6 %collective-permute-start.6 = (f32[200,128]{1,0:T(8,128)S(1)}, f32[200,128]{1,0:T(8,128)S(1)}, u32[]{:S(2)}, u32[]{:S(2)}) collective-permute-start(f32[200,128]{1,0:T(8,128)S(1)} %get-tuple-element.26), channel_id=1, source_target_pairs={{0,8},{4,12},{8,0},{12,4},{16,24},{20,28},{24,16},{28,20},{1,9},{5... | collective-permute-start | bytes 307208 | tf_op jit(solution)/shard_map/ppermute | solution.py:579
  12.3 0.1 collective-permute-start.7
  12.5 1.7 %collective-permute-done.5.refs_1_ = f32[200,128]{1,0:T(8,128)S(1)} collective-permute-done((f32[200,128]{1,0:T(8,128)S(1)}, f32[200,128]{1,0:T(8,128)S(1)}, u32[]{:S(2)}, u32[]{:S(2)}) %collective-permute-start.5) | collective-permute-done | bytes 102432 | tf_op jit(solution)/shard_map/ppermute | solution.py:579
  14.1 1.7 %collective-permute-start.1 = (f32[264,128]{1,0:T(8,128)S(1)}, f32[264,128]{1,0:T(8,128)S(1)}, u32[]{:S(2)}, u32[]{:S(2)}) collective-permute-start(f32[264,128]{1,0:T(8,128)S(1)} %get-tuple-element.19), channel_id=1, source_target_pairs={{0,4},{4,0},{8,12},{12,8},{16,20},{20,16},{24,28},{28,24},{1,5},{5... | collective-permute-start | bytes 405512 | tf_op jit(solution)/shard_map/ppermute | solution.py:579
  15.9 0.6 %collective-permute-done.6.refs_2_ = f32[200,128]{1,0:T(8,128)S(1)} collective-permute-done((f32[200,128]{1,0:T(8,128)S(1)}, f32[200,128]{1,0:T(8,128)S(1)}, u32[]{:S(2)}, u32[]{:S(2)}) %collective-permute-start.6) | collective-permute-done | bytes 102432 | tf_op jit(solution)/shard_map/ppermute | solution.py:579
  16.5 1.6 %collective-permute-start.2 = (f32[264,128]{1,0:T(8,128)S(1)}, f32[264,128]{1,0:T(8,128)S(1)}, u32[]{:S(2)}, u32[]{:S(2)}) collective-permute-start(f32[264,128]{1,0:T(8,128)S(1)} %get-tuple-element.20), channel_id=1, source_target_pairs={{0,8},{4,12},{8,0},{12,4},{16,24},{20,28},{24,16},{28,20},{1,9},{5... | collective-permute-start | bytes 405512 | tf_op jit(solution)/shard_map/ppermute | solution.py:579
  18.1 0.3 collective-permute-done.7.refs_3_
  18.4 2.0 %collective-permute-start.3 = (f32[264,128]{1,0:T(8,128)S(1)}, f32[264,128]{1,0:T(8,128)S(1)}, u32[]{:S(2)}, u32[]{:S(2)}) collective-permute-start(f32[264,128]{1,0:T(8,128)S(1)} %get-tuple-element.21), channel_id=1, source_target_pairs={{0,12},{4,8},{8,4},{12,0},{16,28},{20,24},{24,20},{28,16},{1,13},{... | collective-permute-start | bytes 405512 | tf_op jit(solution)/shard_map/ppermute | solution.py:579
  20.4 0.7 %collective-permute-done.1.refs_1_ = f32[264,128]{1,0:T(8,128)S(1)} collective-permute-done((f32[264,128]{1,0:T(8,128)S(1)}, f32[264,128]{1,0:T(8,128)S(1)}, u32[]{:S(2)}, u32[]{:S(2)}) %collective-permute-start.1) | collective-permute-done | bytes 135200 | tf_op jit(solution)/shard_map/ppermute | solution.py:579
  21.1 2.6 %collective-permute-start.8 = (f32[136,128]{1,0:T(8,128)S(1)}, f32[136,128]{1,0:T(8,128)S(1)}, u32[]{:S(2)}, u32[]{:S(2)}) collective-permute-start(f32[136,128]{1,0:T(8,128)S(1)} %get-tuple-element.29), channel_id=1, source_target_pairs={{0,16},{4,20},{8,24},{12,28},{16,0},{20,4},{24,8},{28,12},{1,17},{... | collective-permute-start | bytes 208904 | tf_op jit(solution)/shard_map/ppermute | solution.py:579
  23.7 0.6 %collective-permute-done.3.refs_3_ = f32[264,128]{1,0:T(8,128)S(1)} collective-permute-done((f32[264,128]{1,0:T(8,128)S(1)}, f32[264,128]{1,0:T(8,128)S(1)}, u32[]{:S(2)}, u32[]{:S(2)}) %collective-permute-start.3) | collective-permute-done | bytes 135200 | tf_op jit(solution)/shard_map/ppermute | solution.py:579
  24.4 2.5 %collective-permute-start.4 = (f32[136,128]{1,0:T(8,128)S(1)}, f32[136,128]{1,0:T(8,128)S(1)}, u32[]{:S(2)}, u32[]{:S(2)}) collective-permute-start(f32[136,128]{1,0:T(8,128)S(1)} %get-tuple-element.23), channel_id=1, source_target_pairs={{0,16},{4,20},{8,24},{12,28},{16,0},{20,4},{24,8},{28,12},{1,17},{... | collective-permute-start | bytes 208904 | tf_op jit(solution)/shard_map/ppermute | solution.py:579
  26.9 0.3 collective-permute-done.8.came
  27.2 5.9 %all-gather = f32[576,128]{1,0:T(8,128)S(1)} all-gather(f32[144,128]{1,0:T(8,128)S(1)} %sums_g.1), channel_id=2, replica_groups=mesh['dp'=8,'tensor'=4] {'tensor'}, dimensions={0}, use_global_device_ids=true | all-gather | bytes 368640 | tf_op jit(solution)/shard_map/all_gather | solution.py:600
  33.2 6.2 %invert_apply.1 = (f32[1024,512]{1,0:T(8,128)}, f32[256,1024]{1,0:T(8,128)}) custom-call(f32[136,128]{1,0:T(8,128)S(1)} %get-tuple-element.22.kept_a, f32[136,128]{1,0:T(8,128)S(1)} %collective-permute-done.4.came_a, f32[4,144,128]{2,1,0:T(8,128)S(1)} %bitcast.2, f32[256,1024]{1,0:T(8,128)S(1)} %copy-done.2, f32[256,2048]{1,0:T(8,128)S(1)} %copy-done, ...), custom_call_target="tpu_custom_call" | custom-call | flops 1000 | bytes 1000 | tf_op jit(solution)/shard_map/invert_apply/pallas_call | solution.py:516
  (17 shorter events, 0.1 us)
Async XLA Ops:
  0.6 1.6 %copy-start = (f32[256,2048]{1,0:T(8,128)S(1)}, f32[256,2048]{1,0:T(8,128)}, u32[]{:S(2)}) copy-start(f32[256,2048]{1,0:T(8,128)} %w_hbm.3) | copy-start | bytes 6291460
  2.2 3.5 %copy-start.1 = (bf16[8,256,512]{2,1,0:T(8,128)(2,1)S(1)}, bf16[8,256,512]{2,1,0:T(8,128)(2,1)}, u32[]{:S(2)}) copy-start(bf16[8,256,512]{2,1,0:T(8,128)(2,1)} %acts.1) | copy-start | bytes 6291460
  2.2 3.5 %copy-start.5 = (s32[64]{0:T(128)S(1)}, s32[64]{0:T(128)}, u32[]{:S(2)}) copy-start(s32[64]{0:T(128)} %param.8) | copy-start | bytes 772
  2.5 3.2 %collective-permute-start = (f32[256,512]{1,0:T(8,128)S(1)}, f32[256,512]{1,0:T(8,128)S(1)}, u32[]{:S(2)}, u32[]{:S(2)}) collective-permute-start(f32[256,512]{1,0:T(8,128)S(1)} %get-tuple-element.17), channel_id=1, source_target_pairs={{0,1},{1,0},{2,3},{3,2},{4,5},{5,4},{6,7},{7,6},{8,9},{9,8},{10,11... | collective-permute-start | bytes 1572872 | tf_op jit(solution)/shard_map/ppermute | solution.py:579
  3.1 30.1 %collective-permute-start.9 = (f32[256,512]{1,0:T(8,128)S(1)}, f32[256,512]{1,0:T(8,128)S(1)}, u32[]{:S(2)}, u32[]{:S(2)}) collective-permute-start(f32[256,512]{1,0:T(8,128)S(1)} %get-tuple-element.30), channel_id=1, source_target_pairs={{0,2},{1,3},{2,0},{3,1},{4,6},{5,7},{6,4},{7,5},{8,10},{9,11},{10,... | collective-permute-start | bytes 1572872 | tf_op jit(solution)/shard_map/ppermute | solution.py:579
  5.6 27.5 %collective-permute-start.10 = (f32[256,512]{1,0:T(8,128)S(1)}, f32[256,512]{1,0:T(8,128)S(1)}, u32[]{:S(2)}, u32[]{:S(2)}) collective-permute-start(f32[256,512]{1,0:T(8,128)S(1)} %get-tuple-element.31), channel_id=1, source_target_pairs={{0,3},{1,2},{2,1},{3,0},{4,7},{5,6},{6,5},{7,4},{8,11},{9,10},{10,... | collective-permute-start | bytes 1572872 | tf_op jit(solution)/shard_map/ppermute | solution.py:579
  5.7 1.2 %copy-start.3 = (bf16[8,256,256]{2,1,0:T(8,128)(2,1)S(1)}, bf16[8,256,256]{2,1,0:T(8,128)(2,1)}, u32[]{:S(2)}) copy-start(bf16[8,256,256]{2,1,0:T(8,128)(2,1)} %cot.1) | copy-start | bytes 3145732
  6.9 0.9 %copy-start.4 = (bf16[256,256]{1,0:T(8,128)(2,1)S(1)}, bf16[256,256]{1,0:T(8,128)(2,1)}, u32[]{:S(2)}) copy-start(bf16[256,256]{1,0:T(8,128)(2,1)} %emb.1) | copy-start | bytes 393220
  7.8 25.3 %copy-start.2 = (f32[256,1024]{1,0:T(8,128)S(1)}, f32[256,1024]{1,0:T(8,128)}, u32[]{:S(2)}) copy-start(f32[256,1024]{1,0:T(8,128)} %e_in.1) | copy-start | bytes 3145732
  8.9 5.2 %collective-permute-start.5 = (f32[200,128]{1,0:T(8,128)S(1)}, f32[200,128]{1,0:T(8,128)S(1)}, u32[]{:S(2)}, u32[]{:S(2)}) collective-permute-start(f32[200,128]{1,0:T(8,128)S(1)} %get-tuple-element.25), channel_id=1, source_target_pairs={{0,4},{4,0},{8,12},{12,8},{16,20},{20,16},{24,28},{28,24},{1,5},{5... | collective-permute-start | bytes 307208 | tf_op jit(solution)/shard_map/ppermute | solution.py:579
  10.8 5.7 %collective-permute-start.6 = (f32[200,128]{1,0:T(8,128)S(1)}, f32[200,128]{1,0:T(8,128)S(1)}, u32[]{:S(2)}, u32[]{:S(2)}) collective-permute-start(f32[200,128]{1,0:T(8,128)S(1)} %get-tuple-element.26), channel_id=1, source_target_pairs={{0,8},{4,12},{8,0},{12,4},{16,24},{20,28},{24,16},{28,20},{1,9},{5... | collective-permute-start | bytes 307208 | tf_op jit(solution)/shard_map/ppermute | solution.py:579
  12.3 6.0 %collective-permute-start.7 = (f32[200,128]{1,0:T(8,128)S(1)}, f32[200,128]{1,0:T(8,128)S(1)}, u32[]{:S(2)}, u32[]{:S(2)}) collective-permute-start(f32[200,128]{1,0:T(8,128)S(1)} %get-tuple-element.27), channel_id=1, source_target_pairs={{0,12},{4,8},{8,4},{12,0},{16,28},{20,24},{24,20},{28,16},{1,13},{... | collective-permute-start | bytes 307208 | tf_op jit(solution)/shard_map/ppermute | solution.py:579
  14.1 7.0 %collective-permute-start.1 = (f32[264,128]{1,0:T(8,128)S(1)}, f32[264,128]{1,0:T(8,128)S(1)}, u32[]{:S(2)}, u32[]{:S(2)}) collective-permute-start(f32[264,128]{1,0:T(8,128)S(1)} %get-tuple-element.19), channel_id=1, source_target_pairs={{0,4},{4,0},{8,12},{12,8},{16,20},{20,16},{24,28},{28,24},{1,5},{5... | collective-permute-start | bytes 405512 | tf_op jit(solution)/shard_map/ppermute | solution.py:579
  16.5 7.2 %collective-permute-start.2 = (f32[264,128]{1,0:T(8,128)S(1)}, f32[264,128]{1,0:T(8,128)S(1)}, u32[]{:S(2)}, u32[]{:S(2)}) collective-permute-start(f32[264,128]{1,0:T(8,128)S(1)} %get-tuple-element.20), channel_id=1, source_target_pairs={{0,8},{4,12},{8,0},{12,4},{16,24},{20,28},{24,16},{28,20},{1,9},{5... | collective-permute-start | bytes 405512 | tf_op jit(solution)/shard_map/ppermute | solution.py:579
  18.4 5.9 %collective-permute-start.3 = (f32[264,128]{1,0:T(8,128)S(1)}, f32[264,128]{1,0:T(8,128)S(1)}, u32[]{:S(2)}, u32[]{:S(2)}) collective-permute-start(f32[264,128]{1,0:T(8,128)S(1)} %get-tuple-element.21), channel_id=1, source_target_pairs={{0,12},{4,8},{8,4},{12,0},{16,28},{20,24},{24,20},{28,16},{1,13},{... | collective-permute-start | bytes 405512 | tf_op jit(solution)/shard_map/ppermute | solution.py:579
  21.1 6.1 %collective-permute-start.8 = (f32[136,128]{1,0:T(8,128)S(1)}, f32[136,128]{1,0:T(8,128)S(1)}, u32[]{:S(2)}, u32[]{:S(2)}) collective-permute-start(f32[136,128]{1,0:T(8,128)S(1)} %get-tuple-element.29), channel_id=1, source_target_pairs={{0,16},{4,20},{8,24},{12,28},{16,0},{20,4},{24,8},{28,12},{1,17},{... | collective-permute-start | bytes 208904 | tf_op jit(solution)/shard_map/ppermute | solution.py:579
  24.4 8.8 %collective-permute-start.4 = (f32[136,128]{1,0:T(8,128)S(1)}, f32[136,128]{1,0:T(8,128)S(1)}, u32[]{:S(2)}, u32[]{:S(2)}) collective-permute-start(f32[136,128]{1,0:T(8,128)S(1)} %get-tuple-element.23), channel_id=1, source_target_pairs={{0,16},{4,20},{8,24},{12,28},{16,0},{20,4},{24,8},{28,12},{1,17},{... | collective-permute-start | bytes 208904 | tf_op jit(solution)/shard_map/ppermute | solution.py:579

commit v5 on v4

--- a/solution.py
+++ b/solution.py
@@ -12,6 +12,7 @@
 LANES = 128
 HALF = HEAD
 ROWS = 8
+REST = 96
 
 
 damp_root = 0.7
@@ -204,6 +205,13 @@
     )
 
 
+def times_left(factor, value):
+    both = jnp.dot(
+        factor, jnp.concatenate(split(value), axis=0), preferred_element_type=jnp.float32
+    )
+    return both[:LANES] + both[LANES:]
+
+
 def add_halves(both):
     return both[:, :LANES] + both[:, LANES:]
 
@@ -264,6 +272,10 @@
 
 def small_cost():
     return pl.CostEstimate(flops=1000, bytes_accessed=1000, transcendentals=0)
+
+
+def long_cost():
+    return pl.CostEstimate(flops=20_000_000_000, bytes_accessed=4_000_000, transcendentals=0)
 
 
 def round_up(value, unit):
@@ -288,47 +300,38 @@
         cost_estimate=small_cost(),
         name="grams",
     )(emb_ids.reshape(1, -1), acts, out_cot, emb_cot, after)
-    return outs[:half], outs[half:]
+    return list(outs[:half]), list(outs[half:])
 
 
 def column_parts_kernel(n_tp, w_hbm, *refs):
-    outs = refs[: n_tp - 1]
-    w, load_sem, move_sem = refs[n_tp - 1 :]
+    outs, sems = refs[:n_tp], refs[n_tp]
     me = lax.axis_index("tensor")
-    part = w.shape[2]
-    loads, moves = [], []
-    for k in range(n_tp - 1, 0, -1):
-        at = pl.multiple_of(lax.bitwise_xor(me, k) * part, part)
-        loads.append(
-            pltpu.make_async_copy(
-                w_hbm.at[:, pl.ds(at, part)], w.at[k - 1], load_sem.at[k - 1]
-            )
-        )
-        moves.append(pltpu.make_async_copy(w.at[k - 1], outs[k - 1], move_sem.at[k - 1]))
-        loads[-1].start()
-    for load, move in zip(loads, moves):
-        load.wait()
+    rows, part = outs[0].shape
+    moves = []
+    for i, out in enumerate(outs):
+        at = lax.bitwise_xor(me, min(i + 1, n_tp - 1)) * part
+        block = w_hbm.at[
+            pl.ds(rows - REST if i == n_tp - 1 else 0, out.shape[0]),
+            pl.ds(pl.multiple_of(at, LANES), part),
+        ]
+        moves.append(pltpu.make_async_copy(block, out, sems.at[i]))
+    for move in moves[::-1]:
         move.start()
-    for move in moves:
+    for move in moves[::-1]:
         move.wait()
 
 
 def column_parts(grad_w, n_tp):
     rows, width = grad_w.shape
-    part = (rows, width // n_tp)
-    hbm = pl.BlockSpec(memory_space=pltpu.HBM)
+    heights = [rows] * (n_tp - 2) + [rows - REST, REST]
     return pl.pallas_call(
         functools.partial(column_parts_kernel, n_tp),
-        in_specs=[hbm],
-        out_specs=[hbm] * (n_tp - 1),
-        out_shape=[jax.ShapeDtypeStruct(part, jnp.float32)] * (n_tp - 1),
-        scratch_shapes=[
-            pltpu.VMEM((n_tp - 1, *part), jnp.float32),
-            pltpu.SemaphoreType.DMA((n_tp - 1,)),
-            pltpu.SemaphoreType.DMA((n_tp - 1,)),
-        ],
+        in_specs=[pl.BlockSpec(memory_space=pltpu.HBM)],
+        out_specs=[pl.BlockSpec(memory_space=pltpu.VMEM)] * n_tp,
+        out_shape=[jax.ShapeDtypeStruct((size, width // n_tp), jnp.float32) for size in heights],
+        scratch_shapes=[pltpu.SemaphoreType.DMA((n_tp,))],
         compiler_params=pltpu.CompilerParams(vmem_limit_bytes=40 * 1024 * 1024),
-        cost_estimate=small_cost(),
+        cost_estimate=long_cost(),
         name="column_parts",
     )(grad_w)
 
@@ -353,18 +356,22 @@
         put_packed(out, take_packed(parts, place * quads_a, quads_a, 2 * quads_a))
 
 
-def half_sum_g_kernel(quads_g, *refs):
-    parts, outs = refs[:-2], refs[-2:]
+def half_sum_g_kernel(quads_g, half, *refs):
+    parts, outs = refs[:half], refs[-2:]
     quads = 3 * quads_g
     shared = take_packed(parts, 2 * quads_g, quads_g, quads)
     at = quads * (HEAD + 1)
-    ids = [part[at + 2 : at + 3, :] for part in parts]
+    ids = [
+        jnp.maximum(one[at + 2 : at + 3, :], pltpu.roll(two[at + 2 : at + 3, :], HALF, 1))
+        for one, two in zip(parts[::2], parts[1::2])
+    ]
     for place, out in enumerate(outs):
         own = take_packed(parts, place * quads_g, quads_g, quads)
         put_packed(out, own + shared, [total_of(parts, at + place, 1)] + ids)
 
 
-def sum_g_kernel(quads_g, half, kept, came, share):
+def sum_g_kernel(quads_g, half, kept, came, *refs):
+    share = refs[-1]
     quads = 2 * quads_g
     row, _, col = pair_masks()
     packed = take_packed((kept, came), 0, quads, quads)
@@ -376,57 +383,32 @@
             trace = trace + diagonal
             trace = trace + jnp.sum(jnp.where(col == row, quad, 0.0), axis=0, keepdims=True)
         traces.append(trace)
-    ids = [ref[at + 1 + i : at + 2 + i, :] for ref in (kept, came) for i in range(half)]
+    ids = [ref[at + 1 + i : at + 2 + i, :] for ref in (kept, came) for i in range(half // 2)]
     put_packed(share, packed, traces + ids)
 
 
-def invert_apply_kernel(sizes, kept_a, came_a, share, e_in, w_hbm, *refs):
-    quads_a, quads_g, n_tp, n_dp, tokens, vocab, inner, width = sizes
-    came_w, w_out, e_out = refs[: n_tp - 1], refs[n_tp - 1], refs[n_tp]
-    w_own, w_done, e_done, w_sem, w_out_sem, e_out_sem = refs[n_tp + 1 :]
-    chunk, part = w_own.shape
-    rows_e = e_in.shape[0]
-    me = lax.axis_index("tensor")
-    w_load = pltpu.make_async_copy(
-        w_hbm.at[:, pl.ds(pl.multiple_of(me * part, part), part)], w_own, w_sem
-    )
-    w_load.start()
-    w_in = [w_own, *came_w]
-    e_parts = 2
-    e_cols = width // e_parts
-    trace_at = 2 * quads_g * (HEAD + 1)
-
-    def trace_of(kind):
-        value = share[0, trace_at + kind : trace_at + kind + 1, :]
+def trace_sums(lines, n_tp):
+    sums = []
+    for kind in range(3):
+        value = lines(0, kind)
         for t in range(1, n_tp):
-            value = value + share[t, trace_at + kind : trace_at + kind + 1, :]
-        return jnp.sum(value, axis=1, keepdims=True)
-
-    trace_a, trace_g, trace_e = trace_of(0), trace_of(1), trace_of(2)
-    ratio = jnp.sqrt(trace_a / (tokens * inner) / (trace_g / (tokens * width)))
-    ratio_e = jnp.sqrt(tokens / vocab / (trace_e / (tokens * width)))
-
-    loaded = take_packed((kept_a, came_a), 0, quads_a, quads_a)
-    diag_at = 2 * quads_g * HEAD
-    for kind in range(2):
-        for t in range(n_tp):
-            source = lax.bitwise_xor(me, t) if kind == 0 else t
-            for q in range(kind * quads_g, (kind + 1) * quads_g):
-                loaded.append(
-                    (
-                        share[source, q * HEAD : (q + 1) * HEAD, :],
-                        share[source, diag_at + q : diag_at + q + 1, :],
-                    )
-                )
+            value = value + lines(t, kind)
+        sums.append(jnp.sum(value, axis=1, keepdims=True))
+    return sums
+
+
+def unpack_all(packed):
     pairs = []
-    for i in range(0, len(loaded), 2):
-        pairs += unpack_quads(*loaded[i], *loaded[i + 1])
-    n_a, n_g = 2 * quads_a, 2 * quads_g * n_tp
-
-    row, lane, col = pair_masks()
+    for i in range(0, len(packed), 2):
+        pairs += unpack_quads(*packed[i], *packed[i + 1])
+    return pairs
+
+
+def invert_pairs(pairs, shifts, tokens):
+    _, lane, _ = pair_masks()
+    row, _, col = pair_masks()
     eye = jnp.where(col == row, 1.0, 0.0)
     low_lane = lane[:1] < HALF
-    shifts = [damp_root * ratio] * n_a + [damp_root / ratio] * n_g + [damp_root / ratio_e] * n_g
     images, over = [], []
     for pair, shift in zip(pairs, shifts):
         damped = pair * (1.0 / tokens) + shift * eye
@@ -461,45 +443,133 @@
             approx = [
                 2.0 * a - split_times(split(a), factor) for a, factor in zip(approx, factors)
             ]
-    inverses = [split(a * b) for a, b in zip(approx, over)]
-    right_a = [blocks_right(*parts) for parts in inverses[:n_a]]
-
-    base = ((lax.axis_index("dp") * n_tp + lax.axis_index("tensor")) * rows_e).astype(jnp.float32)
+    return [split(a * b) for a, b in zip(approx, over)]
+
+
+def apply_g_kernel(sizes, e_in, w_hbm, *refs):
+    quads_g, n_tp, n_dp, tokens, vocab, inner, width = sizes
+    shares, came_w = refs[:n_tp], refs[n_tp : 2 * n_tp - 1]
+    left_out, rest_out, ratio_out, e_out = refs[2 * n_tp - 1 : 2 * n_tp + 3]
+    share, w_own, e_done, w_sem, e_out_sem = refs[2 * n_tp + 3 :]
+    chunk, part = w_own.shape
+    rows_e = e_in.shape[0]
+    me = lax.axis_index("tensor")
+    w_load = pltpu.make_async_copy(
+        w_hbm.at[:, pl.ds(pl.multiple_of(me * part, part), part)], w_own, w_sem
+    )
+    w_load.start()
+    for k, ref in enumerate(shares):
+        share[lax.bitwise_xor(me, k)] = ref[...]
+
+    trace_at = 2 * quads_g * (HEAD + 1)
+    trace_a, trace_g, trace_e = trace_sums(
+        lambda t, kind: share[t, trace_at + kind : trace_at + kind + 1, :], n_tp
+    )
+    ratio = jnp.sqrt(trace_a / (tokens * inner) / (trace_g / (tokens * width)))
+    ratio_e = jnp.sqrt(tokens / vocab / (trace_e / (tokens * width)))
+    ratio_out[...] = jnp.broadcast_to(ratio, ratio_out.shape)
+
+    packed = []
+    diag_at = 2 * quads_g * HEAD
+    for kind in range(2):
+        for t in range(n_tp):
+            source = lax.bitwise_xor(me, t) if kind == 0 else t
+            for q in range(kind * quads_g, (kind + 1) * quads_g):
+                packed.append(
+                    (
+                        share[source, q * HEAD : (q + 1) * HEAD, :],
+                        share[source, diag_at + q : diag_at + q + 1, :],
+                    )
+                )
+    n_g = 2 * quads_g * n_tp
+    shifts = [damp_root / ratio] * n_g + [damp_root / ratio_e] * n_g
+    inverses = invert_pairs(unpack_all(packed), shifts, tokens)
+
+    base = ((lax.axis_index("dp") * n_tp + me) * rows_e).astype(jnp.float32)
     index = lax.broadcasted_iota(jnp.int32, (rows_e, LANES), 0).astype(jnp.float32) + base
     hits = jnp.zeros((rows_e, LANES), jnp.float32)
     for t in range(n_tp):
-        for d in range(n_dp):
+        for d in range(n_dp // 2):
             ids = share[t, trace_at + 3 + d : trace_at + 4 + d, :]
             hits = hits + jnp.where(index == ids, 1.0, 0.0)
     scale = 1.0 / (jnp.sum(hits, axis=1, keepdims=True) + damp_root * ratio_e)
 
     stores = []
+    e_parts = 2
+    e_cols = width // e_parts
     for p in range(e_parts):
         for i in range(p * n_g // e_parts, (p + 1) * n_g // e_parts):
             at = slice(i * LANES, (i + 1) * LANES)
-            factor = blocks_right(*inverses[n_a + n_g + i])
+            factor = blocks_right(*inverses[n_g + i])
             e_done[:, at] = split_times(split(e_in[:, at]), factor) * scale
         cols = pl.ds(p * e_cols, e_cols)
         stores.append(
             pltpu.make_async_copy(e_done.at[:, cols], e_out.at[:, cols], e_out_sem.at[p])
         )
         stores[-1].start()
+    w_load.wait()
     per_chunk = chunk // LANES
+    for k, w_in in enumerate([w_own, *came_w]):
+        for i in range(per_chunk):
+            factor = blocks_left(*inverses[k * per_chunk + i])
+            if (i + 1) * LANES > w_in.shape[0]:
+                rest_out[...] = factor
+            else:
+                rows = slice(i * LANES, (i + 1) * LANES)
+                left_out[k, rows, :] = times_left(factor, w_in[rows, :])
+    for store in stores:
+        store.wait()
+
+
+def apply_g(shares, grad_e, grad_w, came_w, sizes):
+    n_tp = len(shares)
+    chunk, part = came_w[0].shape
+    rows_e, width = grad_e.shape
+    vmem = pl.BlockSpec(memory_space=pltpu.VMEM)
+    hbm = pl.BlockSpec(memory_space=pltpu.HBM)
+    return pl.pallas_call(
+        functools.partial(apply_g_kernel, sizes),
+        in_specs=[vmem, hbm] + [vmem] * (2 * n_tp - 1),
+        out_specs=[vmem, vmem, vmem, hbm],
+        out_shape=[
+            jax.ShapeDtypeStruct((n_tp, chunk, part), jnp.float32),
+            jax.ShapeDtypeStruct((2 * LANES, 2 * LANES), jnp.bfloat16),
+            jax.ShapeDtypeStruct((ROWS, LANES), jnp.float32),
+            jax.ShapeDtypeStruct((rows_e, width), jnp.float32),
+        ],
+        scratch_shapes=[
+            pltpu.VMEM((n_tp, *shares[0].shape), jnp.float32),
+            pltpu.VMEM((chunk, part), jnp.float32),
+            pltpu.VMEM(grad_e.shape, jnp.float32),
+            pltpu.SemaphoreType.DMA,
+            pltpu.SemaphoreType.DMA((2,)),
+        ],
+        compiler_params=pltpu.CompilerParams(vmem_limit_bytes=24 * 1024 * 1024),
+        cost_estimate=pl.CostEstimate(flops=1000, bytes_accessed=8000000, transcendentals=0),
+        name="apply_g",
+    )(grad_e, grad_w, *shares, *came_w)
+
+
+def apply_a_kernel(sizes, kept, came, ratio, left, last_w, rest_w, rest, w_out, w_done, w_out_sem):
+    quads_a, tokens = sizes
+    n_tp, chunk, part = left.shape
+    me = lax.axis_index("tensor")
+    shift = damp_root * ratio[:1, :1]
+    pairs = unpack_all(take_packed((kept, came), 0, quads_a, quads_a))
+    inverses = invert_pairs(pairs, [shift] * len(pairs), tokens)
+    factors = [blocks_right(*parts) for parts in inverses]
+    stores = []
     for k in range(n_tp):
-        if k == 0:
-            w_load.wait()
-        for i in range(per_chunk):
-            rows = slice(i * LANES, (i + 1) * LANES)
-            factor = blocks_left(*inverses[n_a + k * per_chunk + i])
-            both = jnp.dot(
-                factor,
-                jnp.concatenate(split(w_in[k][rows, :]), axis=0),
-                preferred_element_type=jnp.float32,
-            )
-            left = both[:LANES] + both[LANES:]
-            for h in range(n_a):
-                at = slice(h * LANES, (h + 1) * LANES)
-                w_done[k, rows, at] = split_times(split(left[:, at]), right_a[h])
+        value = left[k]
+        if k == n_tp - 1:
+            last = rest_w[...]
+            if REST < LANES:
+                last = jnp.concatenate([last_w[chunk - LANES : chunk - REST, :], last], axis=0)
+            last = times_left(rest[...], last)
+            value = jnp.concatenate([left[k, : chunk - LANES, :], last], axis=0)
+        for h, factor in enumerate(factors):
+            at = slice(h * LANES, (h + 1) * LANES)
+            w_done[k, :, at] = split_times(split(value[:, at]), factor)
         rows = pl.ds(pl.multiple_of(lax.bitwise_xor(me, k) * chunk, chunk), chunk)
         stores.append(pltpu.make_async_copy(w_done.at[k], w_out.at[rows], w_out_sem.at[k]))
         stores[-1].start()
@@ -507,45 +577,54 @@
         store.wait()
 
 
-def invert_apply(kept_a, came_a, shared, grad_e, grad_w, came_w, sizes):
-    n_tp = len(came_w) + 1
-    chunk, part = came_w[0].shape
-    rows_e, width = grad_e.shape
+def apply_a(kept, came, ratio, left, last_w, rest_w, rest, sizes):
+    n_tp, chunk, part = left.shape
+    vmem = pl.BlockSpec(memory_space=pltpu.VMEM)
+    return pl.pallas_call(
+        functools.partial(apply_a_kernel, sizes),
+        in_specs=[vmem] * 7,
+        out_specs=pl.BlockSpec(memory_space=pltpu.HBM),
+        out_shape=jax.ShapeDtypeStruct((n_tp * chunk, part), jnp.float32),
+        scratch_shapes=[
+            pltpu.VMEM(left.shape, jnp.float32),
+            pltpu.SemaphoreType.DMA((n_tp,)),
+        ],
+        compiler_params=pltpu.CompilerParams(vmem_limit_bytes=24 * 1024 * 1024),
+        cost_estimate=small_cost(),
+        name="apply_a",
+    )(kept, came, ratio, left, last_w, rest_w, rest)
+
+
+def hold_kernel(*refs):
+    pass
+
+
+def hold(value, *after):
+    hbm = pl.BlockSpec(memory_space=pltpu.HBM)
+    return pl.pallas_call(
+        hold_kernel,
+        in_specs=[hbm] * (1 + len(after)),
+        out_specs=hbm,
+        out_shape=jax.ShapeDtypeStruct(value.shape, value.dtype),
+        input_output_aliases={0: 0},
+        compiler_params=pltpu.CompilerParams(vmem_limit_bytes=8 * 1024 * 1024),
+        cost_estimate=small_cost(),
+        name="hold",
+    )(value, *after)
+
+
+def add_up(kernel, name, operands, rows, after=()):
     vmem = pl.BlockSpec(memory_space=pltpu.VMEM)
     hbm = pl.BlockSpec(memory_space=pltpu.HBM)
     return pl.pallas_call(
-        functools.partial(invert_apply_kernel, sizes),
-        in_specs=[vmem] * 4 + [hbm] + [vmem] * (n_tp - 1),
-        out_specs=[hbm, hbm],
-        out_shape=[
-            jax.ShapeDtypeStruct((chunk * n_tp, part), jnp.float32),
-            jax.ShapeDtypeStruct((rows_e, width), jnp.float32),
-        ],
-        scratch_shapes=[
-            pltpu.VMEM((chunk, part), jnp.float32),
-            pltpu.VMEM((n_tp, chunk, part), jnp.float32),
-            pltpu.VMEM(grad_e.shape, jnp.float32),
-            pltpu.SemaphoreType.DMA,
-            pltpu.SemaphoreType.DMA((n_tp,)),
-            pltpu.SemaphoreType.DMA((2,)),
-        ],
-        compiler_params=pltpu.CompilerParams(vmem_limit_bytes=24 * 1024 * 1024),
-        cost_estimate=small_cost(),
-        name="invert_apply",
-    )(kept_a, came_a, shared, grad_e, grad_w, *came_w)
-
-
-def add_up(kernel, name, operands, rows):
-    vmem = pl.BlockSpec(memory_space=pltpu.VMEM)
-    return pl.pallas_call(
         kernel,
-        in_specs=[vmem] * len(operands),
+        in_specs=[vmem] * len(operands) + [hbm] * len(after),
         out_specs=[vmem] * len(rows),
         out_shape=[jax.ShapeDtypeStruct((size, LANES), jnp.float32) for size in rows],
         compiler_params=pltpu.CompilerParams(vmem_limit_bytes=8 * 1024 * 1024),
         cost_estimate=small_cost(),
         name=name,
-    )(*operands)
+    )(*operands, *after)
 
 
 def local(acts, out_cot, emb_ids, emb_cot, grad_w, grad_e):
@@ -558,14 +637,15 @@
     tile_rows = grad_w.shape[0] * n_tp
     direct = (
         layers == n_dp
-        and n_dp > 1
+        and n_dp > 2
         and n_dp & (n_dp - 1) == 0
         and tile_rows == width
         and inner_part % (4 * LANES) == 0
         and width_part % (2 * LANES) == 0
         and n_tp > 1
+        and grad_w.shape[0] % (2 * LANES) == 0
         and n_tp & (n_tp - 1) == 0
-        and emb_ids.shape[0] < LANES
+        and emb_ids.shape[0] <= HALF
         and rows_e % ROWS == 0
     )
     if not direct:
@@ -580,12 +660,16 @@
 
     columns = column_parts(grad_w, n_tp)
     came_w = [trade(columns[k - 1], k, "tensor") for k in range(1, n_tp)]
+    rest_w = columns[n_tp - 1]
     parts_g, parts_a = grams(acts, out_cot, emb_cot, emb_ids, came_w[0], n_dp, quads_a, quads_g)
     arrived_g = [parts_g[0]] + [trade(parts_g[k], k) for k in range(1, half)]
+    kept_rows = round_up(2 * quads_g * (HEAD + 1) + 1 + half // 2, ROWS)
     arrived_a = [parts_a[0]] + [trade(parts_a[k], k) for k in range(1, half)]
-    kept_rows = round_up(2 * quads_g * (HEAD + 1) + 1 + half, ROWS)
     kept_g, mirror_g = add_up(
-        functools.partial(half_sum_g_kernel, quads_g), "half_sums_g", arrived_g, [kept_rows] * 2
+        functools.partial(half_sum_g_kernel, quads_g, half),
+        "half_sums_g",
+        arrived_g,
+        [kept_rows] * 2,
     )
     came_g = trade(mirror_g, half)
     kept_rows = round_up(quads_a * (HEAD + 1), ROWS)
@@ -593,22 +677,24 @@
         functools.partial(half_sum_a_kernel, quads_a), "half_sums_a", arrived_a, [kept_rows] * 2
     )
     came_a = trade(mirror_a, half)
-    share_rows = round_up(2 * quads_g * (HEAD + 1) + 3 + n_dp, ROWS)
+    share_rows = round_up(2 * quads_g * (HEAD + 1) + 3 + half, ROWS)
     (share,) = add_up(
-        functools.partial(sum_g_kernel, quads_g, half), "sums_g", [kept_g, came_g], [share_rows]
-    )
-    shared = lax.all_gather(share[None], "tensor", axis=0, tiled=True)
-    sizes = (
-        quads_a,
-        quads_g,
-        n_tp,
-        n_dp,
-        tok_rows * n_dp,
-        rows_e * n_dp * n_tp,
-        inner_part * n_tp,
-        width,
-    )
-    return tuple(invert_apply(kept_a, came_a, shared, grad_e, grad_w, came_w, sizes))
+        functools.partial(sum_g_kernel, quads_g, half), "sums_g", [kept_g, came_g], [share_rows], [mirror_a]
+    )
+    shares = [share]
+    for k in range(1, n_tp):
+        shares.append(share if k & (k - 1) else trade(share, k, "tensor"))
+    for k in range(1, n_tp):
+        if k & (k - 1):
+            shares[k] = trade(shares[k & (k - 1)], k & -k, "tensor")
+    came_rest = trade(hold(rest_w, shares[2]), n_tp - 1, "tensor")
+    tokens = tok_rows * n_dp
+    sizes = (quads_g, n_tp, n_dp, tokens, rows_e * n_dp * n_tp, inner_part * n_tp, width)
+    left, rest, ratio, update_e = apply_g(shares, grad_e, grad_w, came_w, sizes)
+    update_w = apply_a(
+        kept_a, came_a, ratio, left, came_w[-1], came_rest, rest, (quads_a, tokens)
+    )
+    return (update_w, update_e)
 
 
 def solution(mesh):

time: 39.8 us -> 38.1 us (0.957)
  blocking collectives: 5.93 us -> 0 us
  waiting for transfers between devices: 4.21 us -> 9.75 us
  local copies, waits for them, and re-layouts: 3.72 us -> 1.61 us
  starting transfers between devices: 17.1 us -> 18 us
    all_gather x1 -> x0, blocking collectives: 5.93 us -> none  [local(): shared = lax.all_gather(share[None], 'tensor', axis=0, tiled=True)]
    ppermute x11 -> x15, waiting for transfers between devices: 4.21 us -> 9.75 us  [trade(): return lax.ppermute(value, axis, [(i, i ^ k) for i in range(size)])]
    unnamed x12, local copies, waits for them, and re-layouts: 3.72 us -> 1.61 us
    ppermute x11 -> x15, starting transfers between devices: 17.1 us -> 18 us  [trade(): return lax.ppermute(value, axis, [(i, i ^ k) for i in range(size)])]
    pallas_call x5 -> x7, Pallas kernels: 6.59 us -> 6.42 us  [the longest x1 3.32 us: apply_g(): pl.pallas_call(functools.partial(apply_g_kernel, sizes), in_specs=[vmem,...]
  transfers between devices with their start and end apart: 11 -> 15, of which waited for: 6 -> 6; matrix products, arithmetic and copies ran while one was open for 0% -> 0% of each run, Pallas kernels for 3% -> 12%
where the time goes in v5:
time: 38.1 us; the launch traced here: 37.6 us
  starting transfers between devices  18 us (47%)
  waiting for transfers between devices  9.75 us (26%)
  Pallas kernels  7.5 us (20%)
  local copies, waits for them, and re-layouts  1.61 us (4%)
  between operations  0.73 us (2%)
    ppermute x15, starting transfers between devices, trade(): return lax.ppermute(value, axis, [(i, i ^ k) for i in range(size)])  18 us
    ppermute x15, waiting for transfers between devices, trade(): return lax.ppermute(value, axis, [(i, i ^ k) for i in range(size)])  9.75 us
    pallas_call x1, Pallas kernels, apply_g(): pl.pallas_call(functools.partial(apply_g_kernel, sizes), in_specs=[vmem,...  3.32 us
    pallas_call x1, Pallas kernels, apply_a(): pl.pallas_call(functools.partial(apply_a_kernel, sizes), in_specs=[vmem]...  2.75 us
    unnamed x12, local copies, waits for them, and re-layouts  1.61 us
    pallas_call x1, Pallas kernels, grams(): pl.pallas_call(functools.partial(gram_kernel, (quads_a, quads_g, n_dp)),...  1.08 us
  transfers between devices with their start and end apart: 15, of which 6 were waited for; matrix products, arithmetic and copies ran while one was open for 0% of the time, Pallas kernels for 12%

profile of v5, /device:TPU:0, one launch (start us, length us, event | category | flops | bytes accessed | tf_op | source)
XLA Modules:
  0.0 37.6 jit_solution(6797766921610200622)
XLA Ops:
  0.6 1.6 %copy-done = f32[256,2048]{1,0:T(8,128)S(1)} copy-done((f32[256,2048]{1,0:T(8,128)S(1)}, f32[256,2048]{1,0:T(8,128)}, u32[]{:S(2)}) %copy-start) | copy-done | bytes 2097176
  2.2 0.2 column_parts.1
  2.4 0.5 %collective-permute-start = (f32[256,512]{1,0:T(8,128)S(1)}, f32[256,512]{1,0:T(8,128)S(1)}, u32[]{:S(2)}, u32[]{:S(2)}) collective-permute-start(f32[256,512]{1,0:T(8,128)S(1)} %get-tuple-element.22), channel_id=1, source_target_pairs={{0,1},{1,0},{2,3},{3,2},{4,5},{5,4},{6,7},{7,6},{8,9},{9,8},{10,11... | collective-permute-start | bytes 1572872 | tf_op jit(solution)/shard_map/ppermute | solution.py:659
  3.0 2.6 %collective-permute-start.12 = (f32[256,512]{1,0:T(8,128)S(1)}, f32[256,512]{1,0:T(8,128)S(1)}, u32[]{:S(2)}, u32[]{:S(2)}) collective-permute-start(f32[256,512]{1,0:T(8,128)S(1)} %get-tuple-element.35), channel_id=1, source_target_pairs={{0,2},{1,3},{2,0},{3,1},{4,6},{5,7},{6,4},{7,5},{8,10},{9,11},{10,... | collective-permute-start | bytes 1572872 | tf_op jit(solution)/shard_map/ppermute | solution.py:659
  5.6 1.1 %grams.1 = (f32[200,128]{1,0:T(8,128)S(1)}, f32[200,128]{1,0:T(8,128)S(1)}, f32[200,128]{1,0:T(8,128)S(1)}, f32[200,128]{1,0:T(8,128)S(1)}, f32[264,128]{1,0:T(8...) custom-call(s32[1,64]{1,0:T(1,128)S(1)} %bitcast.1, ...), custom_call_target="tpu_custom_call" | custom-call | flops 1000 | bytes 1000 | tf_op jit(solution)/shard_map/grams/pallas_call | solution.py:293
  6.7 1.9 %collective-permute-start.5 = (f32[200,128]{1,0:T(8,128)S(1)}, f32[200,128]{1,0:T(8,128)S(1)}, u32[]{:S(2)}, u32[]{:S(2)}) collective-permute-start(f32[200,128]{1,0:T(8,128)S(1)} %get-tuple-element.30), channel_id=1, source_target_pairs={{0,4},{4,0},{8,12},{12,8},{16,20},{20,16},{24,28},{28,24},{1,5},{5... | collective-permute-start | bytes 307208 | tf_op jit(solution)/shard_map/ppermute | solution.py:659
  8.6 1.6 %collective-permute-start.6 = (f32[200,128]{1,0:T(8,128)S(1)}, f32[200,128]{1,0:T(8,128)S(1)}, u32[]{:S(2)}, u32[]{:S(2)}) collective-permute-start(f32[200,128]{1,0:T(8,128)S(1)} %get-tuple-element.31), channel_id=1, source_target_pairs={{0,8},{4,12},{8,0},{12,4},{16,24},{20,28},{24,16},{28,20},{1,9},{5... | collective-permute-start | bytes 307208 | tf_op jit(solution)/shard_map/ppermute | solution.py:659
  10.1 0.1 collective-permute-start.7
  10.2 1.9 %collective-permute-start.1 = (f32[264,128]{1,0:T(8,128)S(1)}, f32[264,128]{1,0:T(8,128)S(1)}, u32[]{:S(2)}, u32[]{:S(2)}) collective-permute-start(f32[264,128]{1,0:T(8,128)S(1)} %get-tuple-element.24), channel_id=1, source_target_pairs={{0,4},{4,0},{8,12},{12,8},{16,20},{20,16},{24,28},{28,24},{1,5},{5... | collective-permute-start | bytes 405512 | tf_op jit(solution)/shard_map/ppermute | solution.py:659
  12.1 1.6 %collective-permute-start.2 = (f32[264,128]{1,0:T(8,128)S(1)}, f32[264,128]{1,0:T(8,128)S(1)}, u32[]{:S(2)}, u32[]{:S(2)}) collective-permute-start(f32[264,128]{1,0:T(8,128)S(1)} %get-tuple-element.25), channel_id=1, source_target_pairs={{0,8},{4,12},{8,0},{12,4},{16,24},{20,28},{24,16},{28,20},{1,9},{5... | collective-permute-start | bytes 405512 | tf_op jit(solution)/shard_map/ppermute | solution.py:659
  13.6 0.6 %collective-permute-done.6.refs_2_ = f32[200,128]{1,0:T(8,128)S(1)} collective-permute-done((f32[200,128]{1,0:T(8,128)S(1)}, f32[200,128]{1,0:T(8,128)S(1)}, u32[]{:S(2)}, u32[]{:S(2)}) %collective-permute-start.6) | collective-permute-done | bytes 102432 | tf_op jit(solution)/shard_map/ppermute | solution.py:659
  14.2 1.6 %collective-permute-start.3 = (f32[264,128]{1,0:T(8,128)S(1)}, f32[264,128]{1,0:T(8,128)S(1)}, u32[]{:S(2)}, u32[]{:S(2)}) collective-permute-start(f32[264,128]{1,0:T(8,128)S(1)} %get-tuple-element.26), channel_id=1, source_target_pairs={{0,12},{4,8},{8,4},{12,0},{16,28},{20,24},{24,20},{28,16},{1,13},{... | collective-permute-start | bytes 405512 | tf_op jit(solution)/shard_map/ppermute | solution.py:659
  15.8 0.8 %collective-permute-done.7.refs_3_ = f32[200,128]{1,0:T(8,128)S(1)} collective-permute-done((f32[200,128]{1,0:T(8,128)S(1)}, f32[200,128]{1,0:T(8,128)S(1)}, u32[]{:S(2)}, u32[]{:S(2)}) %collective-permute-start.7) | collective-permute-done | bytes 102432 | tf_op jit(solution)/shard_map/ppermute | solution.py:659
  16.6 0.1 half_sums_g.1
  16.7 0.7 %collective-permute-done.1.refs_1_ = f32[264,128]{1,0:T(8,128)S(1)} collective-permute-done((f32[264,128]{1,0:T(8,128)S(1)}, f32[264,128]{1,0:T(8,128)S(1)}, u32[]{:S(2)}, u32[]{:S(2)}) %collective-permute-start.1) | collective-permute-done | bytes 135200 | tf_op jit(solution)/shard_map/ppermute | solution.py:659
  17.4 2.7 %collective-permute-start.8 = (f32[136,128]{1,0:T(8,128)S(1)}, f32[136,128]{1,0:T(8,128)S(1)}, u32[]{:S(2)}, u32[]{:S(2)}) collective-permute-start(f32[136,128]{1,0:T(8,128)S(1)} %get-tuple-element.34), channel_id=1, source_target_pairs={{0,16},{4,20},{8,24},{12,28},{16,0},{20,4},{24,8},{28,12},{1,17},{... | collective-permute-start | bytes 208904 | tf_op jit(solution)/shard_map/ppermute | solution.py:659
  20.1 1.4 %collective-permute-done.3.refs_3_ = f32[264,128]{1,0:T(8,128)S(1)} collective-permute-done((f32[264,128]{1,0:T(8,128)S(1)}, f32[264,128]{1,0:T(8,128)S(1)}, u32[]{:S(2)}, u32[]{:S(2)}) %collective-permute-start.3) | collective-permute-done | bytes 135200 | tf_op jit(solution)/shard_map/ppermute | solution.py:659
  21.5 2.5 %collective-permute-done.8.came = f32[136,128]{1,0:T(8,128)S(1)} collective-permute-done((f32[136,128]{1,0:T(8,128)S(1)}, f32[136,128]{1,0:T(8,128)S(1)}, u32[]{:S(2)}, u32[]{:S(2)}) %collective-permute-start.8) | collective-permute-done | bytes 69664 | tf_op jit(solution)/shard_map/ppermute | solution.py:659
  24.1 0.7 %collective-permute-start.10 = (f32[144,128]{1,0:T(8,128)S(1)}, f32[144,128]{1,0:T(8,128)S(1)}, u32[]{:S(2)}, u32[]{:S(2)}) collective-permute-start(f32[144,128]{1,0:T(8,128)S(1)} %sums_g.1.refs_0_), channel_id=1, source_target_pairs={{0,2},{1,3},{2,0},{3,1},{4,6},{5,7},{6,4},{7,5},{8,10},{9,11},{10,... | collective-permute-start | bytes 221192 | tf_op jit(solution)/shard_map/ppermute | solution.py:659
  24.7 3.8 %collective-permute-done.10.refs_2_.refs_1_ = f32[144,128]{1,0:T(8,128)S(1)} collective-permute-done((f32[144,128]{1,0:T(8,128)S(1)}, f32[144,128]{1,0:T(8,128)S(1)}, u32[]{:S(2)}, u32[]{:S(2)}) %collective-permute-start.10) | collective-permute-done | bytes 73760 | tf_op jit(solution)/shard_map/ppermute | solution.py:659
  28.5 0.7 %collective-permute-start.9 = (f32[144,128]{1,0:T(8,128)S(1)}, f32[144,128]{1,0:T(8,128)S(1)}, u32[]{:S(2)}, u32[]{:S(2)}) collective-permute-start(f32[144,128]{1,0:T(8,128)S(1)} %sums_g.1.refs_0_), channel_id=1, source_target_pairs={{0,1},{1,0},{2,3},{3,2},{4,5},{5,4},{6,7},{7,6},{8,9},{9,8},{10,11... | collective-permute-start | bytes 221192 | tf_op jit(solution)/shard_map/ppermute | solution.py:659
  29.2 2.3 %collective-permute-start.4 = (f32[136,128]{1,0:T(8,128)S(1)}, f32[136,128]{1,0:T(8,128)S(1)}, u32[]{:S(2)}, u32[]{:S(2)}) collective-permute-start(f32[136,128]{1,0:T(8,128)S(1)} %get-tuple-element.28.refs_0_), channel_id=1, source_target_pairs={{0,16},{4,20},{8,24},{12,28},{16,0},{20,4},{24,8},{28,12},{1,17},{... | collective-permute-start | bytes 208904 | tf_op jit(solution)/shard_map/ppermute | solution.py:659
  31.5 3.3 %apply_g.1 = (f32[4,256,512]{2,1,0:T(8,128)S(1)}, bf16[256,256]{1,0:T(8,128)(2,1)S(1)}, f32[8,128]{1,0:T(8,128)S(1)}, f32[256,1024]{1,0:T(8,128)}) custom-call(f32[256,1024]{1,0:T(8,128)S(1)} %copy-done.3, f32[256,2048]{1,0:T(8,128)S(1)} %copy-done, f32[144,128]{1,0:T(8,128)S(1)} %sums_g.1.refs_0_, f32[144,128]{1,0:T(8,128)S(1)} %collective-permute-done.9.refs_1_, ...), custom_call_target="tpu_custom_call" | custom-call | flops 1000 | bytes 8000000 | tf_op jit(solution)/shard_map/apply_g/pallas_call | solution.py:530
  34.9 2.8 %apply_a.1 = f32[1024,512]{1,0:T(8,128)} custom-call(f32[136,128]{1,0:T(8,128)S(1)} %get-tuple-element.27.kept, f32[136,128]{1,0:T(8,128)S(1)} %collective-permute-done.4.came, f32[8,128]{1,0:T(8,128)S(1)} %get-tuple-element.37.ratio, f32[4,256,512]{2,1,0:T(8,128)S(1)} %get-tuple-element.38.left, f32[160,512]{1,0:T(8,128)S(1)} %collective-permute-done.13.refs_6_.last_w, ...), custom_call_target="tpu_custom_call" | custom-call | flops 1000 | bytes 1000 | tf_op jit(solution)/shard_map/apply_a/pallas_call | solution.py:583
  (26 shorter events, 0.1 us)
Async XLA Ops:
  0.6 1.6 %copy-start = (f32[256,2048]{1,0:T(8,128)S(1)}, f32[256,2048]{1,0:T(8,128)}, u32[]{:S(2)}) copy-start(f32[256,2048]{1,0:T(8,128)} %w_hbm.3) | copy-start | bytes 6291460
  2.2 3.3 %copy-start.1 = (bf16[8,256,512]{2,1,0:T(8,128)(2,1)S(1)}, bf16[8,256,512]{2,1,0:T(8,128)(2,1)}, u32[]{:S(2)}) copy-start(bf16[8,256,512]{2,1,0:T(8,128)(2,1)} %acts.1) | copy-start | bytes 6291460
  2.2 3.3 %copy-start.2 = (bf16[8,256,256]{2,1,0:T(8,128)(2,1)S(1)}, bf16[8,256,256]{2,1,0:T(8,128)(2,1)}, u32[]{:S(2)}) copy-start(bf16[8,256,256]{2,1,0:T(8,128)(2,1)} %cot.1) | copy-start | bytes 3145732
  2.2 3.3 %copy-start.4 = (bf16[256,256]{1,0:T(8,128)(2,1)S(1)}, bf16[256,256]{1,0:T(8,128)(2,1)}, u32[]{:S(2)}) copy-start(bf16[256,256]{1,0:T(8,128)(2,1)} %emb.1) | copy-start | bytes 393220
  2.2 3.3 %copy-start.5 = (s32[64]{0:T(128)S(1)}, s32[64]{0:T(128)}, u32[]{:S(2)}) copy-start(s32[64]{0:T(128)} %param.8) | copy-start | bytes 772
  2.4 3.1 %collective-permute-start = (f32[256,512]{1,0:T(8,128)S(1)}, f32[256,512]{1,0:T(8,128)S(1)}, u32[]{:S(2)}, u32[]{:S(2)}) collective-permute-start(f32[256,512]{1,0:T(8,128)S(1)} %get-tuple-element.22), channel_id=1, source_target_pairs={{0,1},{1,0},{2,3},{3,2},{4,5},{5,4},{6,7},{7,6},{8,9},{9,8},{10,11... | collective-permute-start | bytes 1572872 | tf_op jit(solution)/shard_map/ppermute | solution.py:659
  3.0 28.5 %collective-permute-start.12 = (f32[256,512]{1,0:T(8,128)S(1)}, f32[256,512]{1,0:T(8,128)S(1)}, u32[]{:S(2)}, u32[]{:S(2)}) collective-permute-start(f32[256,512]{1,0:T(8,128)S(1)} %get-tuple-element.35), channel_id=1, source_target_pairs={{0,2},{1,3},{2,0},{3,1},{4,6},{5,7},{6,4},{7,5},{8,10},{9,11},{10,... | collective-permute-start | bytes 1572872 | tf_op jit(solution)/shard_map/ppermute | solution.py:659
  5.6 25.9 %copy-start.3 = (f32[256,1024]{1,0:T(8,128)S(1)}, f32[256,1024]{1,0:T(8,128)}, u32[]{:S(2)}) copy-start(f32[256,1024]{1,0:T(8,128)} %e_in.1) | copy-start | bytes 3145732
  6.7 5.4 %collective-permute-start.5 = (f32[200,128]{1,0:T(8,128)S(1)}, f32[200,128]{1,0:T(8,128)S(1)}, u32[]{:S(2)}, u32[]{:S(2)}) collective-permute-start(f32[200,128]{1,0:T(8,128)S(1)} %get-tuple-element.30), channel_id=1, source_target_pairs={{0,4},{4,0},{8,12},{12,8},{16,20},{20,16},{24,28},{28,24},{1,5},{5... | collective-permute-start | bytes 307208 | tf_op jit(solution)/shard_map/ppermute | solution.py:659
  8.6 5.6 %collective-permute-start.6 = (f32[200,128]{1,0:T(8,128)S(1)}, f32[200,128]{1,0:T(8,128)S(1)}, u32[]{:S(2)}, u32[]{:S(2)}) collective-permute-start(f32[200,128]{1,0:T(8,128)S(1)} %get-tuple-element.31), channel_id=1, source_target_pairs={{0,8},{4,12},{8,0},{12,4},{16,24},{20,28},{24,16},{28,20},{1,9},{5... | collective-permute-start | bytes 307208 | tf_op jit(solution)/shard_map/ppermute | solution.py:659
  10.1 6.5 %collective-permute-start.7 = (f32[200,128]{1,0:T(8,128)S(1)}, f32[200,128]{1,0:T(8,128)S(1)}, u32[]{:S(2)}, u32[]{:S(2)}) collective-permute-start(f32[200,128]{1,0:T(8,128)S(1)} %get-tuple-element.32), channel_id=1, source_target_pairs={{0,12},{4,8},{8,4},{12,0},{16,28},{20,24},{24,20},{28,16},{1,13},{... | collective-permute-start | bytes 307208 | tf_op jit(solution)/shard_map/ppermute | solution.py:659
  10.2 7.2 %collective-permute-start.1 = (f32[264,128]{1,0:T(8,128)S(1)}, f32[264,128]{1,0:T(8,128)S(1)}, u32[]{:S(2)}, u32[]{:S(2)}) collective-permute-start(f32[264,128]{1,0:T(8,128)S(1)} %get-tuple-element.24), channel_id=1, source_target_pairs={{0,4},{4,0},{8,12},{12,8},{16,20},{20,16},{24,28},{28,24},{1,5},{5... | collective-permute-start | bytes 405512 | tf_op jit(solution)/shard_map/ppermute | solution.py:659
  12.1 8.0 %collective-permute-start.2 = (f32[264,128]{1,0:T(8,128)S(1)}, f32[264,128]{1,0:T(8,128)S(1)}, u32[]{:S(2)}, u32[]{:S(2)}) collective-permute-start(f32[264,128]{1,0:T(8,128)S(1)} %get-tuple-element.25), channel_id=1, source_target_pairs={{0,8},{4,12},{8,0},{12,4},{16,24},{20,28},{24,16},{28,20},{1,9},{5... | collective-permute-start | bytes 405512 | tf_op jit(solution)/shard_map/ppermute | solution.py:659
  14.2 7.3 %collective-permute-start.3 = (f32[264,128]{1,0:T(8,128)S(1)}, f32[264,128]{1,0:T(8,128)S(1)}, u32[]{:S(2)}, u32[]{:S(2)}) collective-permute-start(f32[264,128]{1,0:T(8,128)S(1)} %get-tuple-element.26), channel_id=1, source_target_pairs={{0,12},{4,8},{8,4},{12,0},{16,28},{20,24},{24,20},{28,16},{1,13},{... | collective-permute-start | bytes 405512 | tf_op jit(solution)/shard_map/ppermute | solution.py:659
  16.6 12.6 %collective-permute-start.13 = (f32[160,512]{1,0:T(8,128)S(1)}, f32[160,512]{1,0:T(8,128)S(1)}, u32[]{:S(2)}, u32[]{:S(2)}) collective-permute-start(f32[160,512]{1,0:T(8,128)S(1)} %get-tuple-element.36), channel_id=1, source_target_pairs={{0,3},{1,2},{2,1},{3,0},{4,7},{5,6},{6,5},{7,4},{8,11},{9,10},{10,... | collective-permute-start | bytes 983048 | tf_op jit(solution)/shard_map/ppermute | solution.py:659
  17.4 6.7 %collective-permute-start.8 = (f32[136,128]{1,0:T(8,128)S(1)}, f32[136,128]{1,0:T(8,128)S(1)}, u32[]{:S(2)}, u32[]{:S(2)}) collective-permute-start(f32[136,128]{1,0:T(8,128)S(1)} %get-tuple-element.34), channel_id=1, source_target_pairs={{0,16},{4,20},{8,24},{12,28},{16,0},{20,4},{24,8},{28,12},{1,17},{... | collective-permute-start | bytes 208904 | tf_op jit(solution)/shard_map/ppermute | solution.py:659
  24.1 4.4 %collective-permute-start.10 = (f32[144,128]{1,0:T(8,128)S(1)}, f32[144,128]{1,0:T(8,128)S(1)}, u32[]{:S(2)}, u32[]{:S(2)}) collective-permute-start(f32[144,128]{1,0:T(8,128)S(1)} %sums_g.1.refs_0_), channel_id=1, source_target_pairs={{0,2},{1,3},{2,0},{3,1},{4,6},{5,7},{6,4},{7,5},{8,10},{9,11},{10,... | collective-permute-start | bytes 221192 | tf_op jit(solution)/shard_map/ppermute | solution.py:659
  28.5 6.4 %collective-permute-start.14 = (f32[96,512]{1,0:T(8,128)S(1)}, f32[96,512]{1,0:T(8,128)S(1)}, u32[]{:S(2)}, u32[]{:S(2)}) collective-permute-start(f32[96,512]{1,0:T(8,128)S(1)} %hold.1), channel_id=1, source_target_pairs={{0,3},{1,2},{2,1},{3,0},{4,7},{5,6},{6,5},{7,4},{8,11},{9,10},{10,... | collective-permute-start | bytes 589832 | tf_op jit(solution)/shard_map/ppermute | solution.py:659
  28.5 3.0 %collective-permute-start.9 = (f32[144,128]{1,0:T(8,128)S(1)}, f32[144,128]{1,0:T(8,128)S(1)}, u32[]{:S(2)}, u32[]{:S(2)}) collective-permute-start(f32[144,128]{1,0:T(8,128)S(1)} %sums_g.1.refs_0_), channel_id=1, source_target_pairs={{0,1},{1,0},{2,3},{3,2},{4,5},{5,4},{6,7},{7,6},{8,9},{9,8},{10,11... | collective-permute-start | bytes 221192 | tf_op jit(solution)/shard_map/ppermute | solution.py:659
  29.2 2.3 %collective-permute-start.11 = (f32[144,128]{1,0:T(8,128)S(1)}, f32[144,128]{1,0:T(8,128)S(1)}, u32[]{:S(2)}, u32[]{:S(2)}) collective-permute-start(f32[144,128]{1,0:T(8,128)S(1)} %collective-permute-done.10.refs_2_.refs_1_), channel_id=1, source_target_pairs={{0,1},{1,0},{2,3},{3,2},{4,5},{5,4},{6,7},{7,6},{8,9},{9,8},{10,11... | collective-permute-start | bytes 221192 | tf_op jit(solution)/shard_map/ppermute | solution.py:659
  29.2 5.6 %collective-permute-start.4 = (f32[136,128]{1,0:T(8,128)S(1)}, f32[136,128]{1,0:T(8,128)S(1)}, u32[]{:S(2)}, u32[]{:S(2)}) collective-permute-start(f32[136,128]{1,0:T(8,128)S(1)} %get-tuple-element.28.refs_0_), channel_id=1, source_target_pairs={{0,16},{4,20},{8,24},{12,28},{16,0},{20,4},{24,8},{28,12},{1,17},{... | collective-permute-start | bytes 208904 | tf_op jit(solution)/shard_map/ppermute | solution.py:659
